TPU v7x, 512 devices: a whole 4x8x8 slice. The times are simulated.
512 devices in a mesh: dom: 128 (over y, z, core), sub: 4 (over x).
Axes of the slice: x: 4, y: 8, z: 8, core: 2. Of those that a mesh axis runs over, the one named last changes fastest.
Arguments:
- fields: float32 [6, 20, 524288], P(None, None, ('dom', 'sub')), may hold values from -6 to 6
- geometry: float32 [9, 524288], P(None, ('dom', 'sub')), may hold values from -4 to 4
- normals: float32 [3, 4, 524288], P(None, None, ('dom', 'sub')), may hold values from -3 to 3
- face_scale: float32 [4, 524288], P(None, ('dom', 'sub')), may hold values from 0.5 to 3
- derivatives: float32 [3, 20, 20], replicated, may hold values from -1.25 to 1.25
- lift_matrix: float32 [20, 40], replicated, may hold values from -1 to 1
- face_nbr: int32 [4, 524288], P(None, ('dom', 'sub')), may hold values from 0 to 4607, as said below
- send_rows: int32 [262144], P(('dom', 'sub')), may hold values from 64 to 1024, as said below
- fine_slots: int32 [65536], P(('dom', 'sub')), may hold values from 0 to 511, as said below
- export_rows: int32 [2, 8192], P(None, ('dom', 'sub')), may hold values from 0 to 127, as said below
- fine_nbr: int32 [4, 65536], P(None, ('dom', 'sub')), may hold values from 0 to 640
Outputs:
- fields_out: float32 [6, 20, 524288], P(None, None, ('dom', 'sub'))
Inputs may be any that keep to these rules, and one draw needn't show every extreme that they name: `face_nbr`: A wall face holds its own number 4 (e - p * 1024) + f. Codes from 4096 up occur only on the first 64 and the last 64 elements of a device: the first 64 use 4 * 1024 to 4351, the last 64 use 4 * 1024 + 4 * 64 and above. `send_rows`: entry p * 512 + j * 4 + c is the row within device p of the c-th element that p hands to the device of dom index j and p's sub index; 1024 marks an empty slot, and filled slots come first in each group of 4. Each group holds 0, 2 or 4 elements; in each sub index half of the dom indices hand 2 * 128 elements each, each of them 4 to some device, the others hand none. Handed rows are distinct and lie in 64 to 959. `fine_slots`: the 128 entries of a device are the filled slots j * 4 + c addressed to it (j the sender's dom index), each exactly once, in some order. `export_rows`: each row of a device holds 16 distinct positions among its 128 fine elements.
All inputs are finite; a program needn't handle non-finite values.
Results may differ from a plain program's by a relative error of at most 0.0001.
Values sent between devices are 32-bit elements; how exact they have to be, the bound alone decides.
No kernel may reach another device: no remote copies, remote signals or barrier semaphores. Data moves between devices by JAX's collectives and lax.ppermute only.
A program may use at most 128 MiB of HBM per device.

v0:
```python
import jax
import jax.numpy as jnp
import numpy as np
from jax import lax
from jax.sharding import PartitionSpec as P

SUBSTEPS = 4


coarse_step = 0.2
highest = lax.Precision.HIGHEST


def with_halo(block, sides, width):
    for axis, dim in sides:
        count = lax.axis_size(axis)
        forward = [(i, i + 1) for i in range(count - 1)]
        forward.append((count - 1, 0))
        backward = [(target, source) for source, target in forward]
        low = lax.ppermute(
            lax.slice_in_dim(block, block.shape[dim] - width, None, axis=dim), axis, forward
        )
        high = lax.ppermute(lax.slice_in_dim(block, 0, width, axis=dim), axis, backward)
        block = jnp.concatenate([low, block, high], axis=dim)
    return block


def face_table():
    places = [
        (along_r, along_s, along_t)
        for along_t in range(4)
        for along_s in range(4 - along_t)
        for along_r in range(4 - along_t - along_s)
    ]
    bottom_face = [number for number, location in enumerate(places) if location[2] == 0]
    front_face = [number for number, location in enumerate(places) if location[1] == 0]
    slanted = [
        number
        for number, location in enumerate(places)
        if location[0] + location[1] + location[2] == 3
    ]
    beside = [number for number, location in enumerate(places) if location[0] == 0]
    return np.array([bottom_face, front_face, slanted, beside], dtype=np.int32).T


def traces_of(vector_field, face_nodes):
    return vector_field[:, face_nodes, :]


def curl_of(vector_field, geometry, derivatives):
    local_grad = jnp.einsum("apq,cqe->acpe", derivatives, vector_field, precision=highest)
    factors = geometry.reshape(3, 3, geometry.shape[-1])

    def derivative(axis_out, component):
        return (
            factors[axis_out, 0] * local_grad[0, component]
            + factors[axis_out, 1] * local_grad[1, component]
            + factors[axis_out, 2] * local_grad[2, component]
        )

    return jnp.stack(
        [
            derivative(1, 2) - derivative(2, 1),
            derivative(2, 0) - derivative(0, 2),
            derivative(0, 1) - derivative(1, 0),
        ]
    )


def cross_product(normals, jump_values):
    return jnp.stack(
        [
            normals[1] * jump_values[2] - normals[2] * jump_values[1],
            normals[2] * jump_values[0] - normals[0] * jump_values[2],
            normals[0] * jump_values[1] - normals[1] * jump_values[0],
        ]
    )


def lift_of(lift_matrix, face_scale, flux_values):
    scaled = flux_values * face_scale
    shaped = lift_matrix.reshape(lift_matrix.shape[0], 4, lift_matrix.shape[1] // 4)
    return 0.5 * jnp.einsum("pfn,cnfe->cpe", shaped, scaled, precision=highest)


def magnetic_rate(curl_e, efield, outside, normals, face_scale, lift_matrix, face_nodes):
    jump_values = outside - traces_of(efield, face_nodes)
    return -curl_e - lift_of(lift_matrix, face_scale, cross_product(normals, jump_values))


def electric_rate(curl_h, hfield, outside, normals, face_scale, lift_matrix, face_nodes):
    jump_values = outside - traces_of(hfield, face_nodes)
    return curl_h + lift_of(lift_matrix, face_scale, cross_product(normals, jump_values))


def exterior_local(extended, own_field, pool_index, mirror, mirror_sign, face_nodes):
    interior = traces_of(own_field, face_nodes)
    flat_traces = traces_of(extended, face_nodes).reshape(
        3, interior.shape[1], 4 * extended.shape[2]
    )
    return jnp.where(mirror, mirror_sign * interior, flat_traces[:, :, pool_index])


def per_device(
    fields,
    geometry,
    normals,
    face_scale,
    derivatives,
    lift_matrix,
    face_nbr,
    send_rows,
    fine_slots,
    export_rows,
    fine_nbr,
):
    face_nodes = face_table()
    node_count = fields.shape[1]
    trace_count = face_nodes.shape[0]
    own_count = fields.shape[2]
    rim_width = own_count // 16
    fine_count = fine_slots.shape[0]
    list_width = export_rows.shape[1]
    slot_count = send_rows.shape[0]
    extended_width = own_count + 2 * rim_width
    quarter = face_nbr // 4
    extended_row = jnp.where(
        face_nbr < 4 * own_count,
        quarter + rim_width,
        jnp.where(face_nbr < 4 * own_count + 4 * rim_width, quarter - own_count, quarter),
    )
    pool_index = face_nbr % 4 * extended_width + extended_row
    own_faces = (
        4 * jnp.arange(own_count, dtype=jnp.int32)[None, :]
        + jnp.arange(4, dtype=jnp.int32)[:, None]
    )
    mirror = face_nbr == own_faces
    safe_rows = jnp.minimum(send_rows, own_count - 1)
    padded = jnp.pad(fields, ((0, 0), (0, 0), (rim_width, rim_width)))
    picked = fields[:, :, safe_rows]
    interior = traces_of(picked, face_nodes)
    flat_traces = traces_of(padded, face_nodes).reshape(6, trace_count, 4 * extended_width)
    mirror_signs = jnp.array([-1.0, -1.0, -1.0, 1.0, 1.0, 1.0], jnp.float32)[:, None, None, None]
    held_traces = jnp.where(
        mirror[:, safe_rows], mirror_signs * interior, flat_traces[:, :, pool_index[:, safe_rows]]
    )
    static = jnp.concatenate(
        [
            geometry[:, safe_rows],
            normals.reshape(12, own_count)[:, safe_rows],
            face_scale[:, safe_rows],
        ],
        axis=0,
    )
    received = (
        lax.all_to_all(
            picked.reshape(6 * node_count, slot_count),
            "dom",
            split_axis=1,
            concat_axis=1,
            tiled=True,
        ),
        lax.all_to_all(
            held_traces.reshape(24 * trace_count, slot_count),
            "dom",
            split_axis=1,
            concat_axis=1,
            tiled=True,
        ),
        lax.all_to_all(static, "dom", split_axis=1, concat_axis=1, tiled=True),
    )
    fine_fields = received[0][:, fine_slots].reshape(6, node_count, fine_count)
    fine_held = received[1][:, fine_slots].reshape(6, trace_count, 4, fine_count)
    fine_static = received[2][:, fine_slots]
    geometry_fine = fine_static[:9]
    normals_fine = fine_static[9:21].reshape(3, 4, fine_count)
    scale_fine = fine_static[21:]
    local_end = 4 * fine_count
    remote_span = 4 * list_width
    first_part = jnp.clip(fine_nbr - local_end, 0, remote_span - 1)
    second_part = jnp.clip(fine_nbr - local_end - remote_span, 0, remote_span - 1)
    nearby_face = fine_nbr < local_end
    lower_side = fine_nbr < local_end + remote_span
    frozen = fine_nbr == local_end + 2 * remote_span
    pool_face = jnp.where(
        nearby_face, fine_nbr % 4, jnp.where(lower_side, first_part % 4, second_part % 4)
    )
    partner_ext = with_halo(export_rows, ((("dom", "sub"), 1),), list_width)
    pool_width = 3 * fine_count
    pool_row = jnp.where(
        nearby_face,
        fine_count + fine_nbr // 4,
        jnp.where(
            lower_side,
            partner_ext[1, :list_width][first_part // 4],
            2 * fine_count + partner_ext[0, 2 * list_width :][second_part // 4],
        ),
    )
    fine_pool_index = pool_face * pool_width + pool_row

    def neighbours(vector_field):
        return with_halo(vector_field, ((("dom", "sub"), 2),), fine_count)

    def fine_outside(vector_field, held_part):
        pool_field = neighbours(vector_field)
        flat_pool = traces_of(pool_field, face_nodes).reshape(3, trace_count, 4 * pool_width)
        return jnp.where(frozen, held_part, flat_pool[:, :, fine_pool_index])

    fine_step = coarse_step / SUBSTEPS
    efield = fine_fields[:3]
    hfield = fine_fields[3:]
    for substep in range(SUBSTEPS):
        outside = fine_outside(efield, fine_held[:3])
        hfield = hfield + fine_step * magnetic_rate(
            curl_of(efield, geometry_fine, derivatives),
            efield,
            outside,
            normals_fine,
            scale_fine,
            lift_matrix,
            face_nodes,
        )
        outside = fine_outside(hfield, fine_held[3:])
        efield = efield + fine_step * electric_rate(
            curl_of(hfield, geometry_fine, derivatives),
            hfield,
            outside,
            normals_fine,
            scale_fine,
            lift_matrix,
            face_nodes,
        )
    results = jnp.concatenate([efield, hfield]).reshape(6 * node_count, fine_count)
    outgoing_back = (
        jnp.zeros((6 * node_count, slot_count), jnp.float32).at[:, fine_slots].set(results)
    )
    returned = lax.all_to_all(outgoing_back, "dom", split_axis=1, concat_axis=1, tiled=True)
    widened = jnp.concatenate(
        [fields.reshape(6 * node_count, own_count), jnp.zeros((6 * node_count, 1), jnp.float32)],
        axis=1,
    )
    merged = widened.at[:, send_rows].set(returned)[:, :own_count].reshape(6, node_count, own_count)
    efield = merged[:3]
    electric_ext = with_halo(efield, ((("dom", "sub"), 2),), rim_width)
    curl_e = curl_of(efield, geometry, derivatives)
    hfield = merged[3:]
    outside = exterior_local(electric_ext, efield, pool_index, mirror, -1.0, face_nodes)
    hfield = hfield + coarse_step * magnetic_rate(
        curl_e, efield, outside, normals, face_scale, lift_matrix, face_nodes
    )
    magnetic_ext = with_halo(hfield, ((("dom", "sub"), 2),), rim_width)
    outside = exterior_local(magnetic_ext, hfield, pool_index, mirror, 1.0, face_nodes)
    efield = efield + coarse_step * electric_rate(
        curl_of(hfield, geometry, derivatives),
        hfield,
        outside,
        normals,
        face_scale,
        lift_matrix,
        face_nodes,
    )
    return jnp.concatenate([efield, hfield])


def solution(mesh):
    return jax.shard_map(
        per_device,
        mesh=mesh,
        in_specs=(
            P(None, None, ("dom", "sub")),
            P(None, ("dom", "sub")),
            P(None, None, ("dom", "sub")),
            P(None, ("dom", "sub")),
            P(),
            P(),
            P(None, ("dom", "sub")),
            P(("dom", "sub")),
            P(("dom", "sub")),
            P(None, ("dom", "sub")),
            P(None, ("dom", "sub")),
        ),
        out_specs=P(None, None, ("dom", "sub")),
        check_vma=False,
    )
```

profile of v0, /device:TPU:1, one launch (start us, length us, event | category | flops | bytes accessed | tf_op | source)
XLA Modules:
  0.0 540.9 jit_solution(9736625430244333714)
XLA Ops:
  15.7 19.9 %all-to-all-start.1 = ((f32[25,128,4]{0,2,1:T(4,128)}), f32[25,128,4]{0,2,1:T(4,128)S(1)}, u32[]{:S(2)}, u32[]{:S(2)}) async-start(f32[25,128,4]{0,2,1:T(4,128)} %bitcast.6), calls=%async_computation.1 | async-start | bytes 524288 | tf_op jit(solution)/shard_map/all_to_all | solution.py:170
  47.2 8.7 %copy.816 = f32[6,10,4,1024]{1,0,3,2:T(8,128)} copy(f32[6,10,4,1024]{3,2,1,0:T(4,128)S(1)} %bitcast.1071) | data formatting | bytes 1966080
  57.4 13.6 %gather.157.clone = f32[6,10,4,1152]{1,0,3,2:T(8,128)} pad(f32[6,10,4,1024]{1,0,3,2:T(8,128)} %copy.816, f32[]{:T(128)} %constant.110.clone.1), padding=0_0x0_0x0_0x64_64 | pad | bytes 2088964 | tf_op jit(solution)/shard_map/gather | solution.py:47
  71.0 22.3 %gather_fusion.10 = f32[2048,6,10]{2,1,0:T(8,128)} fusion(f32[6,10,4608]{1,0,2:T(8,128)} %bitcast.1063, s32[2048]{0:T(1024)S(1)} %broadcast_clamp_fusion), kind=kCustom, calls=%fused_computation.10 | custom fusion | bytes 991232 | tf_op jit(solution)/shard_map/gather | solution.py:145
  93.3 4.9 copy.777
  98.2 17.8 %gather.161 = f32[240,128,4]{2,1,0:T(8,128)} reshape(f32[6,10,4,512]{3,2,1,0:T(4,128)S(1)} %bitcast.1086) | data formatting | bytes 983040 | tf_op jit(solution)/shard_map/gather | solution.py:145
  116.9 17.8 %gather.155 = f32[240,128,4]{2,1,0:T(8,128)} reshape(f32[6,10,4,512]{3,2,1,0:T(4,128)S(1)} %bitcast.1087) | data formatting | bytes 983040 | tf_op jit(solution)/shard_map/gather | solution.py:47
  136.4 18.2 %broadcast_in_dim.155 = pred[240,128,4]{2,1,0:T(8,128)(4,1)} reshape(pred[6,10,4,512]{3,2,1,0:T(4,128)(4,1)S(1)} %broadcast_in_dim.154) | data formatting | bytes 245760 | tf_op jit(solution)/shard_map/jit(_where)/broadcast_in_dim | solution.py:144
  154.7 17.7 %multiply_select_fusion = f32[240,128,4]{2,1,0:T(8,128)} fusion(pred[240,128,4]{2,1,0:T(8,128)(4,1)} %broadcast_in_dim.155, f32[240,128,4]{2,1,0:T(8,128)} %gather.161, f32[240,128,4]{2,1,0:T(8,128)} %gather.155, f32[240]{0:T(256)S(1)} %mul.3087), kind=kLoop, calls=%fused_computation.46 | loop fusion | flops 245760 | bytes 1598400 | tf_op jit(solution)/shard_map/jit(_where)/select_n | solution.py:144
  172.4 10.1 %copy.657 = f32[240,128,4]{0,2,1:T(4,128)} copy(f32[240,128,4]{2,1,0:T(8,128)} %multiply_select_fusion) | data formatting | bytes 983040 | tf_op jit(solution)/shard_map/jit(_where)/select_n | solution.py:144
  189.3 13.7 %all-to-all-start = ((f32[120,128,4]{0,2,1:T(4,128)}), f32[120,128,4]{0,2,1:T(4,128)S(1)}, u32[]{:S(2)}, u32[]{:S(2)}) async-start(f32[120,128,4]{0,2,1:T(4,128)} %all_to_all.30), calls=%async_computation | async-start | bytes 524288 | tf_op jit(solution)/shard_map/all_to_all | solution.py:156
  204.3 13.0 %all-to-all-done = f32[120,128,4]{0,2,1:T(4,128)S(1)} async-done(((f32[120,128,4]{0,2,1:T(4,128)}), f32[120,128,4]{0,2,1:T(4,128)S(1)}, u32[]{:S(2)}, u32[]{:S(2)}) %all-to-all-start) | async-done | bytes 245792 | tf_op jit(solution)/shard_map/all_to_all | solution.py:156
  217.3 6.9 %all-to-all-start.2 = ((f32[240,128,4]{0,2,1:T(4,128)}), f32[240,128,4]{0,2,1:T(4,128)S(1)}, u32[]{:S(2)}, u32[]{:S(2)}) async-start(f32[240,128,4]{0,2,1:T(4,128)} %copy.657), calls=%async_computation.2 | async-start | bytes 1048576 | tf_op jit(solution)/shard_map/all_to_all | solution.py:163
  227.0 4.9 collective-permute-start.1
  247.5 5.3 collective-permute-start.5
  261.5 5.4 %collective-permute-start.6 = (f32[3,20,128]{2,1,0:T(8,128)S(1)}, f32[3,20,128]{2,1,0:T(8,128)S(1)}, u32[]{:S(2)}, u32[]{:S(2)}) collective-permute-start(f32[3,20,128]{2,1,0:T(8,128)S(1)} %fusion.44), channel_id=1, source_target_pairs={{0,1},{1,2},{2,3},{3,4},{4,5},{5,6},{6,7},{7,8},{8,9},{9,10},{10,1... | collective-permute-start | bytes 92168 | tf_op jit(solution)/shard_map/ppermute | solution.py:20
  279.5 4.6 collective-permute-start.8
  296.7 4.6 collective-permute-start.10
  313.9 4.6 collective-permute-start.12
  331.1 4.6 collective-permute-start.14
  348.6 4.3 collective-permute-start.16
  352.9 6.7 %collective-permute-start.17 = (f32[3,20,128]{2,1,0:T(8,128)S(1)}, f32[3,20,128]{2,1,0:T(8,128)S(1)}, u32[]{:S(2)}, u32[]{:S(2)}) collective-permute-start(f32[3,20,128]{2,1,0:T(8,128)S(1)} %fusion.19), channel_id=1, source_target_pairs={{1,0},{2,1},{3,2},{4,3},{5,4},{6,5},{7,6},{8,7},{9,8},{10,9},{11,1... | collective-permute-start | bytes 92168 | tf_op jit(solution)/shard_map/ppermute | solution.py:23
  370.2 31.0 %all-to-all-start.3 = ((f32[120,128,4]{0,2,1:T(4,128)}), f32[120,128,4]{0,2,1:T(4,128)S(1)}, u32[]{:S(2)}, u32[]{:S(2)}) async-start(f32[120,128,4]{0,2,1:T(4,128)} %bitcast.210), calls=%async_computation.3 | async-start | bytes 524288 | tf_op jit(solution)/shard_map/all_to_all | solution.py:237
  401.6 13.8 %all-to-all-done.3 = f32[120,128,4]{0,2,1:T(4,128)S(1)} async-done(((f32[120,128,4]{0,2,1:T(4,128)}), f32[120,128,4]{0,2,1:T(4,128)S(1)}, u32[]{:S(2)}, u32[]{:S(2)}) %all-to-all-start.3) | async-done | bytes 245792 | tf_op jit(solution)/shard_map/all_to_all | solution.py:237
  419.8 8.6 %collective-permute-start.19 = (f32[3,20,64]{2,1,0:T(8,128)S(1)}, f32[3,20,64]{2,1,0:T(8,128)S(1)}, u32[]{:S(2)}, u32[]{:S(2)}) collective-permute-start(f32[3,20,64]{2,1,0:T(8,128)S(1)} %get-tuple-element.17), channel_id=1, source_target_pairs={{1,0},{2,1},{3,2},{4,3},{5,4},{6,5},{7,6},{8,7},{9,8},{10,9},{11,1... | collective-permute-start | bytes 46088 | tf_op jit(solution)/shard_map/ppermute | solution.py:23
  432.1 6.6 %copy.802 = f32[3,10,4,1152]{1,0,3,2:T(4,128)} copy(f32[3,10,4,1152]{3,0,2,1:T(4,128)S(1)} %bitcast.1081) | data formatting | bytes 1105920 | tf_op jit(solution)/shard_map/reshape | solution.py:98
  438.6 33.9 %gather_fusion.40 = f32[4096,3,10]{2,1,0:T(4,128)} fusion(f32[3,10,4608]{1,0,2:T(4,128)} %bitcast.1065, s32[4096]{0:T(1024)S(1)} %bitcast_clamp_fusion), kind=kCustom, calls=%fused_computation.40 | custom fusion | bytes 999424 | tf_op jit(solution)/shard_map/gather | solution.py:101
  472.5 6.5 %copy.803 = f32[4,1024,3,10]{1,0,2,3:T(4,128)S(1)} copy(f32[4,1024,3,10]{3,2,1,0:T(4,128)} %bitcast.1070) | data formatting | bytes 983040 | tf_op jit(solution)/shard_map/gather | solution.py:101
  483.8 4.9 collective-permute-start.21
  491.1 6.6 %copy.804 = f32[3,10,4,1152]{1,0,3,2:T(4,128)} copy(f32[3,10,4,1152]{3,0,2,1:T(4,128)S(1)} %bitcast.1080) | data formatting | bytes 1105920 | tf_op jit(solution)/shard_map/reshape | solution.py:98
  497.7 33.9 %gather_fusion.43 = f32[4096,3,10]{2,1,0:T(4,128)} fusion(f32[3,10,4608]{1,0,2:T(4,128)} %bitcast.1064, s32[4096]{0:T(1024)S(1)} %bitcast_clamp_fusion), kind=kCustom, calls=%fused_computation.43 | custom fusion | bytes 999424 | tf_op jit(solution)/shard_map/gather | solution.py:101
  531.6 6.5 %copy.805 = f32[4,1024,3,10]{1,0,2,3:T(4,128)S(1)} copy(f32[4,1024,3,10]{3,2,1,0:T(4,128)} %bitcast.1069) | data formatting | bytes 983040 | tf_op jit(solution)/shard_map/gather | solution.py:101
  (300 shorter events, 157.3 us)
Async XLA Ops:
  0.0 231.9 %copy-start = (f32[3,20,20]{2,1,0:T(8,128)S(1)}, f32[3,20,20]{2,1,0:T(8,128)}, u32[]{:S(2)}) copy-start(f32[3,20,20]{2,1,0:T(8,128)} %param.41) | copy-start | bytes 14404
  0.0 44.4 %copy-start.9 = (s32[40]{0:T(128)S(1)}, s32[40]{0:T(128)}, u32[]{:S(2)}) copy-start(s32[40]{0:T(128)} %constant.153) | copy-start | bytes 484
  0.0 44.5 %copy-start.1 = (f32[6,20,1024]{2,1,0:T(8,128)S(1)}, f32[6,20,1024]{2,1,0:T(8,128)}, u32[]{:S(2)}) copy-start(f32[6,20,1024]{2,1,0:T(8,128)} %param.37) | copy-start | bytes 1474564
  0.0 44.4 %copy-start.10 = (s32[128]{0:T(128)S(1)}, s32[128]{0:T(128)}, u32[]{:S(2)}) copy-start(s32[128]{0:T(128)} %param.45) | copy-start | bytes 1540
  0.0 182.5 %collective-permute-start.2 = (s32[2,16]{1,0:T(2,128)}, s32[2,16]{1,0:T(2,128)S(1)}, u32[]{:S(2)}, u32[]{:S(2)}) collective-permute-start(s32[2,16]{1,0:T(2,128)} %param.46), channel_id=1, source_target_pairs={{0,1},{1,2},{2,3},{3,4},{4,5},{5,6},{6,7},{7,8},{8,9},{9,10},{10,1... | collective-permute-start | bytes 392 | tf_op jit(solution)/shard_map/ppermute | solution.py:20
  4.1 181.8 %collective-permute-start.3 = (s32[2,16]{1,0:T(2,128)}, s32[2,16]{1,0:T(2,128)S(1)}, u32[]{:S(2)}, u32[]{:S(2)}) collective-permute-start(s32[2,16]{1,0:T(2,128)} %param.46), channel_id=1, source_target_pairs={{1,0},{2,1},{3,2},{4,3},{5,4},{6,5},{7,6},{8,7},{9,8},{10,9},{11,1... | collective-permute-start | bytes 392 | tf_op jit(solution)/shard_map/ppermute | solution.py:23
  15.7 173.7 %all-to-all-start.1 = ((f32[25,128,4]{0,2,1:T(4,128)}), f32[25,128,4]{0,2,1:T(4,128)S(1)}, u32[]{:S(2)}, u32[]{:S(2)}) async-start(f32[25,128,4]{0,2,1:T(4,128)} %bitcast.6), calls=%async_computation.1 | async-start | bytes 524288 | tf_op jit(solution)/shard_map/all_to_all | solution.py:170
  189.3 28.0 %all-to-all-start = ((f32[120,128,4]{0,2,1:T(4,128)}), f32[120,128,4]{0,2,1:T(4,128)S(1)}, u32[]{:S(2)}, u32[]{:S(2)}) async-start(f32[120,128,4]{0,2,1:T(4,128)} %all_to_all.30), calls=%async_computation | async-start | bytes 524288 | tf_op jit(solution)/shard_map/all_to_all | solution.py:156
  217.3 26.5 %all-to-all-start.2 = ((f32[240,128,4]{0,2,1:T(4,128)}), f32[240,128,4]{0,2,1:T(4,128)S(1)}, u32[]{:S(2)}, u32[]{:S(2)}) async-start(f32[240,128,4]{0,2,1:T(4,128)} %copy.657), calls=%async_computation.2 | async-start | bytes 1048576 | tf_op jit(solution)/shard_map/all_to_all | solution.py:163
  225.1 7.9 %collective-permute-start = (f32[3,20,128]{2,1,0:T(8,128)S(1)}, f32[3,20,128]{2,1,0:T(8,128)S(1)}, u32[]{:S(2)}, u32[]{:S(2)}) collective-permute-start(f32[3,20,128]{2,1,0:T(8,128)S(1)} %slice.343), channel_id=1, source_target_pairs={{0,1},{1,2},{2,3},{3,4},{4,5},{5,6},{6,7},{7,8},{8,9},{9,10},{10,1... | collective-permute-start | bytes 92168 | tf_op jit(solution)/shard_map/ppermute | solution.py:20
  227.0 6.0 %collective-permute-start.1 = (f32[3,20,128]{2,1,0:T(8,128)S(1)}, f32[3,20,128]{2,1,0:T(8,128)S(1)}, u32[]{:S(2)}, u32[]{:S(2)}) collective-permute-start(f32[3,20,128]{2,1,0:T(8,128)S(1)} %slice.343), channel_id=1, source_target_pairs={{1,0},{2,1},{3,2},{4,3},{5,4},{6,5},{7,6},{8,7},{9,8},{10,9},{11,1... | collective-permute-start | bytes 92168 | tf_op jit(solution)/shard_map/ppermute | solution.py:23
  245.6 8.0 %collective-permute-start.4 = (f32[3,20,128]{2,1,0:T(8,128)S(1)}, f32[3,20,128]{2,1,0:T(8,128)S(1)}, u32[]{:S(2)}, u32[]{:S(2)}) collective-permute-start(f32[3,20,128]{2,1,0:T(8,128)S(1)} %fusion.49), channel_id=1, source_target_pairs={{0,1},{1,2},{2,3},{3,4},{4,5},{5,6},{6,7},{7,8},{8,9},{9,10},{10,1... | collective-permute-start | bytes 92168 | tf_op jit(solution)/shard_map/ppermute | solution.py:20
  247.5 6.0 %collective-permute-start.5 = (f32[3,20,128]{2,1,0:T(8,128)S(1)}, f32[3,20,128]{2,1,0:T(8,128)S(1)}, u32[]{:S(2)}, u32[]{:S(2)}) collective-permute-start(f32[3,20,128]{2,1,0:T(8,128)S(1)} %fusion.49), channel_id=1, source_target_pairs={{1,0},{2,1},{3,2},{4,3},{5,4},{6,5},{7,6},{8,7},{9,8},{10,9},{11,1... | collective-permute-start | bytes 92168 | tf_op jit(solution)/shard_map/ppermute | solution.py:23
  261.5 8.0 %collective-permute-start.6 = (f32[3,20,128]{2,1,0:T(8,128)S(1)}, f32[3,20,128]{2,1,0:T(8,128)S(1)}, u32[]{:S(2)}, u32[]{:S(2)}) collective-permute-start(f32[3,20,128]{2,1,0:T(8,128)S(1)} %fusion.44), channel_id=1, source_target_pairs={{0,1},{1,2},{2,3},{3,4},{4,5},{5,6},{6,7},{7,8},{8,9},{9,10},{10,1... | collective-permute-start | bytes 92168 | tf_op jit(solution)/shard_map/ppermute | solution.py:20
  266.9 4.7 collective-permute-start.7
  279.5 7.5 %collective-permute-start.8 = (f32[3,20,128]{2,1,0:T(8,128)S(1)}, f32[3,20,128]{2,1,0:T(8,128)S(1)}, u32[]{:S(2)}, u32[]{:S(2)}) collective-permute-start(f32[3,20,128]{2,1,0:T(8,128)S(1)} %fusion.39), channel_id=1, source_target_pairs={{0,1},{1,2},{2,3},{3,4},{4,5},{5,6},{6,7},{7,8},{8,9},{9,10},{10,1... | collective-permute-start | bytes 92168 | tf_op jit(solution)/shard_map/ppermute | solution.py:20
  284.1 4.7 collective-permute-start.9
  296.7 7.5 %collective-permute-start.10 = (f32[3,20,128]{2,1,0:T(8,128)S(1)}, f32[3,20,128]{2,1,0:T(8,128)S(1)}, u32[]{:S(2)}, u32[]{:S(2)}) collective-permute-start(f32[3,20,128]{2,1,0:T(8,128)S(1)} %fusion.34), channel_id=1, source_target_pairs={{0,1},{1,2},{2,3},{3,4},{4,5},{5,6},{6,7},{7,8},{8,9},{9,10},{10,1... | collective-permute-start | bytes 92168 | tf_op jit(solution)/shard_map/ppermute | solution.py:20
  301.3 4.7 collective-permute-start.11
  313.9 7.5 %collective-permute-start.12 = (f32[3,20,128]{2,1,0:T(8,128)S(1)}, f32[3,20,128]{2,1,0:T(8,128)S(1)}, u32[]{:S(2)}, u32[]{:S(2)}) collective-permute-start(f32[3,20,128]{2,1,0:T(8,128)S(1)} %fusion.29), channel_id=1, source_target_pairs={{0,1},{1,2},{2,3},{3,4},{4,5},{5,6},{6,7},{7,8},{8,9},{9,10},{10,1... | collective-permute-start | bytes 92168 | tf_op jit(solution)/shard_map/ppermute | solution.py:20
  318.5 4.7 collective-permute-start.13
  330.5 70.8 %copy-start.2 = (f32[9,1024]{1,0:T(8,128)S(1)}, f32[9,1024]{1,0:T(8,128)}, u32[]{:S(2)}) copy-start(f32[9,1024]{1,0:T(8,128)} %param.38) | copy-start | bytes 110596
  331.1 8.8 %collective-permute-start.14 = (f32[3,20,128]{2,1,0:T(8,128)S(1)}, f32[3,20,128]{2,1,0:T(8,128)S(1)}, u32[]{:S(2)}, u32[]{:S(2)}) collective-permute-start(f32[3,20,128]{2,1,0:T(8,128)S(1)} %fusion.24), channel_id=1, source_target_pairs={{0,1},{1,2},{2,3},{3,4},{4,5},{5,6},{6,7},{7,8},{8,9},{9,10},{10,1... | collective-permute-start | bytes 92168 | tf_op jit(solution)/shard_map/ppermute | solution.py:20
  335.7 5.0 collective-permute-start.15
  341.5 60.1 %copy-start.3 = (f32[3,4,1024]{2,1,0:T(4,128)S(1)}, f32[3,4,1024]{2,1,0:T(4,128)}, u32[]{:S(2)}) copy-start(f32[3,4,1024]{2,1,0:T(4,128)} %param.39) | copy-start | bytes 147460
  348.6 11.7 %collective-permute-start.16 = (f32[3,20,128]{2,1,0:T(8,128)S(1)}, f32[3,20,128]{2,1,0:T(8,128)S(1)}, u32[]{:S(2)}, u32[]{:S(2)}) collective-permute-start(f32[3,20,128]{2,1,0:T(8,128)S(1)} %fusion.19), channel_id=1, source_target_pairs={{0,1},{1,2},{2,3},{3,4},{4,5},{5,6},{6,7},{7,8},{8,9},{9,10},{10,1... | collective-permute-start | bytes 92168 | tf_op jit(solution)/shard_map/ppermute | solution.py:20
  352.9 8.0 %collective-permute-start.17 = (f32[3,20,128]{2,1,0:T(8,128)S(1)}, f32[3,20,128]{2,1,0:T(8,128)S(1)}, u32[]{:S(2)}, u32[]{:S(2)}) collective-permute-start(f32[3,20,128]{2,1,0:T(8,128)S(1)} %fusion.19), channel_id=1, source_target_pairs={{1,0},{2,1},{3,2},{4,3},{5,4},{6,5},{7,6},{8,7},{9,8},{10,9},{11,1... | collective-permute-start | bytes 92168 | tf_op jit(solution)/shard_map/ppermute | solution.py:23
  370.2 45.3 %all-to-all-start.3 = ((f32[120,128,4]{0,2,1:T(4,128)}), f32[120,128,4]{0,2,1:T(4,128)S(1)}, u32[]{:S(2)}, u32[]{:S(2)}) async-start(f32[120,128,4]{0,2,1:T(4,128)} %bitcast.210), calls=%async_computation.3 | async-start | bytes 524288 | tf_op jit(solution)/shard_map/all_to_all | solution.py:237
  417.9 12.9 %collective-permute-start.18 = (f32[3,20,64]{2,1,0:T(8,128)S(1)}, f32[3,20,64]{2,1,0:T(8,128)S(1)}, u32[]{:S(2)}, u32[]{:S(2)}) collective-permute-start(f32[3,20,64]{2,1,0:T(8,128)S(1)} %get-tuple-element.18), channel_id=1, source_target_pairs={{0,1},{1,2},{2,3},{3,4},{4,5},{5,6},{6,7},{7,8},{8,9},{9,10},{10,1... | collective-permute-start | bytes 46088 | tf_op jit(solution)/shard_map/ppermute | solution.py:20
  419.8 11.0 %collective-permute-start.19 = (f32[3,20,64]{2,1,0:T(8,128)S(1)}, f32[3,20,64]{2,1,0:T(8,128)S(1)}, u32[]{:S(2)}, u32[]{:S(2)}) collective-permute-start(f32[3,20,64]{2,1,0:T(8,128)S(1)} %get-tuple-element.17), channel_id=1, source_target_pairs={{1,0},{2,1},{3,2},{4,3},{5,4},{6,5},{7,6},{8,7},{9,8},{10,9},{11,1... | collective-permute-start | bytes 46088 | tf_op jit(solution)/shard_map/ppermute | solution.py:23
  481.8 8.0 %collective-permute-start.20 = (f32[3,20,64]{2,1,0:T(8,128)S(1)}, f32[3,20,64]{2,1,0:T(8,128)S(1)}, u32[]{:S(2)}, u32[]{:S(2)}) collective-permute-start(f32[3,20,64]{2,1,0:T(8,128)S(1)} %get-tuple-element.16), channel_id=1, source_target_pairs={{0,1},{1,2},{2,3},{3,4},{4,5},{5,6},{6,7},{7,8},{8,9},{9,10},{10,1... | collective-permute-start | bytes 46088 | tf_op jit(solution)/shard_map/ppermute | solution.py:20
  483.8 6.1 %collective-permute-start.21 = (f32[3,20,64]{2,1,0:T(8,128)S(1)}, f32[3,20,64]{2,1,0:T(8,128)S(1)}, u32[]{:S(2)}, u32[]{:S(2)}) collective-permute-start(f32[3,20,64]{2,1,0:T(8,128)S(1)} %get-tuple-element.15), channel_id=1, source_target_pairs={{1,0},{2,1},{3,2},{4,3},{5,4},{6,5},{7,6},{8,7},{9,8},{10,9},{11,1... | collective-permute-start | bytes 46088 | tf_op jit(solution)/shard_map/ppermute | solution.py:23
  (5 other events, 141.8 us)
where the time goes:
time: 548 us; the launch traced here: 541 us
  local copies, waits for them, and re-layouts  311 us (57%)
  starting transfers between devices  157 us (29%)
  waiting for transfers between devices  39.5 us (7%)
  other arithmetic  23.1 us (4%)
  matrix products  7.77 us (1%)
    gather x4, local copies, waits for them, and re-layouts, exterior_local(): flat_traces[:, :, pool_index]  80.8 us
    gather x26, local copies, waits for them, and re-layouts, traces_of(): return vector_field[:, face_nodes, :]  49.6 us
    ppermute x11, starting transfers between devices, with_halo(): lax.ppermute(lax.slice_in_dim(block, 0, width, axis=dim), axis, backward)  45.9 us
    gather x3, local copies, waits for them, and re-layouts, per_device(): flat_traces[:, :, pool_index[:, safe_rows]]  45 us
    ppermute x11, starting transfers between devices, with_halo(): lax.ppermute(lax.slice_in_dim(block, block.shape[dim] - width, None, axis...  39.9 us
    all_to_all x1, starting transfers between devices, per_device(): lax.all_to_all(outgoing_back, 'dom', split_axis=1, concat_axis=1, tiled=T...  31 us
    gather x16, local copies, waits for them, and re-layouts, fine_outside(): return jnp.where(frozen, held_part, flat_pool[:, :, fine_pool_index])  29.5 us
    reshape x8, local copies, waits for them, and re-layouts, fine_outside(): traces_of(pool_field, face_nodes).reshape(3, trace_count, 4 * pool_width)  21.9 us
  transfers between devices with their start and end apart: 26, of which 9 were waited for; matrix products, arithmetic and copies ran while one was open for 33% of the time, Pallas kernels for 0%

commit v1 on v0

v1 whole, which is shorter than its diff:
```python
import functools

import jax
import jax.numpy as jnp
import numpy as np
from jax import lax
from jax.experimental import pallas as pl
from jax.experimental.pallas import tpu as pltpu
from jax.sharding import PartitionSpec as P

SUBSTEPS = 4
COARSE_STEP = 0.2
FINE_STEP = COARSE_STEP / SUBSTEPS
LANES = 128
VMEM_BYTES = 48 * 2**20
RING = ("dom", "sub")
highest = lax.Precision.HIGHEST


def face_table():
    places = [
        (along_r, along_s, along_t)
        for along_t in range(4)
        for along_s in range(4 - along_t)
        for along_r in range(4 - along_t - along_s)
    ]
    bottom = [i for i, at in enumerate(places) if at[2] == 0]
    front = [i for i, at in enumerate(places) if at[1] == 0]
    slanted = [i for i, at in enumerate(places) if sum(at) == 3]
    beside = [i for i, at in enumerate(places) if at[0] == 0]
    return [bottom, front, slanted, beside]


def runs_of(nodes):
    runs = []
    for place, node in enumerate(nodes):
        if runs and runs[-1][1] + runs[-1][2] == node:
            runs[-1][2] += 1
        else:
            runs.append([place, node, 1])
    return runs


RUNS = [runs_of(nodes) for nodes in face_table()]


def take(block, lane):
    return jnp.take_along_axis(block, lane, axis=1, mode="promise_in_bounds")


def rows8(row):
    return jnp.broadcast_to(row, (8, LANES))


def lanes_at(block):
    if isinstance(block, int):
        return slice(block * LANES, (block + 1) * LANES)
    return pl.ds(pl.multiple_of(block * LANES, LANES), LANES)


def gather32(sources, which, lane, start):
    groups = list(start)
    for number, source in enumerate(sources):
        hit = which == number
        for group in range(4):
            groups[group] = jnp.where(hit, take(source(group), lane), groups[group])
    return groups


def spread_normals(normal_rows, out_ref):
    for c in range(3):
        for f in range(4):
            out_ref[c, f * 10 : f * 10 + 10, :] = jnp.broadcast_to(normal_rows(c, f), (10, LANES))


def regroup(jump_ref, sorted_ref):
    for f in range(4):
        for c in range(3):
            sorted_ref[c, f * 10 : f * 10 + 10, :] = jump_ref[f, c * 10 : c * 10 + 10, :]


def crossed(normals, jumps):
    def part(c):
        a, b = (c + 1) % 3, (c + 2) % 3
        return normals[a] * jumps[b] - normals[b] * jumps[a]

    return [part(c) for c in range(3)]


def curl_part(c, factor, grad):
    m, n = (c + 1) % 3, (c + 2) % 3
    total = factor(m, 0) * grad(0, n) - factor(n, 0) * grad(0, m)
    for a in (1, 2):
        total += factor(m, a) * grad(a, n) - factor(n, a) * grad(a, m)
    return total


def stack_derivatives(derivatives_ref, out_ref):
    out_ref[...] = jnp.zeros_like(out_ref)
    for a in range(3):
        out_ref[a * 24 : a * 24 + 20, :] = derivatives_ref[a]


def dot(a, b):
    return jnp.dot(a, b, precision=highest, preferred_element_type=jnp.float32)


def inverse_of(row_of, count, width, none):
    columns = [
        jnp.transpose(jnp.broadcast_to(row_of(b), (LANES, LANES))) for b in range(count)
    ]
    lane = lax.broadcasted_iota(jnp.int32, (LANES, LANES), 1)
    number = lax.broadcasted_iota(jnp.int32, (LANES, LANES), 0)
    out = []
    for w in range(width):
        best = jnp.full((LANES, LANES), none, jnp.int32)
        for b in range(count):
            best = jnp.maximum(
                best, jnp.where(columns[b] == lane + w * LANES, number + b * LANES, none)
            )
        out.append(jnp.max(best, axis=0, keepdims=True))
    return out


def pack_kernel(
    fields_ref, geometry_ref, normals_ref, scale_ref, nbr_ref, send_ref,
    out_ref, ends_ref, home_ref,
    flat_ref, nb_ref, pool_ref, feature_ref,
):
    own = fields_ref.shape[2]
    for c in range(6):
        flat_ref[c * 20 : c * 20 + 20, :] = fields_ref[c]
    flat_ref[120:129, :] = geometry_ref[...]
    for c in range(3):
        flat_ref[129 + 4 * c : 133 + 4 * c, :] = normals_ref[c] * scale_ref[...]
    flat_ref[141:144, :] = jnp.zeros((3, own), jnp.float32)
    nb_ref[0:4, :] = nbr_ref[...]
    nb_ref[4:8, :] = nbr_ref[...]
    low_half = lax.broadcasted_iota(jnp.int32, (20, LANES), 1) < LANES // 2
    for c in range(3):
        ends_ref[c * 20 : c * 20 + 20, :] = jnp.where(
            low_half, fields_ref[c, :, 0:LANES], fields_ref[c, :, own - LANES : own]
        )
    ends_ref[60:64, :] = jnp.zeros((4, LANES), jnp.float32)
    for eh in range(2):
        for f in range(4):
            for c in range(3):
                for place, node, length in RUNS[f]:
                    pool_ref[eh, f, c * 10 + place : c * 10 + place + length, :] = fields_ref[
                        eh * 3 + c, node : node + length, :
                    ]
            pool_ref[eh, f, 30:32, :] = jnp.zeros((2, own), jnp.float32)
    blocks = own // LANES
    sublane = lax.broadcasted_iota(jnp.int32, (8, LANES), 0)

    def slots(sb, carry):
        row = rows8(jnp.minimum(send_ref[pl.ds(sb, 1), :], own - 1))
        lane, which = row & (LANES - 1), row >> 7
        hits = [which == b for b in range(blocks)]
        for group in range(18):
            value = take(flat_ref[group * 8 : group * 8 + 8, 0:LANES], lane)
            for b in range(1, blocks):
                value = jnp.where(
                    hits[b], take(flat_ref[group * 8 : group * 8 + 8, lanes_at(b)], lane), value
                )
            feature_ref[group * 8 : group * 8 + 8, lanes_at(sb)] = value
        nbr = take(nb_ref[:, 0:LANES], lane)
        for b in range(1, blocks):
            nbr = jnp.where(hits[b], take(nb_ref[:, lanes_at(b)], lane), nbr)
        wall = jnp.where(nbr == 4 * row + sublane, -1.0, 1.0)
        for f in range(4):
            code = rows8(nbr[f : f + 1, :])
            sign = rows8(wall[f : f + 1, :])
            lane_f = (code >> 2) & (LANES - 1)
            which_f = (code & 3) * blocks + (code >> 9)
            groups = [jnp.zeros((8, LANES), jnp.float32)] * 8
            for number in range(4 * blocks):
                hit = which_f == number
                for group in range(8):
                    block = pool_ref[
                        group // 4,
                        number // blocks,
                        group % 4 * 8 : group % 4 * 8 + 8,
                        lanes_at(number % blocks),
                    ]
                    groups[group] = jnp.where(hit, take(block, lane_f), groups[group])
            for group in range(8):
                value = groups[group] * sign if group < 4 else groups[group]
                length = 8 if group % 4 < 3 else 6
                at = 144 + (group // 4 * 4 + f) * 30 + group % 4 * 8
                feature_ref[at : at + length, lanes_at(sb)] = value[:length]
        return carry

    lax.fori_loop(0, send_ref.shape[0], slots, 0)
    out_ref[...] = jnp.transpose(feature_ref[...])
    homes = inverse_of(lambda b: send_ref[b : b + 1, :], send_ref.shape[0], blocks, -1)
    for b in range(blocks):
        home_ref[b : b + 1, :] = homes[b]


def fine_pool(state_ref, pool_ref):
    for f in range(4):
        for c in range(3):
            for place, node, length in RUNS[f]:
                pool_ref[f, c * 10 + place : c * 10 + place + length, :] = state_ref[
                    node : node + length, lanes_at(c)
                ]
        pool_ref[f, 30:32, :] = jnp.zeros((2, LANES), jnp.float32)


def exported(pool_ref, lane):
    face = lax.broadcasted_iota(jnp.int32, (8, LANES), 1) & 3
    zero = jnp.zeros((8, LANES), jnp.float32)
    return gather32(
        [lambda g, f=f: pool_ref[f, g * 8 : g * 8 + 8, :] for f in range(4)], face, lane, [zero] * 4
    )


def unpack_kernel(
    received_ref, slots_ref, nbr_ref, export_ref, ends_ref,
    efield_ref, hfield_ref, normal_ref, geometry_ref, held_ref, pool_ref, halo_ref, lane_ref,
    back_ref,
    feature_ref, picked_ref, small_ref,
):
    slot_blocks = received_ref.shape[0] // LANES
    feature_ref[...] = jnp.transpose(received_ref[...])
    slot = rows8(slots_ref[...])
    lane, which = slot & (LANES - 1), slot >> 7
    hits = [which == b for b in range(slot_blocks)]
    for group in range(feature_ref.shape[0] // 8):
        at = slice(group * 8, group * 8 + 8)
        value = take(feature_ref[at, 0:LANES], lane)
        for b in range(1, slot_blocks):
            value = jnp.where(hits[b], take(feature_ref[at, lanes_at(b)], lane), value)
        picked_ref[at, :] = value
    for c in range(3):
        efield_ref[:, lanes_at(c)] = picked_ref[c * 20 : c * 20 + 20, :]
        hfield_ref[:, lanes_at(c)] = picked_ref[60 + c * 20 : 80 + c * 20, :]
    geometry_ref[...] = picked_ref[120:136, :]
    spread_normals(
        lambda c, f: picked_ref[129 + 4 * c + f : 130 + 4 * c + f, :], normal_ref
    )
    frozen_code = 4 * LANES + 4 * 2 * export_ref.shape[1]
    for f in range(4):
        frozen = jnp.broadcast_to(nbr_ref[f : f + 1, :] == frozen_code, (30, LANES))
        for eh in range(2):
            at = 144 + (eh * 4 + f) * 30
            held_ref[eh, f, 0:30, :] = jnp.where(frozen, picked_ref[at : at + 30, :], 0.0)
            held_ref[eh, f, 30:32, :] = jnp.zeros((2, LANES), jnp.float32)
    width = export_ref.shape[1]
    small_ref[...] = jnp.zeros_like(small_ref)
    small_ref[0:2, 0:width] = export_ref[...]
    place = lax.broadcasted_iota(jnp.int32, (8, LANES), 1)
    both = take(small_ref[...], (place >> 2) & (width - 1))
    lane_ref[...] = jnp.where(place < LANES // 2, rows8(both[1:2, :]), rows8(both[0:1, :]))
    fine_pool(efield_ref, pool_ref)
    groups = exported(pool_ref, lane_ref[...])
    for g in range(4):
        halo_ref[g * 8 : g * 8 + 8, :] = groups[g]
    halo_ref[32:96, :] = ends_ref[...]
    backs = inverse_of(lambda b: slots_ref[...], 1, slot_blocks, 0)
    for b in range(slot_blocks):
        back_ref[b : b + 1, :] = backs[b]


def fine_rate(
    source_ref, pool_ref, low_ref, high_ref, held_ref, normal_ref, geometry_ref, nbr_ref,
    derivatives_ref, lift_ref,
    stack_ref, jump_ref, sorted_ref, flux_ref,
):
    stack_derivatives(derivatives_ref, stack_ref)
    grads = dot(stack_ref[...], source_ref[...])
    half = lax.broadcasted_iota(jnp.int32, (8, LANES), 1) < LANES // 2
    halo = [
        jnp.where(half, low_ref[g * 8 : g * 8 + 8, :], high_ref[g * 8 : g * 8 + 8, :])
        for g in range(4)
    ]
    sources = [lambda g, f=f: pool_ref[f, g * 8 : g * 8 + 8, :] for f in range(4)]
    sources.append(lambda g: halo[g])
    for f in range(4):
        code = rows8(nbr_ref[f : f + 1, :])
        local = code < 4 * LANES
        which = jnp.where(local, code & 3, code >> 7)
        lane = jnp.where(local, code >> 2, code) & (LANES - 1)
        groups = gather32(
            sources, which, lane, [held_ref[f, g * 8 : g * 8 + 8, :] for g in range(4)]
        )
        for g in range(4):
            jump_ref[f, g * 8 : g * 8 + 8, :] = groups[g] - pool_ref[f, g * 8 : g * 8 + 8, :]
    regroup(jump_ref, sorted_ref)
    flux = crossed([normal_ref[c] for c in range(3)], [sorted_ref[c] for c in range(3)])
    for c in range(3):
        flux_ref[:, lanes_at(c)] = flux[c]
    lifted = dot(0.5 * lift_ref[...], flux_ref[...])

    def factor(m, a):
        return geometry_ref[3 * m + a : 3 * m + a + 1, :]

    def grad(a, c):
        return grads[a * 24 : a * 24 + 20, c * LANES : (c + 1) * LANES]

    return [
        curl_part(c, factor, grad) + lifted[:, c * LANES : (c + 1) * LANES] for c in range(3)
    ]


def fine_kernel(
    magnetic,
    source_ref, target_ref, pool_ref, low_ref, high_ref, held_ref, normal_ref, geometry_ref,
    nbr_ref, lane_ref, derivatives_ref, lift_ref,
    out_ref, new_pool_ref, halo_ref,
    *scratch,
):
    field = 0 if magnetic else 1
    step = -FINE_STEP if magnetic else FINE_STEP
    rate = fine_rate(
        source_ref, pool_ref, low_ref, high_ref, held_ref.at[field], normal_ref, geometry_ref,
        nbr_ref, derivatives_ref, lift_ref, *scratch,
    )
    for c in range(3):
        out_ref[:, lanes_at(c)] = target_ref[:, lanes_at(c)] + step * rate[c]
    fine_pool(out_ref, new_pool_ref)
    groups = exported(new_pool_ref, lane_ref[...])
    for g in range(4):
        halo_ref[g * 8 : g * 8 + 8, :] = groups[g]


def last_fine_kernel(
    source_ref, target_ref, pool_ref, low_ref, high_ref, held_ref, normal_ref, geometry_ref,
    nbr_ref, back_ref, derivatives_ref, lift_ref,
    out_ref,
    result_ref, feature_ref,
    *scratch,
):
    rate = fine_rate(
        source_ref, pool_ref, low_ref, high_ref, held_ref.at[1], normal_ref, geometry_ref,
        nbr_ref, derivatives_ref, lift_ref, *scratch,
    )
    for c in range(3):
        result_ref[c * 20 : c * 20 + 20, :] = target_ref[:, lanes_at(c)] + FINE_STEP * rate[c]
        result_ref[60 + c * 20 : 80 + c * 20, :] = source_ref[:, lanes_at(c)]
    result_ref[120:128, :] = jnp.zeros((8, LANES), jnp.float32)
    for b in range(back_ref.shape[0]):
        lane = rows8(back_ref[b : b + 1, :])
        for g in range(16):
            feature_ref[g * 8 : g * 8 + 8, lanes_at(b)] = take(
                result_ref[g * 8 : g * 8 + 8, :], lane
            )
    out_ref[...] = jnp.transpose(feature_ref[...])


def coarse_pool(field_ref, first, pool_ref):
    own = field_ref.shape[2]
    for f in range(4):
        for c in range(3):
            for place, node, length in RUNS[f]:
                pool_ref[f, c * 10 + place : c * 10 + place + length, 0:own] = field_ref[
                    first + c, node : node + length, :
                ]


def halo_rows(below, above):
    half = lax.broadcasted_iota(jnp.int32, below.shape, 1) >= LANES // 2
    return pltpu.roll(jnp.where(half, below, above), LANES // 2, 1)


def coarse_halo(halo, store):
    for f in range(4):
        for c in range(3):
            for place, node, length in RUNS[f]:
                store(f, c * 10 + place, length, halo[c * 20 + node : c * 20 + node + length, :])


def coarse_flux(
    blocks, mirror, nbr_ref, normals_ref, scale_ref, pool_ref, flux_ref, jump_ref, sorted_ref,
    spread_ref,
):
    own_blocks = flux_ref.shape[2] // LANES
    sources = [
        lambda g, n=n: pool_ref[n // blocks, g * 8 : g * 8 + 8, lanes_at(n % blocks)]
        for n in range(4 * blocks)
    ]
    lane_number = lax.broadcasted_iota(jnp.int32, (8, LANES), 1)
    zero = jnp.zeros((8, LANES), jnp.float32)

    def one(eb, carry):
        at = lanes_at(eb)
        for f in range(4):
            code = rows8(nbr_ref[f : f + 1, at])
            block = code >> 9
            which = jnp.where(block < blocks, (code & 3) * blocks + block, 4 * blocks)
            groups = gather32(sources, which, (code >> 2) & (LANES - 1), [zero] * 4)
            if mirror:
                wall = code == 4 * (lane_number + eb * LANES) + f
                sign = jnp.where(wall, -1.0, 1.0)
                groups = [group * sign for group in groups]
            for g in range(4):
                jump_ref[f, g * 8 : g * 8 + 8, :] = (
                    groups[g] - pool_ref[f, g * 8 : g * 8 + 8, at]
                )
        regroup(jump_ref, sorted_ref)
        scale = scale_ref[:, at]
        scaled = [normals_ref[c, :, at] * scale for c in range(3)]
        spread_normals(lambda c, f: scaled[c][f : f + 1, :], spread_ref)
        flux = crossed([spread_ref[c] for c in range(3)], [sorted_ref[c] for c in range(3)])
        for c in range(3):
            flux_ref[c, :, at] = flux[c]
        return carry

    lax.fori_loop(0, own_blocks, one, 0)


def coarse_update(
    step, source, target, out, geometry_ref, derivatives_ref, lift_ref, stack_ref, flux_ref,
    grad_ref, lifted_ref,
):
    own_blocks = flux_ref.shape[2] // LANES
    stack_derivatives(derivatives_ref, stack_ref)
    lift = 0.5 * lift_ref[...]
    for c in range(3):
        grad_ref[c] = dot(stack_ref[...], source(c))
        lifted_ref[c] = dot(lift, flux_ref[c])

    def one(eb, carry):
        at = lanes_at(eb)

        def factor(m, a):
            return geometry_ref[3 * m + a : 3 * m + a + 1, at]

        def grad(a, c):
            return grad_ref[c, a * 24 : a * 24 + 20, at]

        for c in range(3):
            out(c, at, target(c, at) + step * (curl_part(c, factor, grad) + lifted_ref[c, :, at]))
        return carry

    lax.fori_loop(0, own_blocks, one, 0)


def coarse_magnetic_kernel(
    returned_ref, home_ref, fields_ref, below_ref, above_ref, geometry_ref, normals_ref,
    scale_ref, nbr_ref, derivatives_ref, lift_ref,
    merged_ref, ends_ref,
    flat_ref, back_ref, pool_ref, flux_ref, jump_ref, sorted_ref, spread_ref, stack_ref,
    grad_ref, lifted_ref,
):
    own = fields_ref.shape[2]
    slot_blocks = returned_ref.shape[0] // LANES
    back_ref[...] = jnp.transpose(returned_ref[...])
    for c in range(6):
        flat_ref[c * 20 : c * 20 + 20, :] = fields_ref[c]

    def merge(eb, carry):
        at = lanes_at(eb)
        home = rows8(home_ref[pl.ds(eb, 1), :])
        lane = home & (LANES - 1)
        hits = [(home >> 7) == b for b in range(slot_blocks)]
        for group in range(15):
            rows = slice(group * 8, group * 8 + 8)
            value = flat_ref[rows, at]
            for b in range(slot_blocks):
                value = jnp.where(hits[b], take(back_ref[rows, lanes_at(b)], lane), value)
            flat_ref[rows, at] = value
        return carry

    lax.fori_loop(0, own // LANES, merge, 0)
    for c in range(6):
        merged_ref[c] = flat_ref[c * 20 : c * 20 + 20, :]
    coarse_pool(merged_ref, 0, pool_ref)
    halo = halo_rows(below_ref[32:96, :], above_ref[32:96, :])

    def store(f, place, length, value):
        pool_ref[f, place : place + length, own : own + LANES] = value

    coarse_halo(halo, store)
    coarse_flux(
        own // LANES + 1, True, nbr_ref, normals_ref, scale_ref, pool_ref, flux_ref, jump_ref,
        sorted_ref, spread_ref,
    )

    def out(c, at, value):
        merged_ref[3 + c, :, at] = value

    coarse_update(
        -COARSE_STEP, lambda c: merged_ref[c], lambda c, at: merged_ref[3 + c, :, at], out,
        geometry_ref, derivatives_ref, lift_ref, stack_ref, flux_ref, grad_ref, lifted_ref,
    )
    low_half = lax.broadcasted_iota(jnp.int32, (20, LANES), 1) < LANES // 2
    for c in range(3):
        ends_ref[c * 20 : c * 20 + 20, :] = jnp.where(
            low_half, merged_ref[3 + c, :, 0:LANES], merged_ref[3 + c, :, own - LANES : own]
        )
    ends_ref[60:64, :] = jnp.zeros((4, LANES), jnp.float32)


def coarse_electric_kernel(
    merged_ref, geometry_ref, normals_ref, scale_ref, nbr_ref, derivatives_ref, lift_ref,
    out_ref,
    pool_ref, flux_ref, jump_ref, sorted_ref, spread_ref, stack_ref, grad_ref, lifted_ref,
):
    own = merged_ref.shape[2]
    coarse_pool(merged_ref, 3, pool_ref)
    coarse_flux(
        own // LANES, False, nbr_ref, normals_ref, scale_ref, pool_ref, flux_ref, jump_ref,
        sorted_ref, spread_ref,
    )

    def out(c, at, value):
        out_ref[c, :, at] = value

    coarse_update(
        COARSE_STEP, lambda c: merged_ref[3 + c], lambda c, at: merged_ref[c, :, at], out,
        geometry_ref, derivatives_ref, lift_ref, stack_ref, flux_ref, grad_ref, lifted_ref,
    )


def finish_kernel(
    merged_ref, electric_ref, below_ref, above_ref, normals_ref, scale_ref, nbr_ref, lift_ref,
    out_ref,
    pool_ref, flux_ref, jump_ref, sorted_ref, spread_ref,
):
    own = merged_ref.shape[2]
    halo = halo_rows(below_ref[...], above_ref[...])

    def store(f, place, length, value):
        pool_ref[f, place : place + length, :] = value

    coarse_halo(halo, store)
    zero = jnp.zeros((8, LANES), jnp.float32)
    sources = [lambda g, f=f: pool_ref[f, g * 8 : g * 8 + 8, :] for f in range(4)]
    ends = (0, own // LANES - 1)
    for number, eb in enumerate(ends):
        at = lanes_at(eb)
        for f in range(4):
            code = rows8(nbr_ref[f : f + 1, at])
            which = jnp.where(code >= 4 * own, code & 3, 4)
            groups = gather32(sources, which, (code >> 2) & (LANES - 1), [zero] * 4)
            for g in range(4):
                jump_ref[f, g * 8 : g * 8 + 8, :] = groups[g]
        regroup(jump_ref, sorted_ref)
        scale = scale_ref[:, at]
        scaled = [normals_ref[c, :, at] * scale for c in range(3)]
        spread_normals(lambda c, f: scaled[c][f : f + 1, :], spread_ref)
        flux = crossed([spread_ref[c] for c in range(3)], [sorted_ref[c] for c in range(3)])
        for c in range(3):
            flux_ref[:, lanes_at(number * 3 + c)] = flux[c]
    lifted = dot(0.5 * lift_ref[...], flux_ref[...])
    for c in range(3):
        out_ref[c, :, LANES : own - LANES] = electric_ref[c, :, LANES : own - LANES]
        for number, eb in enumerate(ends):
            at = (number * 3 + c) * LANES
            out_ref[c, :, lanes_at(eb)] = (
                electric_ref[c, :, lanes_at(eb)] + COARSE_STEP * lifted[:, at : at + LANES]
            )
        out_ref[3 + c] = merged_ref[3 + c]


def call(kernel, outs, scratch, *args):
    whole = pl.BlockSpec(memory_space=pltpu.VMEM)
    return pl.pallas_call(
        kernel,
        out_shape=[jax.ShapeDtypeStruct(shape, dtype) for shape, dtype in outs],
        in_specs=[whole] * len(args),
        out_specs=[whole] * len(outs),
        scratch_shapes=[pltpu.VMEM(shape, dtype) for shape, dtype in scratch],
        compiler_params=pltpu.CompilerParams(vmem_limit_bytes=VMEM_BYTES),
    )(*args)


def exchange(block):
    count = lax.axis_size(RING)
    up = [(i, (i + 1) % count) for i in range(count)]
    down = [(target, source) for source, target in up]
    return lax.ppermute(block, RING, up), lax.ppermute(block, RING, down)


def swap_slots(rows, width):
    peers = lax.axis_size("dom")
    chunks = rows.reshape(peers, rows.shape[0] // peers, width)
    return lax.all_to_all(chunks, "dom", split_axis=0, concat_axis=0, tiled=True).reshape(
        rows.shape[0], width
    )


def per_device(
    fields, geometry, normals, face_scale, derivatives, lift_matrix, face_nbr, send_rows,
    fine_slots, export_rows, fine_nbr,
):
    f32, i32 = jnp.float32, jnp.int32
    own = fields.shape[2]
    slots = send_rows.shape[0]
    fine = fine_slots.shape[0]
    send = send_rows.reshape(slots // LANES, LANES)
    packed, ends, home = call(
        pack_kernel,
        [((slots, 384), f32), ((64, LANES), f32), ((own // LANES, LANES), i32)],
        [((144, own), f32), ((8, own), i32), ((2, 4, 32, own), f32), ((384, slots), f32)],
        fields, geometry, normals, face_scale, face_nbr, send,
    )
    received = swap_slots(packed, 384)
    state, traces = ((20, 3 * fine), f32), ((4, 32, fine), f32)
    efield, hfield, normal, factors, held, pool, halo, lane, back = call(
        unpack_kernel,
        [
            state, state, ((3, 40, fine), f32), ((16, fine), f32), ((2, 4, 32, fine), f32),
            traces, ((96, fine), f32), ((8, fine), i32), ((slots // LANES, LANES), i32),
        ],
        [((384, slots), f32), ((384, fine), f32), ((8, LANES), i32)],
        received, fine_slots.reshape(1, fine), fine_nbr, export_rows, ends,
    )
    scratch = [((72, 20), f32), traces, ((3, 40, fine), f32), ((40, 3 * fine), f32)]
    first = None
    for half in range(2 * SUBSTEPS - 1):
        below, above = exchange(halo)
        first = first or (below, above)
        magnetic = half % 2 == 0
        source, target = (efield, hfield) if magnetic else (hfield, efield)
        new, pool, halo = call(
            functools.partial(fine_kernel, magnetic),
            [state, traces, ((32, fine), f32)],
            scratch,
            source, target, pool, below, above, held, normal, factors, fine_nbr, lane,
            derivatives, lift_matrix,
        )
        efield, hfield = (efield, new) if magnetic else (new, hfield)
    below, above = exchange(halo)
    (outgoing,) = call(
        last_fine_kernel,
        [((slots, LANES), f32)],
        [((128, fine), f32), ((128, slots), f32)] + scratch,
        hfield, efield, pool, below, above, held, normal, factors, fine_nbr, back, derivatives,
        lift_matrix,
    )
    returned = swap_slots(outgoing, LANES)
    work = [
        ((3, 40, own), f32), ((4, 32, LANES), f32), ((3, 40, LANES), f32), ((3, 40, LANES), f32),
        ((72, 20), f32), ((3, 72, own), f32), ((3, 20, own), f32),
    ]
    merged, ends = call(
        coarse_magnetic_kernel,
        [((6, 20, own), f32), ((64, LANES), f32)],
        [((120, own), f32), ((128, slots), f32), ((4, 32, own + LANES), f32)] + work,
        returned, home, fields, first[0], first[1], geometry, normals, face_scale, face_nbr,
        derivatives, lift_matrix,
    )
    below, above = exchange(ends)
    (electric,) = call(
        coarse_electric_kernel,
        [((3, 20, own), f32)],
        [((4, 32, own), f32)] + work,
        merged, geometry, normals, face_scale, face_nbr, derivatives, lift_matrix,
    )
    (out,) = call(
        finish_kernel,
        [((6, 20, own), f32)],
        [
            traces, ((40, 6 * LANES), f32), ((4, 32, LANES), f32), ((3, 40, LANES), f32),
            ((3, 40, LANES), f32),
        ],
        merged, electric, below, above, normals, face_scale, face_nbr, lift_matrix,
    )
    return out


def solution(mesh):
    return jax.shard_map(
        per_device,
        mesh=mesh,
        in_specs=(
            P(None, None, ("dom", "sub")),
            P(None, ("dom", "sub")),
            P(None, None, ("dom", "sub")),
            P(None, ("dom", "sub")),
            P(),
            P(),
            P(None, ("dom", "sub")),
            P(("dom", "sub")),
            P(("dom", "sub")),
            P(None, ("dom", "sub")),
            P(None, ("dom", "sub")),
        ),
        out_specs=P(None, None, ("dom", "sub")),
        check_vma=False,
    )
```

time: 548 us -> 208 us (0.38); the launches traced: 541 us -> 207 us
  local copies, waits for them, and re-layouts: 311 us -> 6.03 us
  starting transfers between devices: 157 us -> 54.4 us
  blocking collectives: 0 us -> 74.2 us
  Pallas kernels: 0 us -> 28.4 us
  other arithmetic: 23.1 us -> 0 us
  matrix products: 7.77 us -> 0 us
    gather x62 -> x0, local copies, waits for them, and re-layouts: 223 us -> none  [the longest x4 80.8 us: exterior_local(): flat_traces[:, :, pool_index]]
    all_to_all x0 -> x2, blocking collectives: none -> 74.2 us  [swap_slots(): lax.all_to_all(chunks, 'dom', split_axis=0, concat_axis=0, tiled=True)]
    all_to_all x4 -> x0, starting transfers between devices: 71.6 us -> none  [the longest x1 31 us: per_device(): lax.all_to_all(outgoing_back, 'dom', split_axis=1, concat_axis=1, tiled=T...]
    reshape x19 -> x2, local copies, waits for them, and re-layouts: 36.5 us -> 0.5 us  [the longest x1 0.27 us: swap_slots(): lax.all_to_all(chunks, 'dom', split_axis=0, concat_axis=0, tiled=True)]
    ppermute x22 -> x18, waiting for transfers between devices: 9.1 us -> 44 us  [exchange(): return (lax.ppermute(block, RING, up), lax.ppermute(block, RING, down))]
    ppermute x22 -> x18, starting transfers between devices: 85.8 us -> 54.4 us  [exchange(): return (lax.ppermute(block, RING, up), lax.ppermute(block, RING, down))]
    all_to_all x4 -> x0, waiting for transfers between devices: 30.4 us -> none  [the longest x1 13.8 us: per_device(): lax.all_to_all(outgoing_back, 'dom', split_axis=1, concat_axis=1, tiled=T...]
    pallas_call x0 -> x13, Pallas kernels: none -> 28.4 us  [call(): pl.pallas_call(kernel, out_shape=[jax.ShapeDtypeStruct(shape, dtype) for...]
  transfers between devices with their start and end apart: 26 -> 18, of which waited for: 9 -> 8; matrix products, arithmetic and copies ran while one was open for 33% -> 0% of each run, Pallas kernels for 0% -> 3%
where the time goes in v1:
time: 208 us; the launch traced here: 207 us
  blocking collectives  74.2 us (36%)
  starting transfers between devices  54.4 us (26%)
  waiting for transfers between devices  44 us (21%)
  Pallas kernels  28.4 us (14%)
  local copies, waits for them, and re-layouts  6.03 us (3%)
    all_to_all x2, blocking collectives, swap_slots(): lax.all_to_all(chunks, 'dom', split_axis=0, concat_axis=0, tiled=True)  74.2 us
    ppermute x18, starting transfers between devices, exchange(): return (lax.ppermute(block, RING, up), lax.ppermute(block, RING, down))  54.4 us
    ppermute x18, waiting for transfers between devices, exchange(): return (lax.ppermute(block, RING, up), lax.ppermute(block, RING, down))  44 us
    pallas_call x13, Pallas kernels, call(): pl.pallas_call(kernel, out_shape=[jax.ShapeDtypeStruct(shape, dtype) for...  28.4 us
    unnamed x32, local copies, waits for them, and re-layouts  5.53 us
  transfers between devices with their start and end apart: 18, of which 8 were waited for; matrix products, arithmetic and copies ran while one was open for 0% of the time, Pallas kernels for 3%

profile of v1, /device:TPU:1, one launch (start us, length us, event | category | flops | bytes accessed | tf_op | source)
XLA Modules:
  0.0 207.4 jit_solution(4599052340058611106)
XLA Ops:
  4.8 6.6 %shard_map.109 = (f32[512,384]{1,0:T(8,128)S(1)}, f32[64,128]{1,0:T(8,128)S(1)}, s32[8,128]{1,0:T(8,128)S(1)}) custom-call(f32[6,20,1024]{2,1,0:T(8,128)S(1)} %copy-done.1, f32[9,1024]{1,0:T(8,128)S(1)} %copy-done.6, f32[3,4,1024]{2,1,0:T(4,128)S(1)} %copy-done.4, f32[4,1024]{1,0:T(4,128)S(1)} %copy-done.8, s32[4,1024]{1,0:T(4,128)S(1)} %copy-done.10, ...), custom_call_target="tpu_custom_call" | custom-call | tf_op jit(solution)/shard_map/pallas_call | solution.py:560
  11.7 43.4 %all_to_all.10 = f32[128,4,384]{2,1,0:T(4,128)S(1)} all-to-all(f32[128,4,384]{2,1,0:T(4,128)S(1)} %reshape.19), channel_id=1, replica_groups=mesh['dom'=128,'sub'=4] {'dom'}, dimensions={0} | all-to-all | bytes 1572864 | tf_op jit(solution)/shard_map/all_to_all | solution.py:580
  56.7 5.9 %collective-permute-start.1 = (f32[96,128]{1,0:T(8,128)S(1)}, f32[96,128]{1,0:T(8,128)S(1)}, u32[]{:S(2)}, u32[]{:S(2)}) collective-permute-start(f32[96,128]{1,0:T(8,128)S(1)} %get-tuple-element.45), channel_id=1, source_target_pairs={{1,0},{2,1},{3,2},{4,3},{5,4},{6,5},{7,6},{8,7},{9,8},{10,9},{11,1... | collective-permute-start | bytes 147464 | tf_op jit(solution)/shard_map/ppermute | solution.py:574
  62.6 1.9 collective-permute-start
  64.6 4.7 %collective-permute-done.low_ref.below_ref = f32[96,128]{1,0:T(8,128)S(1)} collective-permute-done((f32[96,128]{1,0:T(8,128)S(1)}, f32[96,128]{1,0:T(8,128)S(1)}, u32[]{:S(2)}, u32[]{:S(2)}) %collective-permute-start) | collective-permute-done | bytes 49184 | tf_op jit(solution)/shard_map/ppermute | solution.py:574
  69.8 2.1 %collective-permute-start.3 = (f32[32,128]{1,0:T(8,128)S(1)}, f32[32,128]{1,0:T(8,128)S(1)}, u32[]{:S(2)}, u32[]{:S(2)}) collective-permute-start(f32[32,128]{1,0:T(8,128)S(1)} %get-tuple-element.52), channel_id=1, source_target_pairs={{1,0},{2,1},{3,2},{4,3},{5,4},{6,5},{7,6},{8,7},{9,8},{10,9},{11,1... | collective-permute-start | bytes 49160 | tf_op jit(solution)/shard_map/ppermute | solution.py:574
  71.9 3.2 %collective-permute-start.2 = (f32[32,128]{1,0:T(8,128)S(1)}, f32[32,128]{1,0:T(8,128)S(1)}, u32[]{:S(2)}, u32[]{:S(2)}) collective-permute-start(f32[32,128]{1,0:T(8,128)S(1)} %get-tuple-element.52), channel_id=1, source_target_pairs={{0,1},{1,2},{2,3},{3,4},{4,5},{5,6},{6,7},{7,8},{8,9},{9,10},{10,1... | collective-permute-start | bytes 49160 | tf_op jit(solution)/shard_map/ppermute | solution.py:574
  75.1 3.1 %collective-permute-done.2.low_ref = f32[32,128]{1,0:T(8,128)S(1)} collective-permute-done((f32[32,128]{1,0:T(8,128)S(1)}, f32[32,128]{1,0:T(8,128)S(1)}, u32[]{:S(2)}, u32[]{:S(2)}) %collective-permute-start.2) | collective-permute-done | bytes 16416 | tf_op jit(solution)/shard_map/ppermute | solution.py:574
  78.7 1.9 collective-permute-start.5
  80.7 3.3 %collective-permute-start.4 = (f32[32,128]{1,0:T(8,128)S(1)}, f32[32,128]{1,0:T(8,128)S(1)}, u32[]{:S(2)}, u32[]{:S(2)}) collective-permute-start(f32[32,128]{1,0:T(8,128)S(1)} %get-tuple-element.55), channel_id=1, source_target_pairs={{0,1},{1,2},{2,3},{3,4},{4,5},{5,6},{6,7},{7,8},{8,9},{9,10},{10,1... | collective-permute-start | bytes 49160 | tf_op jit(solution)/shard_map/ppermute | solution.py:574
  84.0 4.9 %collective-permute-done.4.low_ref = f32[32,128]{1,0:T(8,128)S(1)} collective-permute-done((f32[32,128]{1,0:T(8,128)S(1)}, f32[32,128]{1,0:T(8,128)S(1)}, u32[]{:S(2)}, u32[]{:S(2)}) %collective-permute-start.4) | collective-permute-done | bytes 16416 | tf_op jit(solution)/shard_map/ppermute | solution.py:574
  89.5 4.2 %collective-permute-start.7 = (f32[32,128]{1,0:T(8,128)S(1)}, f32[32,128]{1,0:T(8,128)S(1)}, u32[]{:S(2)}, u32[]{:S(2)}) collective-permute-start(f32[32,128]{1,0:T(8,128)S(1)} %get-tuple-element.58), channel_id=1, source_target_pairs={{1,0},{2,1},{3,2},{4,3},{5,4},{6,5},{7,6},{8,7},{9,8},{10,9},{11,1... | collective-permute-start | bytes 49160 | tf_op jit(solution)/shard_map/ppermute | solution.py:574
  93.8 1.9 collective-permute-start.6
  95.7 6.2 %collective-permute-done.6.low_ref = f32[32,128]{1,0:T(8,128)S(1)} collective-permute-done((f32[32,128]{1,0:T(8,128)S(1)}, f32[32,128]{1,0:T(8,128)S(1)}, u32[]{:S(2)}, u32[]{:S(2)}) %collective-permute-start.6) | collective-permute-done | bytes 16416 | tf_op jit(solution)/shard_map/ppermute | solution.py:574
  102.5 4.2 %collective-permute-start.9 = (f32[32,128]{1,0:T(8,128)S(1)}, f32[32,128]{1,0:T(8,128)S(1)}, u32[]{:S(2)}, u32[]{:S(2)}) collective-permute-start(f32[32,128]{1,0:T(8,128)S(1)} %get-tuple-element.61), channel_id=1, source_target_pairs={{1,0},{2,1},{3,2},{4,3},{5,4},{6,5},{7,6},{8,7},{9,8},{10,9},{11,1... | collective-permute-start | bytes 49160 | tf_op jit(solution)/shard_map/ppermute | solution.py:574
  106.7 1.9 collective-permute-start.8
  108.7 6.3 %collective-permute-done.8.low_ref = f32[32,128]{1,0:T(8,128)S(1)} collective-permute-done((f32[32,128]{1,0:T(8,128)S(1)}, f32[32,128]{1,0:T(8,128)S(1)}, u32[]{:S(2)}, u32[]{:S(2)}) %collective-permute-start.8) | collective-permute-done | bytes 16416 | tf_op jit(solution)/shard_map/ppermute | solution.py:574
  115.5 4.2 %collective-permute-start.11 = (f32[32,128]{1,0:T(8,128)S(1)}, f32[32,128]{1,0:T(8,128)S(1)}, u32[]{:S(2)}, u32[]{:S(2)}) collective-permute-start(f32[32,128]{1,0:T(8,128)S(1)} %get-tuple-element.64), channel_id=1, source_target_pairs={{1,0},{2,1},{3,2},{4,3},{5,4},{6,5},{7,6},{8,7},{9,8},{10,9},{11,1... | collective-permute-start | bytes 49160 | tf_op jit(solution)/shard_map/ppermute | solution.py:574
  119.7 1.9 collective-permute-start.10
  121.6 6.3 %collective-permute-done.10.low_ref = f32[32,128]{1,0:T(8,128)S(1)} collective-permute-done((f32[32,128]{1,0:T(8,128)S(1)}, f32[32,128]{1,0:T(8,128)S(1)}, u32[]{:S(2)}, u32[]{:S(2)}) %collective-permute-start.10) | collective-permute-done | bytes 16416 | tf_op jit(solution)/shard_map/ppermute | solution.py:574
  128.4 4.2 %collective-permute-start.13 = (f32[32,128]{1,0:T(8,128)S(1)}, f32[32,128]{1,0:T(8,128)S(1)}, u32[]{:S(2)}, u32[]{:S(2)}) collective-permute-start(f32[32,128]{1,0:T(8,128)S(1)} %get-tuple-element.67), channel_id=1, source_target_pairs={{1,0},{2,1},{3,2},{4,3},{5,4},{6,5},{7,6},{8,7},{9,8},{10,9},{11,1... | collective-permute-start | bytes 49160 | tf_op jit(solution)/shard_map/ppermute | solution.py:574
  132.6 1.9 collective-permute-start.12
  134.6 6.2 %collective-permute-done.12.low_ref = f32[32,128]{1,0:T(8,128)S(1)} collective-permute-done((f32[32,128]{1,0:T(8,128)S(1)}, f32[32,128]{1,0:T(8,128)S(1)}, u32[]{:S(2)}, u32[]{:S(2)}) %collective-permute-start.12) | collective-permute-done | bytes 16416 | tf_op jit(solution)/shard_map/ppermute | solution.py:574
  141.4 4.2 %collective-permute-start.15 = (f32[32,128]{1,0:T(8,128)S(1)}, f32[32,128]{1,0:T(8,128)S(1)}, u32[]{:S(2)}, u32[]{:S(2)}) collective-permute-start(f32[32,128]{1,0:T(8,128)S(1)} %get-tuple-element.70), channel_id=1, source_target_pairs={{1,0},{2,1},{3,2},{4,3},{5,4},{6,5},{7,6},{8,7},{9,8},{10,9},{11,1... | collective-permute-start | bytes 49160 | tf_op jit(solution)/shard_map/ppermute | solution.py:574
  145.6 1.9 collective-permute-start.14
  147.5 6.3 %collective-permute-done.14.low_ref = f32[32,128]{1,0:T(8,128)S(1)} collective-permute-done((f32[32,128]{1,0:T(8,128)S(1)}, f32[32,128]{1,0:T(8,128)S(1)}, u32[]{:S(2)}, u32[]{:S(2)}) %collective-permute-start.14) | collective-permute-done | bytes 16416 | tf_op jit(solution)/shard_map/ppermute | solution.py:574
  154.5 30.9 %all_to_all.11 = f32[128,4,128]{2,1,0:T(4,128)S(1)} all-to-all(f32[128,4,128]{2,1,0:T(4,128)S(1)} %bitcast.4), channel_id=1, replica_groups=mesh['dom'=128,'sub'=4] {'dom'}, dimensions={0} | all-to-all | bytes 524288 | tf_op jit(solution)/shard_map/all_to_all | solution.py:580
  185.4 8.5 %shard_map.119 = (f32[6,20,1024]{2,1,0:T(8,128)S(1)}, f32[64,128]{1,0:T(8,128)S(1)}) custom-call(f32[512,128]{1,0:T(8,128)S(1)} %bitcast.5, s32[8,128]{1,0:T(8,128)S(1)} %get-tuple-element.72.home_ref, f32[6,20,1024]{2,1,0:T(8,128)S(1)} %copy-done.2, f32[96,128]{1,0:T(8,128)S(1)} %collective-permute-done.low_ref.below_ref, ...), custom_call_target="tpu_custom_call" | custom-call | tf_op jit(solution)/shard_map/pallas_call | solution.py:560
  194.0 1.9 collective-permute-start.17
  195.9 3.4 %collective-permute-start.16 = (f32[64,128]{1,0:T(8,128)S(1)}, f32[64,128]{1,0:T(8,128)S(1)}, u32[]{:S(2)}, u32[]{:S(2)}) collective-permute-start(f32[64,128]{1,0:T(8,128)S(1)} %get-tuple-element.74), channel_id=1, source_target_pairs={{0,1},{1,2},{2,3},{3,4},{4,5},{5,6},{6,7},{7,8},{8,9},{9,10},{10,1... | collective-permute-start | bytes 98312 | tf_op jit(solution)/shard_map/ppermute | solution.py:574
  199.3 6.7 %shard_map.120.electric_ref = f32[3,20,1024]{2,1,0:T(8,128)S(1)} custom-call(f32[6,20,1024]{2,1,0:T(8,128)S(1)} %get-tuple-element.73.merged_ref, f32[9,1024]{1,0:T(8,128)S(1)} %copy-done.7, f32[3,4,1024]{2,1,0:T(4,128)S(1)} %copy-done.5, f32[4,1024]{1,0:T(4,128)S(1)} %copy-done.9, s32[4,1024]{1,0:T(4,128)S(1)} %copy-done.11, f32[3,20,20]{2,1,0:T(8,128)S(1)} %copy-done, ...), custom_call_target="tpu_custom_call" | custom-call | tf_op jit(solution)/shard_map/pallas_call | solution.py:560
  206.0 1.4 shard_map.121
  (53 shorter events, 11.1 us)
Async XLA Ops:
  0.0 1.1 copy-start.1
  1.1 0.8 copy-start.4
  1.9 0.8 copy-start.6
  2.7 0.7 copy-start.8
  3.4 0.7 copy-start.10
  55.3 0.7 copy-start.12
  55.4 0.7 copy-start.14
  56.0 13.2 %copy-start = (f32[3,20,20]{2,1,0:T(8,128)S(1)}, f32[3,20,20]{2,1,0:T(8,128)}, u32[]{:S(2)}) copy-start(f32[3,20,20]{2,1,0:T(8,128)} %derivatives_ref.19) | copy-start | bytes 14404
  56.7 12.6 %copy-start.3 = (f32[20,40]{1,0:T(8,128)S(1)}, f32[20,40]{1,0:T(8,128)}, u32[]{:S(2)}) copy-start(f32[20,40]{1,0:T(8,128)} %lift_ref.21) | copy-start | bytes 9604
  56.7 7.9 %collective-permute-start.1 = (f32[96,128]{1,0:T(8,128)S(1)}, f32[96,128]{1,0:T(8,128)S(1)}, u32[]{:S(2)}, u32[]{:S(2)}) collective-permute-start(f32[96,128]{1,0:T(8,128)S(1)} %get-tuple-element.45), channel_id=1, source_target_pairs={{1,0},{2,1},{3,2},{4,3},{5,4},{6,5},{7,6},{8,7},{9,8},{10,9},{11,1... | collective-permute-start | bytes 147464 | tf_op jit(solution)/shard_map/ppermute | solution.py:574
  62.6 6.6 %collective-permute-start = (f32[96,128]{1,0:T(8,128)S(1)}, f32[96,128]{1,0:T(8,128)S(1)}, u32[]{:S(2)}, u32[]{:S(2)}) collective-permute-start(f32[96,128]{1,0:T(8,128)S(1)} %get-tuple-element.45), channel_id=1, source_target_pairs={{0,1},{1,2},{2,3},{3,4},{4,5},{5,6},{6,7},{7,8},{8,9},{9,10},{10,1... | collective-permute-start | bytes 147464 | tf_op jit(solution)/shard_map/ppermute | solution.py:574
  69.8 5.3 %collective-permute-start.3 = (f32[32,128]{1,0:T(8,128)S(1)}, f32[32,128]{1,0:T(8,128)S(1)}, u32[]{:S(2)}, u32[]{:S(2)}) collective-permute-start(f32[32,128]{1,0:T(8,128)S(1)} %get-tuple-element.52), channel_id=1, source_target_pairs={{1,0},{2,1},{3,2},{4,3},{5,4},{6,5},{7,6},{8,7},{9,8},{10,9},{11,1... | collective-permute-start | bytes 49160 | tf_op jit(solution)/shard_map/ppermute | solution.py:574
  71.9 6.3 %collective-permute-start.2 = (f32[32,128]{1,0:T(8,128)S(1)}, f32[32,128]{1,0:T(8,128)S(1)}, u32[]{:S(2)}, u32[]{:S(2)}) collective-permute-start(f32[32,128]{1,0:T(8,128)S(1)} %get-tuple-element.52), channel_id=1, source_target_pairs={{0,1},{1,2},{2,3},{3,4},{4,5},{5,6},{6,7},{7,8},{8,9},{9,10},{10,1... | collective-permute-start | bytes 49160 | tf_op jit(solution)/shard_map/ppermute | solution.py:574
  78.7 5.3 %collective-permute-start.5 = (f32[32,128]{1,0:T(8,128)S(1)}, f32[32,128]{1,0:T(8,128)S(1)}, u32[]{:S(2)}, u32[]{:S(2)}) collective-permute-start(f32[32,128]{1,0:T(8,128)S(1)} %get-tuple-element.55), channel_id=1, source_target_pairs={{1,0},{2,1},{3,2},{4,3},{5,4},{6,5},{7,6},{8,7},{9,8},{10,9},{11,1... | collective-permute-start | bytes 49160 | tf_op jit(solution)/shard_map/ppermute | solution.py:574
  80.7 8.3 %collective-permute-start.4 = (f32[32,128]{1,0:T(8,128)S(1)}, f32[32,128]{1,0:T(8,128)S(1)}, u32[]{:S(2)}, u32[]{:S(2)}) collective-permute-start(f32[32,128]{1,0:T(8,128)S(1)} %get-tuple-element.55), channel_id=1, source_target_pairs={{0,1},{1,2},{2,3},{3,4},{4,5},{5,6},{6,7},{7,8},{8,9},{9,10},{10,1... | collective-permute-start | bytes 49160 | tf_op jit(solution)/shard_map/ppermute | solution.py:574
  89.5 6.2 %collective-permute-start.7 = (f32[32,128]{1,0:T(8,128)S(1)}, f32[32,128]{1,0:T(8,128)S(1)}, u32[]{:S(2)}, u32[]{:S(2)}) collective-permute-start(f32[32,128]{1,0:T(8,128)S(1)} %get-tuple-element.58), channel_id=1, source_target_pairs={{1,0},{2,1},{3,2},{4,3},{5,4},{6,5},{7,6},{8,7},{9,8},{10,9},{11,1... | collective-permute-start | bytes 49160 | tf_op jit(solution)/shard_map/ppermute | solution.py:574
  93.8 8.2 %collective-permute-start.6 = (f32[32,128]{1,0:T(8,128)S(1)}, f32[32,128]{1,0:T(8,128)S(1)}, u32[]{:S(2)}, u32[]{:S(2)}) collective-permute-start(f32[32,128]{1,0:T(8,128)S(1)} %get-tuple-element.58), channel_id=1, source_target_pairs={{0,1},{1,2},{2,3},{3,4},{4,5},{5,6},{6,7},{7,8},{8,9},{9,10},{10,1... | collective-permute-start | bytes 49160 | tf_op jit(solution)/shard_map/ppermute | solution.py:574
  102.5 6.2 %collective-permute-start.9 = (f32[32,128]{1,0:T(8,128)S(1)}, f32[32,128]{1,0:T(8,128)S(1)}, u32[]{:S(2)}, u32[]{:S(2)}) collective-permute-start(f32[32,128]{1,0:T(8,128)S(1)} %get-tuple-element.61), channel_id=1, source_target_pairs={{1,0},{2,1},{3,2},{4,3},{5,4},{6,5},{7,6},{8,7},{9,8},{10,9},{11,1... | collective-permute-start | bytes 49160 | tf_op jit(solution)/shard_map/ppermute | solution.py:574
  106.7 8.2 %collective-permute-start.8 = (f32[32,128]{1,0:T(8,128)S(1)}, f32[32,128]{1,0:T(8,128)S(1)}, u32[]{:S(2)}, u32[]{:S(2)}) collective-permute-start(f32[32,128]{1,0:T(8,128)S(1)} %get-tuple-element.61), channel_id=1, source_target_pairs={{0,1},{1,2},{2,3},{3,4},{4,5},{5,6},{6,7},{7,8},{8,9},{9,10},{10,1... | collective-permute-start | bytes 49160 | tf_op jit(solution)/shard_map/ppermute | solution.py:574
  115.5 6.2 %collective-permute-start.11 = (f32[32,128]{1,0:T(8,128)S(1)}, f32[32,128]{1,0:T(8,128)S(1)}, u32[]{:S(2)}, u32[]{:S(2)}) collective-permute-start(f32[32,128]{1,0:T(8,128)S(1)} %get-tuple-element.64), channel_id=1, source_target_pairs={{1,0},{2,1},{3,2},{4,3},{5,4},{6,5},{7,6},{8,7},{9,8},{10,9},{11,1... | collective-permute-start | bytes 49160 | tf_op jit(solution)/shard_map/ppermute | solution.py:574
  119.7 8.2 %collective-permute-start.10 = (f32[32,128]{1,0:T(8,128)S(1)}, f32[32,128]{1,0:T(8,128)S(1)}, u32[]{:S(2)}, u32[]{:S(2)}) collective-permute-start(f32[32,128]{1,0:T(8,128)S(1)} %get-tuple-element.64), channel_id=1, source_target_pairs={{0,1},{1,2},{2,3},{3,4},{4,5},{5,6},{6,7},{7,8},{8,9},{9,10},{10,1... | collective-permute-start | bytes 49160 | tf_op jit(solution)/shard_map/ppermute | solution.py:574
  128.4 6.2 %collective-permute-start.13 = (f32[32,128]{1,0:T(8,128)S(1)}, f32[32,128]{1,0:T(8,128)S(1)}, u32[]{:S(2)}, u32[]{:S(2)}) collective-permute-start(f32[32,128]{1,0:T(8,128)S(1)} %get-tuple-element.67), channel_id=1, source_target_pairs={{1,0},{2,1},{3,2},{4,3},{5,4},{6,5},{7,6},{8,7},{9,8},{10,9},{11,1... | collective-permute-start | bytes 49160 | tf_op jit(solution)/shard_map/ppermute | solution.py:574
  132.6 8.2 %collective-permute-start.12 = (f32[32,128]{1,0:T(8,128)S(1)}, f32[32,128]{1,0:T(8,128)S(1)}, u32[]{:S(2)}, u32[]{:S(2)}) collective-permute-start(f32[32,128]{1,0:T(8,128)S(1)} %get-tuple-element.67), channel_id=1, source_target_pairs={{0,1},{1,2},{2,3},{3,4},{4,5},{5,6},{6,7},{7,8},{8,9},{9,10},{10,1... | collective-permute-start | bytes 49160 | tf_op jit(solution)/shard_map/ppermute | solution.py:574
  141.4 6.2 %collective-permute-start.15 = (f32[32,128]{1,0:T(8,128)S(1)}, f32[32,128]{1,0:T(8,128)S(1)}, u32[]{:S(2)}, u32[]{:S(2)}) collective-permute-start(f32[32,128]{1,0:T(8,128)S(1)} %get-tuple-element.70), channel_id=1, source_target_pairs={{1,0},{2,1},{3,2},{4,3},{5,4},{6,5},{7,6},{8,7},{9,8},{10,9},{11,1... | collective-permute-start | bytes 49160 | tf_op jit(solution)/shard_map/ppermute | solution.py:574
  145.6 8.2 %collective-permute-start.14 = (f32[32,128]{1,0:T(8,128)S(1)}, f32[32,128]{1,0:T(8,128)S(1)}, u32[]{:S(2)}, u32[]{:S(2)}) collective-permute-start(f32[32,128]{1,0:T(8,128)S(1)} %get-tuple-element.70), channel_id=1, source_target_pairs={{0,1},{1,2},{2,3},{3,4},{4,5},{5,6},{6,7},{7,8},{8,9},{9,10},{10,1... | collective-permute-start | bytes 49160 | tf_op jit(solution)/shard_map/ppermute | solution.py:574
  153.8 31.6 %copy-start.2 = (f32[6,20,1024]{2,1,0:T(8,128)S(1)}, f32[6,20,1024]{2,1,0:T(8,128)}, u32[]{:S(2)}) copy-start(f32[6,20,1024]{2,1,0:T(8,128)} %fields_ref.3) | copy-start | bytes 1474564
  154.5 30.9 %copy-start.5 = (f32[3,4,1024]{2,1,0:T(4,128)S(1)}, f32[3,4,1024]{2,1,0:T(4,128)}, u32[]{:S(2)}) copy-start(f32[3,4,1024]{2,1,0:T(4,128)} %normals_ref.7) | copy-start | bytes 147460
  154.5 30.9 %copy-start.7 = (f32[9,1024]{1,0:T(8,128)S(1)}, f32[9,1024]{1,0:T(8,128)}, u32[]{:S(2)}) copy-start(f32[9,1024]{1,0:T(8,128)} %geometry_ref.5) | copy-start | bytes 110596
  154.5 30.9 %copy-start.9 = (f32[4,1024]{1,0:T(4,128)S(1)}, f32[4,1024]{1,0:T(4,128)}, u32[]{:S(2)}) copy-start(f32[4,1024]{1,0:T(4,128)} %scale_ref.7) | copy-start | bytes 49156
  154.5 30.9 %copy-start.11 = (s32[4,1024]{1,0:T(4,128)S(1)}, s32[4,1024]{1,0:T(4,128)}, u32[]{:S(2)}) copy-start(s32[4,1024]{1,0:T(4,128)} %nbr_ref.25) | copy-start | bytes 49156
  194.0 12.0 %collective-permute-start.17 = (f32[64,128]{1,0:T(8,128)S(1)}, f32[64,128]{1,0:T(8,128)S(1)}, u32[]{:S(2)}, u32[]{:S(2)}) collective-permute-start(f32[64,128]{1,0:T(8,128)S(1)} %get-tuple-element.74), channel_id=1, source_target_pairs={{1,0},{2,1},{3,2},{4,3},{5,4},{6,5},{7,6},{8,7},{9,8},{10,9},{11,1... | collective-permute-start | bytes 98312 | tf_op jit(solution)/shard_map/ppermute | solution.py:574
  195.9 10.1 %collective-permute-start.16 = (f32[64,128]{1,0:T(8,128)S(1)}, f32[64,128]{1,0:T(8,128)S(1)}, u32[]{:S(2)}, u32[]{:S(2)}) collective-permute-start(f32[64,128]{1,0:T(8,128)S(1)} %get-tuple-element.74), channel_id=1, source_target_pairs={{0,1},{1,2},{2,3},{3,4},{4,5},{5,6},{6,7},{7,8},{8,9},{9,10},{10,1... | collective-permute-start | bytes 98312 | tf_op jit(solution)/shard_map/ppermute | solution.py:574
  (2 other events, 1.4 us)

commit v2 on v1

--- a/solution.py
+++ b/solution.py
@@ -12,7 +12,8 @@
 COARSE_STEP = 0.2
 FINE_STEP = COARSE_STEP / SUBSTEPS
 LANES = 128
-VMEM_BYTES = 48 * 2**20
+VMEM_BYTES = 40 * 2**20
+PACK_VMEM_BYTES = 60 * 2**20
 RING = ("dom", "sub")
 highest = lax.Precision.HIGHEST
 
@@ -42,6 +43,25 @@
 
 
 RUNS = [runs_of(nodes) for nodes in face_table()]
+
+
+def seat(block, rows, columns):
+    chip, core = block // 2, block % 2
+    y, z = chip // columns, chip % columns
+    if y % 2:
+        z, core = columns - 1 - z, 1 - core
+    return (y * columns + z) * 2 + core
+
+
+def seats(count):
+    chips = count // 2
+    rows = max(r for r in range(1, chips + 1) if chips % r == 0 and r * r <= chips)
+    return np.array([seat(block, rows, chips // rows) for block in range(count)], np.int32)
+
+
+def slot_order(count, cap):
+    block_at = np.argsort(seats(count))
+    return (block_at[:, None] * cap + np.arange(cap)[None, :]).reshape(-1).astype(np.int32)
 
 
 def take(block, lane):
@@ -123,11 +143,36 @@
 
 
 def pack_kernel(
-    fields_ref, geometry_ref, normals_ref, scale_ref, nbr_ref, send_ref,
+    plain_send_hbm, order_hbm, fields_hbm, nbr_hbm, geometry_hbm, normals_hbm, scale_hbm,
     out_ref, ends_ref, home_ref,
-    flat_ref, nb_ref, pool_ref, feature_ref,
-):
+    plain_send_ref, order_ref, fields_ref, nbr_ref, geometry_ref, normals_ref, scale_ref,
+    send_ref, flat_ref, nb_ref, pool_ref, feature_ref,
+    *sems,
+):
+    pairs = [
+        (plain_send_hbm, plain_send_ref), (order_hbm, order_ref), (fields_hbm, fields_ref),
+        (nbr_hbm, nbr_ref), (geometry_hbm, geometry_ref), (normals_hbm, normals_ref),
+        (scale_hbm, scale_ref),
+    ]
+    copies = [pltpu.make_async_copy(a, b, sem) for (a, b), sem in zip(pairs, sems)]
+    for copy in copies:
+        copy.start()
+    copies[0].wait()
+    copies[1].wait()
     own = fields_ref.shape[2]
+    send_blocks = plain_send_ref.shape[0]
+    for sb in range(send_blocks):
+        order = rows8(order_ref[sb : sb + 1, :])
+        row = jnp.zeros((8, LANES), jnp.int32)
+        for b in range(send_blocks):
+            block = take(rows8(plain_send_ref[b : b + 1, :]), order & (LANES - 1))
+            row = jnp.where((order >> 7) == b, block, row)
+        send_ref[sb : sb + 1, :] = row[0:1, :]
+    homes = inverse_of(lambda b: send_ref[b : b + 1, :], send_blocks, own // LANES, -1)
+    for b in range(own // LANES):
+        home_ref[b : b + 1, :] = homes[b]
+    for copy in copies[2:]:
+        copy.wait()
     for c in range(6):
         flat_ref[c * 20 : c * 20 + 20, :] = fields_ref[c]
     flat_ref[120:129, :] = geometry_ref[...]
@@ -191,11 +236,8 @@
                 feature_ref[at : at + length, lanes_at(sb)] = value[:length]
         return carry
 
-    lax.fori_loop(0, send_ref.shape[0], slots, 0)
+    lax.fori_loop(0, send_blocks, slots, 0)
     out_ref[...] = jnp.transpose(feature_ref[...])
-    homes = inverse_of(lambda b: send_ref[b : b + 1, :], send_ref.shape[0], blocks, -1)
-    for b in range(blocks):
-        home_ref[b : b + 1, :] = homes[b]
 
 
 def fine_pool(state_ref, pool_ref):
@@ -217,11 +259,12 @@
 
 
 def unpack_kernel(
-    received_ref, slots_ref, nbr_ref, export_ref, ends_ref,
+    width, received_ref, table_ref,
     efield_ref, hfield_ref, normal_ref, geometry_ref, held_ref, pool_ref, halo_ref, lane_ref,
     back_ref,
-    feature_ref, picked_ref, small_ref,
-):
+    feature_ref, picked_ref,
+):
+    nbr_ref, slots_ref = table_ref.at[0:4], table_ref.at[4:5]
     slot_blocks = received_ref.shape[0] // LANES
     feature_ref[...] = jnp.transpose(received_ref[...])
     slot = rows8(slots_ref[...])
@@ -240,24 +283,20 @@
     spread_normals(
         lambda c, f: picked_ref[129 + 4 * c + f : 130 + 4 * c + f, :], normal_ref
     )
-    frozen_code = 4 * LANES + 4 * 2 * export_ref.shape[1]
+    frozen_code = 4 * LANES + 4 * 2 * width
     for f in range(4):
         frozen = jnp.broadcast_to(nbr_ref[f : f + 1, :] == frozen_code, (30, LANES))
         for eh in range(2):
             at = 144 + (eh * 4 + f) * 30
             held_ref[eh, f, 0:30, :] = jnp.where(frozen, picked_ref[at : at + 30, :], 0.0)
             held_ref[eh, f, 30:32, :] = jnp.zeros((2, LANES), jnp.float32)
-    width = export_ref.shape[1]
-    small_ref[...] = jnp.zeros_like(small_ref)
-    small_ref[0:2, 0:width] = export_ref[...]
     place = lax.broadcasted_iota(jnp.int32, (8, LANES), 1)
-    both = take(small_ref[...], (place >> 2) & (width - 1))
-    lane_ref[...] = jnp.where(place < LANES // 2, rows8(both[1:2, :]), rows8(both[0:1, :]))
+    both = take(table_ref[...], (place >> 2) & (width - 1))
+    lane_ref[...] = jnp.where(place < LANES // 2, rows8(both[6:7, :]), rows8(both[5:6, :]))
     fine_pool(efield_ref, pool_ref)
     groups = exported(pool_ref, lane_ref[...])
     for g in range(4):
         halo_ref[g * 8 : g * 8 + 8, :] = groups[g]
-    halo_ref[32:96, :] = ends_ref[...]
     backs = inverse_of(lambda b: slots_ref[...], 1, slot_blocks, 0)
     for b in range(slot_blocks):
         back_ref[b : b + 1, :] = backs[b]
@@ -467,7 +506,7 @@
     for c in range(6):
         merged_ref[c] = flat_ref[c * 20 : c * 20 + 20, :]
     coarse_pool(merged_ref, 0, pool_ref)
-    halo = halo_rows(below_ref[32:96, :], above_ref[32:96, :])
+    halo = halo_rows(below_ref[...], above_ref[...])
 
     def store(f, place, length, value):
         pool_ref[f, place : place + length, own : own + LANES] = value
@@ -555,23 +594,35 @@
         out_ref[3 + c] = merged_ref[3 + c]
 
 
-def call(kernel, outs, scratch, *args):
+def call(kernel, outs, scratch, *args, hbm=(), vmem=VMEM_BYTES):
     whole = pl.BlockSpec(memory_space=pltpu.VMEM)
+    specs = [
+        pl.BlockSpec(memory_space=pltpu.HBM) if number in hbm else whole for number in range(len(args))
+    ]
     return pl.pallas_call(
         kernel,
         out_shape=[jax.ShapeDtypeStruct(shape, dtype) for shape, dtype in outs],
-        in_specs=[whole] * len(args),
+        in_specs=specs,
         out_specs=[whole] * len(outs),
-        scratch_shapes=[pltpu.VMEM(shape, dtype) for shape, dtype in scratch],
-        compiler_params=pltpu.CompilerParams(vmem_limit_bytes=VMEM_BYTES),
+        scratch_shapes=[pltpu.VMEM(shape, dtype) for shape, dtype in scratch]
+        + [pltpu.SemaphoreType.DMA(())] * len(hbm),
+        compiler_params=pltpu.CompilerParams(vmem_limit_bytes=vmem),
     )(*args)
 
 
-def exchange(block):
+def device_of(block):
+    sub = lax.axis_size("sub")
+    return int(seats(lax.axis_size("dom"))[block // sub]) * sub + block % sub
+
+
+def shifted(block, by, place=int):
     count = lax.axis_size(RING)
-    up = [(i, (i + 1) % count) for i in range(count)]
-    down = [(target, source) for source, target in up]
-    return lax.ppermute(block, RING, up), lax.ppermute(block, RING, down)
+    pairs = [(place(i), place((i + by) % count)) for i in range(count)]
+    return lax.ppermute(block, RING, pairs)
+
+
+def exchange(block, place=int):
+    return shifted(block, 1, place), shifted(block, -1, place)
 
 
 def swap_slots(rows, width):
@@ -590,45 +641,69 @@
     own = fields.shape[2]
     slots = send_rows.shape[0]
     fine = fine_slots.shape[0]
+    width = export_rows.shape[1]
+    table = jnp.concatenate(
+        [
+            fine_nbr,
+            fine_slots.reshape(1, fine),
+            jnp.pad(export_rows, ((0, 0), (0, fine - width))),
+            jnp.zeros((1, fine), i32),
+        ]
+    )
+    count = lax.axis_size(RING)
+    table = lax.ppermute(table, RING, [(i, device_of(i)) for i in range(count)])
     send = send_rows.reshape(slots // LANES, LANES)
+    order = slot_order(lax.axis_size("dom"), slots // lax.axis_size("dom"))
     packed, ends, home = call(
         pack_kernel,
         [((slots, 384), f32), ((64, LANES), f32), ((own // LANES, LANES), i32)],
-        [((144, own), f32), ((8, own), i32), ((2, 4, 32, own), f32), ((384, slots), f32)],
-        fields, geometry, normals, face_scale, face_nbr, send,
+        [
+            (send.shape, i32), (send.shape, i32), (fields.shape, f32), (face_nbr.shape, i32),
+            (geometry.shape, f32), (normals.shape, f32), (face_scale.shape, f32),
+            (send.shape, i32), ((144, own), f32), ((8, own), i32), ((2, 4, 32, own), f32),
+            ((384, slots), f32),
+        ],
+        send, jnp.asarray(order.reshape(send.shape)), fields, face_nbr, geometry, normals,
+        face_scale,
+        hbm=range(7),
+        vmem=PACK_VMEM_BYTES,
     )
     received = swap_slots(packed, 384)
     state, traces = ((20, 3 * fine), f32), ((4, 32, fine), f32)
     efield, hfield, normal, factors, held, pool, halo, lane, back = call(
-        unpack_kernel,
+        functools.partial(unpack_kernel, width),
         [
             state, state, ((3, 40, fine), f32), ((16, fine), f32), ((2, 4, 32, fine), f32),
-            traces, ((96, fine), f32), ((8, fine), i32), ((slots // LANES, LANES), i32),
+            traces, ((32, fine), f32), ((8, fine), i32), ((slots // LANES, LANES), i32),
         ],
-        [((384, slots), f32), ((384, fine), f32), ((8, LANES), i32)],
-        received, fine_slots.reshape(1, fine), fine_nbr, export_rows, ends,
+        [((384, slots), f32), ((384, fine), f32)],
+        received, table,
     )
     scratch = [((72, 20), f32), traces, ((3, 40, fine), f32), ((40, 3 * fine), f32)]
-    first = None
+    end_parts = []
     for half in range(2 * SUBSTEPS - 1):
-        below, above = exchange(halo)
-        first = first or (below, above)
+        below, above = exchange(halo, device_of)
+        if half in (0, 1):
+            halo, ends = lax.optimization_barrier((halo, ends))
+            part = shifted(ends, 1 - 2 * half)
+            below, above, part = lax.optimization_barrier((below, above, part))
+            end_parts.append(part)
         magnetic = half % 2 == 0
         source, target = (efield, hfield) if magnetic else (hfield, efield)
         new, pool, halo = call(
             functools.partial(fine_kernel, magnetic),
             [state, traces, ((32, fine), f32)],
             scratch,
-            source, target, pool, below, above, held, normal, factors, fine_nbr, lane,
+            source, target, pool, below, above, held, normal, factors, table, lane,
             derivatives, lift_matrix,
         )
         efield, hfield = (efield, new) if magnetic else (new, hfield)
-    below, above = exchange(halo)
+    below, above = exchange(halo, device_of)
     (outgoing,) = call(
         last_fine_kernel,
         [((slots, LANES), f32)],
         [((128, fine), f32), ((128, slots), f32)] + scratch,
-        hfield, efield, pool, below, above, held, normal, factors, fine_nbr, back, derivatives,
+        hfield, efield, pool, below, above, held, normal, factors, table, back, derivatives,
         lift_matrix,
     )
     returned = swap_slots(outgoing, LANES)
@@ -640,7 +715,7 @@
         coarse_magnetic_kernel,
         [((6, 20, own), f32), ((64, LANES), f32)],
         [((120, own), f32), ((128, slots), f32), ((4, 32, own + LANES), f32)] + work,
-        returned, home, fields, first[0], first[1], geometry, normals, face_scale, face_nbr,
+        returned, home, fields, end_parts[0], end_parts[1], geometry, normals, face_scale, face_nbr,
         derivatives, lift_matrix,
     )
     below, above = exchange(ends)

time: 208 us -> 203 us (0.976)
  blocking collectives: 74.2 us -> 35.7 us
  starting transfers between devices: 54.4 us -> 92.3 us
  waiting for transfers between devices: 44 us -> 39.3 us
  local copies, waits for them, and re-layouts: 6.03 us -> 3.4 us
    all_to_all x2 -> x1, blocking collectives: 74.2 us -> 35.7 us  [swap_slots(): lax.all_to_all(chunks, 'dom', split_axis=0, concat_axis=0, tiled=True)]
    ppermute x18 -> x21, waiting for transfers between devices: 44 us -> 15.7 us  [the longest x20 15.7 us: shifted(): return lax.ppermute(block, RING, pairs)]
    all_to_all x0 -> x1, waiting for transfers between devices: none -> 23.6 us  [swap_slots(): lax.all_to_all(chunks, 'dom', split_axis=0, concat_axis=0, tiled=True)]
    ppermute x18 -> x21, starting transfers between devices: 54.4 us -> 73.9 us  [the longest x20 73.3 us: shifted(): return lax.ppermute(block, RING, pairs)]
    all_to_all x0 -> x1, starting transfers between devices: none -> 18.4 us  [swap_slots(): lax.all_to_all(chunks, 'dom', split_axis=0, concat_axis=0, tiled=True)]
    unnamed x32 -> x24, local copies, waits for them, and re-layouts: 5.53 us -> 0.81 us
  transfers between devices with their start and end apart: 18 -> 22, of which waited for: 8 -> 9; matrix products, arithmetic and copies ran while one was open for 0% -> 0% of each run, Pallas kernels for 3% -> 3%
where the time goes in v2:
time: 203 us; the launch traced here: 202 us
  starting transfers between devices  92.3 us (45%)
  waiting for transfers between devices  39.3 us (19%)
  blocking collectives  35.7 us (18%)
  Pallas kernels  30.2 us (15%)
  local copies, waits for them, and re-layouts  3.4 us (2%)
    ppermute x20, starting transfers between devices, shifted(): return lax.ppermute(block, RING, pairs)  73.3 us
    all_to_all x1, blocking collectives, swap_slots(): lax.all_to_all(chunks, 'dom', split_axis=0, concat_axis=0, tiled=True)  35.7 us
    pallas_call x13, Pallas kernels, call(): pl.pallas_call(kernel, out_shape=[jax.ShapeDtypeStruct(shape, dtype) for...  30.2 us
    all_to_all x1, waiting for transfers between devices, swap_slots(): lax.all_to_all(chunks, 'dom', split_axis=0, concat_axis=0, tiled=True)  23.6 us
    all_to_all x1, starting transfers between devices, swap_slots(): lax.all_to_all(chunks, 'dom', split_axis=0, concat_axis=0, tiled=True)  18.4 us
    ppermute x20, waiting for transfers between devices, shifted(): return lax.ppermute(block, RING, pairs)  15.7 us
  transfers between devices with their start and end apart: 22, of which 9 were waited for; matrix products, arithmetic and copies ran while one was open for 0% of the time, Pallas kernels for 3%

profile of v2, /device:TPU:1, one launch (start us, length us, event | category | flops | bytes accessed | tf_op | source)
XLA Modules:
  0.0 201.6 jit_solution(17918580529817584807)
XLA Ops:
  0.0 8.5 %shard_map.118 = (f32[512,384]{1,0:T(8,128)}, f32[64,128]{1,0:T(8,128)}, s32[8,128]{1,0:T(8,128)}) custom-call(s32[4,128]{1,0:T(4,128)} %bitcast.7, s32[4,128]{1,0:T(4,128)} %constant.1.clone.order_hbm, f32[6,20,1024]{2,1,0:T(8,128)} %fields_ref.1, s32[4,1024]{1,0:T(4,128)} %nbr_ref.5, f32[9,1024]{1,0:T(8,128)} %geometry_ref.3, f32[3,4,1024]{2,1,0:T(4,128)} %normals_ref.5, ...), custom_call_target="tpu_custom_call" | custom-call | tf_op jit(solution)/shard_map/pallas_call | solution.py:602
  8.5 2.2 %reshape.19 = f32[128,4,384]{2,1,0:T(4,128)} reshape(f32[512,384]{1,0:T(8,128)} %get-tuple-element.48) | data formatting | bytes 1572864 | tf_op jit(solution)/shard_map/reshape | solution.py:630
  10.7 18.4 %all-to-all-start = ((f32[128,4,384]{2,1,0:T(4,128)}), f32[128,4,384]{2,1,0:T(4,128)S(1)}, u32[]{:S(2)}, u32[]{:S(2)}) async-start(f32[128,4,384]{2,1,0:T(4,128)} %reshape.19), calls=%async_computation | async-start | bytes 1572864 | tf_op jit(solution)/shard_map/all_to_all | solution.py:631
  30.7 23.6 %all-to-all-done = f32[128,4,384]{2,1,0:T(4,128)S(1)} async-done(((f32[128,4,384]{2,1,0:T(4,128)}), f32[128,4,384]{2,1,0:T(4,128)S(1)}, u32[]{:S(2)}, u32[]{:S(2)}) %all-to-all-start) | async-done | bytes 786464 | tf_op jit(solution)/shard_map/all_to_all | solution.py:631
  55.3 3.1 %collective-permute-start.3 = (f32[64,128]{1,0:T(8,128)S(1)}, f32[64,128]{1,0:T(8,128)S(1)}, u32[]{:S(2)}, u32[]{:S(2)}) collective-permute-start(f32[64,128]{1,0:T(8,128)S(1)} %copy-done.11), channel_id=1, source_target_pairs={{0,1},{1,2},{2,3},{3,4},{4,5},{5,6},{6,7},{7,8},{8,9},{9,10},{10,1... | collective-permute-start | bytes 98312 | tf_op jit(solution)/shard_map/ppermute | solution.py:621
  58.4 3.1 %collective-permute-start.1 = (f32[32,128]{1,0:T(8,128)S(1)}, f32[32,128]{1,0:T(8,128)S(1)}, u32[]{:S(2)}, u32[]{:S(2)}) collective-permute-start(f32[32,128]{1,0:T(8,128)S(1)} %get-tuple-element.52), channel_id=1, source_target_pairs={{0,1},{1,2},{2,3},{3,4},{4,5},{5,6},{6,7},{7,8},{8,9},{9,10},{10,1... | collective-permute-start | bytes 49160 | tf_op jit(solution)/shard_map/ppermute | solution.py:621
  61.6 3.7 %collective-permute-start.2 = (f32[32,128]{1,0:T(8,128)S(1)}, f32[32,128]{1,0:T(8,128)S(1)}, u32[]{:S(2)}, u32[]{:S(2)}) collective-permute-start(f32[32,128]{1,0:T(8,128)S(1)} %get-tuple-element.52), channel_id=1, source_target_pairs={{0,451},{1,0},{2,1},{3,2},{4,3},{5,4},{6,5},{7,6},{8,7},{9,8},{10,... | collective-permute-start | bytes 49160 | tf_op jit(solution)/shard_map/ppermute | solution.py:621
  66.9 5.1 %collective-permute-start.6 = (f32[64,128]{1,0:T(8,128)S(1)}, f32[64,128]{1,0:T(8,128)S(1)}, u32[]{:S(2)}, u32[]{:S(2)}) collective-permute-start(f32[64,128]{1,0:T(8,128)S(1)} %copy-done.11), channel_id=1, source_target_pairs={{0,511},{1,0},{2,1},{3,2},{4,3},{5,4},{6,5},{7,6},{8,7},{9,8},{10,... | collective-permute-start | bytes 98312 | tf_op jit(solution)/shard_map/ppermute | solution.py:621
  72.1 1.9 collective-permute-start.4
  74.0 4.9 %collective-permute-start.5 = (f32[32,128]{1,0:T(8,128)S(1)}, f32[32,128]{1,0:T(8,128)S(1)}, u32[]{:S(2)}, u32[]{:S(2)}) collective-permute-start(f32[32,128]{1,0:T(8,128)S(1)} %get-tuple-element.63), channel_id=1, source_target_pairs={{0,451},{1,0},{2,1},{3,2},{4,3},{5,4},{6,5},{7,6},{8,7},{9,8},{10,... | collective-permute-start | bytes 49160 | tf_op jit(solution)/shard_map/ppermute | solution.py:621
  80.3 2.4 %collective-permute-start.7 = (f32[32,128]{1,0:T(8,128)S(1)}, f32[32,128]{1,0:T(8,128)S(1)}, u32[]{:S(2)}, u32[]{:S(2)}) collective-permute-start(f32[32,128]{1,0:T(8,128)S(1)} %get-tuple-element.69), channel_id=1, source_target_pairs={{0,1},{1,2},{2,3},{3,4},{4,5},{5,6},{6,7},{7,8},{8,9},{9,10},{10,1... | collective-permute-start | bytes 49160 | tf_op jit(solution)/shard_map/ppermute | solution.py:621
  82.7 4.9 %collective-permute-start.8 = (f32[32,128]{1,0:T(8,128)S(1)}, f32[32,128]{1,0:T(8,128)S(1)}, u32[]{:S(2)}, u32[]{:S(2)}) collective-permute-start(f32[32,128]{1,0:T(8,128)S(1)} %get-tuple-element.69), channel_id=1, source_target_pairs={{0,451},{1,0},{2,1},{3,2},{4,3},{5,4},{6,5},{7,6},{8,7},{9,8},{10,... | collective-permute-start | bytes 49160 | tf_op jit(solution)/shard_map/ppermute | solution.py:621
  87.6 1.9 collective-permute-done.8.high_ref
  90.1 6.0 %collective-permute-start.9 = (f32[32,128]{1,0:T(8,128)S(1)}, f32[32,128]{1,0:T(8,128)S(1)}, u32[]{:S(2)}, u32[]{:S(2)}) collective-permute-start(f32[32,128]{1,0:T(8,128)S(1)} %get-tuple-element.72), channel_id=1, source_target_pairs={{0,1},{1,2},{2,3},{3,4},{4,5},{5,6},{6,7},{7,8},{8,9},{9,10},{10,1... | collective-permute-start | bytes 49160 | tf_op jit(solution)/shard_map/ppermute | solution.py:621
  96.1 1.9 collective-permute-start.10
  98.1 2.5 %collective-permute-done.10.high_ref = f32[32,128]{1,0:T(8,128)S(1)} collective-permute-done((f32[32,128]{1,0:T(8,128)S(1)}, f32[32,128]{1,0:T(8,128)S(1)}, u32[]{:S(2)}, u32[]{:S(2)}) %collective-permute-start.10) | collective-permute-done | bytes 16416 | tf_op jit(solution)/shard_map/ppermute | solution.py:621
  101.2 4.6 %collective-permute-start.11 = (f32[32,128]{1,0:T(8,128)S(1)}, f32[32,128]{1,0:T(8,128)S(1)}, u32[]{:S(2)}, u32[]{:S(2)}) collective-permute-start(f32[32,128]{1,0:T(8,128)S(1)} %get-tuple-element.75), channel_id=1, source_target_pairs={{0,1},{1,2},{2,3},{3,4},{4,5},{5,6},{6,7},{7,8},{8,9},{9,10},{10,1... | collective-permute-start | bytes 49160 | tf_op jit(solution)/shard_map/ppermute | solution.py:621
  105.8 2.2 %collective-permute-start.12 = (f32[32,128]{1,0:T(8,128)S(1)}, f32[32,128]{1,0:T(8,128)S(1)}, u32[]{:S(2)}, u32[]{:S(2)}) collective-permute-start(f32[32,128]{1,0:T(8,128)S(1)} %get-tuple-element.75), channel_id=1, source_target_pairs={{0,451},{1,0},{2,1},{3,2},{4,3},{5,4},{6,5},{7,6},{8,7},{9,8},{10,... | collective-permute-start | bytes 49160 | tf_op jit(solution)/shard_map/ppermute | solution.py:621
  108.0 2.3 %collective-permute-done.12.high_ref = f32[32,128]{1,0:T(8,128)S(1)} collective-permute-done((f32[32,128]{1,0:T(8,128)S(1)}, f32[32,128]{1,0:T(8,128)S(1)}, u32[]{:S(2)}, u32[]{:S(2)}) %collective-permute-start.12) | collective-permute-done | bytes 16416 | tf_op jit(solution)/shard_map/ppermute | solution.py:621
  110.8 4.6 %collective-permute-start.13 = (f32[32,128]{1,0:T(8,128)S(1)}, f32[32,128]{1,0:T(8,128)S(1)}, u32[]{:S(2)}, u32[]{:S(2)}) collective-permute-start(f32[32,128]{1,0:T(8,128)S(1)} %get-tuple-element.78), channel_id=1, source_target_pairs={{0,1},{1,2},{2,3},{3,4},{4,5},{5,6},{6,7},{7,8},{8,9},{9,10},{10,1... | collective-permute-start | bytes 49160 | tf_op jit(solution)/shard_map/ppermute | solution.py:621
  115.5 2.2 %collective-permute-start.14 = (f32[32,128]{1,0:T(8,128)S(1)}, f32[32,128]{1,0:T(8,128)S(1)}, u32[]{:S(2)}, u32[]{:S(2)}) collective-permute-start(f32[32,128]{1,0:T(8,128)S(1)} %get-tuple-element.78), channel_id=1, source_target_pairs={{0,451},{1,0},{2,1},{3,2},{4,3},{5,4},{6,5},{7,6},{8,7},{9,8},{10,... | collective-permute-start | bytes 49160 | tf_op jit(solution)/shard_map/ppermute | solution.py:621
  117.6 2.3 %collective-permute-done.14.high_ref = f32[32,128]{1,0:T(8,128)S(1)} collective-permute-done((f32[32,128]{1,0:T(8,128)S(1)}, f32[32,128]{1,0:T(8,128)S(1)}, u32[]{:S(2)}, u32[]{:S(2)}) %collective-permute-start.14) | collective-permute-done | bytes 16416 | tf_op jit(solution)/shard_map/ppermute | solution.py:621
  120.5 4.6 %collective-permute-start.15 = (f32[32,128]{1,0:T(8,128)S(1)}, f32[32,128]{1,0:T(8,128)S(1)}, u32[]{:S(2)}, u32[]{:S(2)}) collective-permute-start(f32[32,128]{1,0:T(8,128)S(1)} %get-tuple-element.81), channel_id=1, source_target_pairs={{0,1},{1,2},{2,3},{3,4},{4,5},{5,6},{6,7},{7,8},{8,9},{9,10},{10,1... | collective-permute-start | bytes 49160 | tf_op jit(solution)/shard_map/ppermute | solution.py:621
  125.1 2.2 %collective-permute-start.16 = (f32[32,128]{1,0:T(8,128)S(1)}, f32[32,128]{1,0:T(8,128)S(1)}, u32[]{:S(2)}, u32[]{:S(2)}) collective-permute-start(f32[32,128]{1,0:T(8,128)S(1)} %get-tuple-element.81), channel_id=1, source_target_pairs={{0,451},{1,0},{2,1},{3,2},{4,3},{5,4},{6,5},{7,6},{8,7},{9,8},{10,... | collective-permute-start | bytes 49160 | tf_op jit(solution)/shard_map/ppermute | solution.py:621
  127.3 2.6 %collective-permute-done.16.high_ref = f32[32,128]{1,0:T(8,128)S(1)} collective-permute-done((f32[32,128]{1,0:T(8,128)S(1)}, f32[32,128]{1,0:T(8,128)S(1)}, u32[]{:S(2)}, u32[]{:S(2)}) %collective-permute-start.16) | collective-permute-done | bytes 16416 | tf_op jit(solution)/shard_map/ppermute | solution.py:621
  130.5 4.3 %collective-permute-start.17 = (f32[32,128]{1,0:T(8,128)S(1)}, f32[32,128]{1,0:T(8,128)S(1)}, u32[]{:S(2)}, u32[]{:S(2)}) collective-permute-start(f32[32,128]{1,0:T(8,128)S(1)} %get-tuple-element.84), channel_id=1, source_target_pairs={{0,1},{1,2},{2,3},{3,4},{4,5},{5,6},{6,7},{7,8},{8,9},{9,10},{10,1... | collective-permute-start | bytes 49160 | tf_op jit(solution)/shard_map/ppermute | solution.py:621
  134.8 2.4 %collective-permute-start.18 = (f32[32,128]{1,0:T(8,128)S(1)}, f32[32,128]{1,0:T(8,128)S(1)}, u32[]{:S(2)}, u32[]{:S(2)}) collective-permute-start(f32[32,128]{1,0:T(8,128)S(1)} %get-tuple-element.84), channel_id=1, source_target_pairs={{0,451},{1,0},{2,1},{3,2},{4,3},{5,4},{6,5},{7,6},{8,7},{9,8},{10,... | collective-permute-start | bytes 49160 | tf_op jit(solution)/shard_map/ppermute | solution.py:621
  137.3 2.0 %collective-permute-done.18.high_ref = f32[32,128]{1,0:T(8,128)S(1)} collective-permute-done((f32[32,128]{1,0:T(8,128)S(1)}, f32[32,128]{1,0:T(8,128)S(1)}, u32[]{:S(2)}, u32[]{:S(2)}) %collective-permute-start.18) | collective-permute-done | bytes 16416 | tf_op jit(solution)/shard_map/ppermute | solution.py:621
  140.0 35.7 %all_to_all.10 = f32[128,4,128]{2,1,0:T(4,128)S(1)} all-to-all(f32[128,4,128]{2,1,0:T(4,128)S(1)} %bitcast.6), channel_id=1, replica_groups=mesh['dom'=128,'sub'=4] {'dom'}, dimensions={0} | all-to-all | bytes 524288 | tf_op jit(solution)/shard_map/all_to_all | solution.py:631
  175.8 8.5 %shard_map.128 = (f32[6,20,1024]{2,1,0:T(8,128)S(1)}, f32[64,128]{1,0:T(8,128)S(1)}) custom-call(f32[512,128]{1,0:T(8,128)S(1)} %bitcast.5, s32[8,128]{1,0:T(8,128)S(1)} %copy-done.7, f32[6,20,1024]{2,1,0:T(8,128)S(1)} %copy-done.1, f32[64,128]{1,0:T(8,128)S(1)} %collective-permute-done.3.below_ref, f32[64,128]{1,0:T(8,128)S(1)} %collective-permute-done.6.above_ref, ...), custom_call_target="tpu_custom_call" | custom-call | tf_op jit(solution)/shard_map/pallas_call | solution.py:602
  186.2 7.2 %collective-permute-start.20 = (f32[64,128]{1,0:T(8,128)S(1)}, f32[64,128]{1,0:T(8,128)S(1)}, u32[]{:S(2)}, u32[]{:S(2)}) collective-permute-start(f32[64,128]{1,0:T(8,128)S(1)} %get-tuple-element.90), channel_id=1, source_target_pairs={{0,511},{1,0},{2,1},{3,2},{4,3},{5,4},{6,5},{7,6},{8,7},{9,8},{10,... | collective-permute-start | bytes 98312 | tf_op jit(solution)/shard_map/ppermute | solution.py:621
  193.4 6.7 %shard_map.129.electric_ref = f32[3,20,1024]{2,1,0:T(8,128)S(1)} custom-call(f32[6,20,1024]{2,1,0:T(8,128)S(1)} %get-tuple-element.89.merged_ref, f32[9,1024]{1,0:T(8,128)S(1)} %copy-done.4, f32[3,4,1024]{2,1,0:T(4,128)S(1)} %copy-done.3, f32[4,1024]{1,0:T(4,128)S(1)} %copy-done.6, s32[4,1024]{1,0:T(4,128)S(1)} %copy-done.5, f32[3,20,20]{2,1,0:T(8,128)S(1)} %copy-done, ...), custom_call_target="tpu_custom_call" | custom-call | tf_op jit(solution)/shard_map/pallas_call | solution.py:602
  (54 shorter events, 12.3 us)
Async XLA Ops:
  10.7 43.6 %all-to-all-start = ((f32[128,4,384]{2,1,0:T(4,128)}), f32[128,4,384]{2,1,0:T(4,128)S(1)}, u32[]{:S(2)}, u32[]{:S(2)}) async-start(f32[128,4,384]{2,1,0:T(4,128)} %reshape.19), calls=%async_computation | async-start | bytes 1572864 | tf_op jit(solution)/shard_map/all_to_all | solution.py:631
  29.2 0.7 copy-start.8
  30.0 24.6 %collective-permute-start = (s32[8,128]{1,0:T(8,128)S(1)}, s32[8,128]{1,0:T(8,128)S(1)}, u32[]{:S(2)}, u32[]{:S(2)}) collective-permute-start(s32[8,128]{1,0:T(8,128)S(1)} %fusion), channel_id=1, source_target_pairs={{0,0},{1,1},{2,2},{3,3},{4,4},{5,5},{6,6},{7,7},{8,8},{9,9},{10,10... | collective-permute-start | bytes 12296 | tf_op jit(solution)/shard_map/ppermute | solution.py:654
  54.6 0.8 copy-start.11
  54.6 11.8 %copy-start = (f32[3,20,20]{2,1,0:T(8,128)S(1)}, f32[3,20,20]{2,1,0:T(8,128)}, u32[]{:S(2)}) copy-start(f32[3,20,20]{2,1,0:T(8,128)} %derivatives_ref.19) | copy-start | bytes 14404
  55.2 11.1 %copy-start.2 = (f32[20,40]{1,0:T(8,128)S(1)}, f32[20,40]{1,0:T(8,128)}, u32[]{:S(2)}) copy-start(f32[20,40]{1,0:T(8,128)} %lift_ref.21) | copy-start | bytes 9604
  55.3 11.0 %collective-permute-start.3 = (f32[64,128]{1,0:T(8,128)S(1)}, f32[64,128]{1,0:T(8,128)S(1)}, u32[]{:S(2)}, u32[]{:S(2)}) collective-permute-start(f32[64,128]{1,0:T(8,128)S(1)} %copy-done.11), channel_id=1, source_target_pairs={{0,1},{1,2},{2,3},{3,4},{4,5},{5,6},{6,7},{7,8},{8,9},{9,10},{10,1... | collective-permute-start | bytes 98312 | tf_op jit(solution)/shard_map/ppermute | solution.py:621
  58.4 6.8 %collective-permute-start.1 = (f32[32,128]{1,0:T(8,128)S(1)}, f32[32,128]{1,0:T(8,128)S(1)}, u32[]{:S(2)}, u32[]{:S(2)}) collective-permute-start(f32[32,128]{1,0:T(8,128)S(1)} %get-tuple-element.52), channel_id=1, source_target_pairs={{0,1},{1,2},{2,3},{3,4},{4,5},{5,6},{6,7},{7,8},{8,9},{9,10},{10,1... | collective-permute-start | bytes 49160 | tf_op jit(solution)/shard_map/ppermute | solution.py:621
  61.6 4.8 %collective-permute-start.2 = (f32[32,128]{1,0:T(8,128)S(1)}, f32[32,128]{1,0:T(8,128)S(1)}, u32[]{:S(2)}, u32[]{:S(2)}) collective-permute-start(f32[32,128]{1,0:T(8,128)S(1)} %get-tuple-element.52), channel_id=1, source_target_pairs={{0,451},{1,0},{2,1},{3,2},{4,3},{5,4},{6,5},{7,6},{8,7},{9,8},{10,... | collective-permute-start | bytes 49160 | tf_op jit(solution)/shard_map/ppermute | solution.py:621
  66.9 12.8 %collective-permute-start.6 = (f32[64,128]{1,0:T(8,128)S(1)}, f32[64,128]{1,0:T(8,128)S(1)}, u32[]{:S(2)}, u32[]{:S(2)}) collective-permute-start(f32[64,128]{1,0:T(8,128)S(1)} %copy-done.11), channel_id=1, source_target_pairs={{0,511},{1,0},{2,1},{3,2},{4,3},{5,4},{6,5},{7,6},{8,7},{9,8},{10,... | collective-permute-start | bytes 98312 | tf_op jit(solution)/shard_map/ppermute | solution.py:621
  72.1 6.8 %collective-permute-start.4 = (f32[32,128]{1,0:T(8,128)S(1)}, f32[32,128]{1,0:T(8,128)S(1)}, u32[]{:S(2)}, u32[]{:S(2)}) collective-permute-start(f32[32,128]{1,0:T(8,128)S(1)} %get-tuple-element.63), channel_id=1, source_target_pairs={{0,1},{1,2},{2,3},{3,4},{4,5},{5,6},{6,7},{7,8},{8,9},{9,10},{10,1... | collective-permute-start | bytes 49160 | tf_op jit(solution)/shard_map/ppermute | solution.py:621
  74.0 5.7 %collective-permute-start.5 = (f32[32,128]{1,0:T(8,128)S(1)}, f32[32,128]{1,0:T(8,128)S(1)}, u32[]{:S(2)}, u32[]{:S(2)}) collective-permute-start(f32[32,128]{1,0:T(8,128)S(1)} %get-tuple-element.63), channel_id=1, source_target_pairs={{0,451},{1,0},{2,1},{3,2},{4,3},{5,4},{6,5},{7,6},{8,7},{9,8},{10,... | collective-permute-start | bytes 49160 | tf_op jit(solution)/shard_map/ppermute | solution.py:621
  80.3 7.3 %collective-permute-start.7 = (f32[32,128]{1,0:T(8,128)S(1)}, f32[32,128]{1,0:T(8,128)S(1)}, u32[]{:S(2)}, u32[]{:S(2)}) collective-permute-start(f32[32,128]{1,0:T(8,128)S(1)} %get-tuple-element.69), channel_id=1, source_target_pairs={{0,1},{1,2},{2,3},{3,4},{4,5},{5,6},{6,7},{7,8},{8,9},{9,10},{10,1... | collective-permute-start | bytes 49160 | tf_op jit(solution)/shard_map/ppermute | solution.py:621
  82.7 6.9 %collective-permute-start.8 = (f32[32,128]{1,0:T(8,128)S(1)}, f32[32,128]{1,0:T(8,128)S(1)}, u32[]{:S(2)}, u32[]{:S(2)}) collective-permute-start(f32[32,128]{1,0:T(8,128)S(1)} %get-tuple-element.69), channel_id=1, source_target_pairs={{0,451},{1,0},{2,1},{3,2},{4,3},{5,4},{6,5},{7,6},{8,7},{9,8},{10,... | collective-permute-start | bytes 49160 | tf_op jit(solution)/shard_map/ppermute | solution.py:621
  90.1 8.0 %collective-permute-start.9 = (f32[32,128]{1,0:T(8,128)S(1)}, f32[32,128]{1,0:T(8,128)S(1)}, u32[]{:S(2)}, u32[]{:S(2)}) collective-permute-start(f32[32,128]{1,0:T(8,128)S(1)} %get-tuple-element.72), channel_id=1, source_target_pairs={{0,1},{1,2},{2,3},{3,4},{4,5},{5,6},{6,7},{7,8},{8,9},{9,10},{10,1... | collective-permute-start | bytes 49160 | tf_op jit(solution)/shard_map/ppermute | solution.py:621
  96.1 4.5 %collective-permute-start.10 = (f32[32,128]{1,0:T(8,128)S(1)}, f32[32,128]{1,0:T(8,128)S(1)}, u32[]{:S(2)}, u32[]{:S(2)}) collective-permute-start(f32[32,128]{1,0:T(8,128)S(1)} %get-tuple-element.72), channel_id=1, source_target_pairs={{0,451},{1,0},{2,1},{3,2},{4,3},{5,4},{6,5},{7,6},{8,7},{9,8},{10,... | collective-permute-start | bytes 49160 | tf_op jit(solution)/shard_map/ppermute | solution.py:621
  101.2 6.8 %collective-permute-start.11 = (f32[32,128]{1,0:T(8,128)S(1)}, f32[32,128]{1,0:T(8,128)S(1)}, u32[]{:S(2)}, u32[]{:S(2)}) collective-permute-start(f32[32,128]{1,0:T(8,128)S(1)} %get-tuple-element.75), channel_id=1, source_target_pairs={{0,1},{1,2},{2,3},{3,4},{4,5},{5,6},{6,7},{7,8},{8,9},{9,10},{10,1... | collective-permute-start | bytes 49160 | tf_op jit(solution)/shard_map/ppermute | solution.py:621
  105.8 4.5 %collective-permute-start.12 = (f32[32,128]{1,0:T(8,128)S(1)}, f32[32,128]{1,0:T(8,128)S(1)}, u32[]{:S(2)}, u32[]{:S(2)}) collective-permute-start(f32[32,128]{1,0:T(8,128)S(1)} %get-tuple-element.75), channel_id=1, source_target_pairs={{0,451},{1,0},{2,1},{3,2},{4,3},{5,4},{6,5},{7,6},{8,7},{9,8},{10,... | collective-permute-start | bytes 49160 | tf_op jit(solution)/shard_map/ppermute | solution.py:621
  110.8 6.8 %collective-permute-start.13 = (f32[32,128]{1,0:T(8,128)S(1)}, f32[32,128]{1,0:T(8,128)S(1)}, u32[]{:S(2)}, u32[]{:S(2)}) collective-permute-start(f32[32,128]{1,0:T(8,128)S(1)} %get-tuple-element.78), channel_id=1, source_target_pairs={{0,1},{1,2},{2,3},{3,4},{4,5},{5,6},{6,7},{7,8},{8,9},{9,10},{10,1... | collective-permute-start | bytes 49160 | tf_op jit(solution)/shard_map/ppermute | solution.py:621
  115.5 4.5 %collective-permute-start.14 = (f32[32,128]{1,0:T(8,128)S(1)}, f32[32,128]{1,0:T(8,128)S(1)}, u32[]{:S(2)}, u32[]{:S(2)}) collective-permute-start(f32[32,128]{1,0:T(8,128)S(1)} %get-tuple-element.78), channel_id=1, source_target_pairs={{0,451},{1,0},{2,1},{3,2},{4,3},{5,4},{6,5},{7,6},{8,7},{9,8},{10,... | collective-permute-start | bytes 49160 | tf_op jit(solution)/shard_map/ppermute | solution.py:621
  120.5 6.8 %collective-permute-start.15 = (f32[32,128]{1,0:T(8,128)S(1)}, f32[32,128]{1,0:T(8,128)S(1)}, u32[]{:S(2)}, u32[]{:S(2)}) collective-permute-start(f32[32,128]{1,0:T(8,128)S(1)} %get-tuple-element.81), channel_id=1, source_target_pairs={{0,1},{1,2},{2,3},{3,4},{4,5},{5,6},{6,7},{7,8},{8,9},{9,10},{10,1... | collective-permute-start | bytes 49160 | tf_op jit(solution)/shard_map/ppermute | solution.py:621
  125.1 4.8 %collective-permute-start.16 = (f32[32,128]{1,0:T(8,128)S(1)}, f32[32,128]{1,0:T(8,128)S(1)}, u32[]{:S(2)}, u32[]{:S(2)}) collective-permute-start(f32[32,128]{1,0:T(8,128)S(1)} %get-tuple-element.81), channel_id=1, source_target_pairs={{0,451},{1,0},{2,1},{3,2},{4,3},{5,4},{6,5},{7,6},{8,7},{9,8},{10,... | collective-permute-start | bytes 49160 | tf_op jit(solution)/shard_map/ppermute | solution.py:621
  130.5 6.8 %collective-permute-start.17 = (f32[32,128]{1,0:T(8,128)S(1)}, f32[32,128]{1,0:T(8,128)S(1)}, u32[]{:S(2)}, u32[]{:S(2)}) collective-permute-start(f32[32,128]{1,0:T(8,128)S(1)} %get-tuple-element.84), channel_id=1, source_target_pairs={{0,1},{1,2},{2,3},{3,4},{4,5},{5,6},{6,7},{7,8},{8,9},{9,10},{10,1... | collective-permute-start | bytes 49160 | tf_op jit(solution)/shard_map/ppermute | solution.py:621
  134.8 4.5 %collective-permute-start.18 = (f32[32,128]{1,0:T(8,128)S(1)}, f32[32,128]{1,0:T(8,128)S(1)}, u32[]{:S(2)}, u32[]{:S(2)}) collective-permute-start(f32[32,128]{1,0:T(8,128)S(1)} %get-tuple-element.84), channel_id=1, source_target_pairs={{0,451},{1,0},{2,1},{3,2},{4,3},{5,4},{6,5},{7,6},{8,7},{9,8},{10,... | collective-permute-start | bytes 49160 | tf_op jit(solution)/shard_map/ppermute | solution.py:621
  139.3 36.5 %copy-start.1 = (f32[6,20,1024]{2,1,0:T(8,128)S(1)}, f32[6,20,1024]{2,1,0:T(8,128)}, u32[]{:S(2)}) copy-start(f32[6,20,1024]{2,1,0:T(8,128)} %fields_ref.1) | copy-start | bytes 1474564
  139.9 35.8 %copy-start.3 = (f32[3,4,1024]{2,1,0:T(4,128)S(1)}, f32[3,4,1024]{2,1,0:T(4,128)}, u32[]{:S(2)}) copy-start(f32[3,4,1024]{2,1,0:T(4,128)} %normals_ref.5) | copy-start | bytes 147460
  140.0 35.8 %copy-start.4 = (f32[9,1024]{1,0:T(8,128)S(1)}, f32[9,1024]{1,0:T(8,128)}, u32[]{:S(2)}) copy-start(f32[9,1024]{1,0:T(8,128)} %geometry_ref.3) | copy-start | bytes 110596
  140.0 35.8 %copy-start.5 = (s32[4,1024]{1,0:T(4,128)S(1)}, s32[4,1024]{1,0:T(4,128)}, u32[]{:S(2)}) copy-start(s32[4,1024]{1,0:T(4,128)} %nbr_ref.5) | copy-start | bytes 49156
  140.0 35.8 %copy-start.6 = (f32[4,1024]{1,0:T(4,128)S(1)}, f32[4,1024]{1,0:T(4,128)}, u32[]{:S(2)}) copy-start(f32[4,1024]{1,0:T(4,128)} %scale_ref.5) | copy-start | bytes 49156
  140.0 35.8 %copy-start.7 = (s32[8,128]{1,0:T(8,128)S(1)}, s32[8,128]{1,0:T(8,128)}, u32[]{:S(2)}) copy-start(s32[8,128]{1,0:T(8,128)} %get-tuple-element.86.home_ref) | copy-start | bytes 12292
  184.3 15.8 %collective-permute-start.19 = (f32[64,128]{1,0:T(8,128)S(1)}, f32[64,128]{1,0:T(8,128)S(1)}, u32[]{:S(2)}, u32[]{:S(2)}) collective-permute-start(f32[64,128]{1,0:T(8,128)S(1)} %get-tuple-element.90), channel_id=1, source_target_pairs={{0,1},{1,2},{2,3},{3,4},{4,5},{5,6},{6,7},{7,8},{8,9},{9,10},{10,1... | collective-permute-start | bytes 98312 | tf_op jit(solution)/shard_map/ppermute | solution.py:621
  186.2 13.9 %collective-permute-start.20 = (f32[64,128]{1,0:T(8,128)S(1)}, f32[64,128]{1,0:T(8,128)S(1)}, u32[]{:S(2)}, u32[]{:S(2)}) collective-permute-start(f32[64,128]{1,0:T(8,128)S(1)} %get-tuple-element.90), channel_id=1, source_target_pairs={{0,511},{1,0},{2,1},{3,2},{4,3},{5,4},{6,5},{7,6},{8,7},{9,8},{10,... | collective-permute-start | bytes 98312 | tf_op jit(solution)/shard_map/ppermute | solution.py:621
  (2 other events, 1.4 us)

commit v3 on v2

--- a/solution.py
+++ b/solution.py
@@ -144,9 +144,9 @@
 
 def pack_kernel(
     plain_send_hbm, order_hbm, fields_hbm, nbr_hbm, geometry_hbm, normals_hbm, scale_hbm,
-    out_ref, ends_ref, home_ref,
+    out_ref, ends_ref, home_ref, slot_ref, before_ref,
     plain_send_ref, order_ref, fields_ref, nbr_ref, geometry_ref, normals_ref, scale_ref,
-    send_ref, flat_ref, nb_ref, pool_ref, feature_ref,
+    send_ref, rank_ref, row_ref, flat_ref, nb_ref, pool_ref, dense_ref, feature_ref,
     *sems,
 ):
     pairs = [
@@ -160,7 +160,9 @@
     copies[0].wait()
     copies[1].wait()
     own = fields_ref.shape[2]
+    blocks = own // LANES
     send_blocks = plain_send_ref.shape[0]
+    dense_blocks = dense_ref.shape[1] // LANES
     for sb in range(send_blocks):
         order = rows8(order_ref[sb : sb + 1, :])
         row = jnp.zeros((8, LANES), jnp.int32)
@@ -168,8 +170,29 @@
             block = take(rows8(plain_send_ref[b : b + 1, :]), order & (LANES - 1))
             row = jnp.where((order >> 7) == b, block, row)
         send_ref[sb : sb + 1, :] = row[0:1, :]
-    homes = inverse_of(lambda b: send_ref[b : b + 1, :], send_blocks, own // LANES, -1)
-    for b in range(own // LANES):
+    upper = lax.broadcasted_iota(jnp.int32, (LANES, LANES), 0) <= lax.broadcasted_iota(
+        jnp.int32, (LANES, LANES), 1
+    )
+    upper = jnp.where(upper, 1.0, 0.0)
+    total = jnp.full((8, LANES), -1.0, jnp.float32)
+    for sb in range(send_blocks):
+        filled = rows8(send_ref[sb : sb + 1, :]) < own
+        counts = jnp.where(filled, 1.0, 0.0)
+        rank = total + dot(counts, upper)
+        total += jnp.sum(counts, axis=1, keepdims=True)
+        rank = jnp.where(filled, rank.astype(jnp.int32), LANES * LANES)
+        rank_ref[sb : sb + 1, :] = rank[0:1, :]
+    slots = inverse_of(lambda b: rank_ref[b : b + 1, :], send_blocks, dense_blocks, -1)
+    for b in range(dense_blocks):
+        slot_ref[b : b + 1, :] = slots[b]
+        slot = rows8(slots[b])
+        row = jnp.full((8, LANES), LANES * LANES, jnp.int32)
+        for sb in range(send_blocks):
+            block = take(rows8(send_ref[sb : sb + 1, :]), slot & (LANES - 1))
+            row = jnp.where((slot >> 7) == sb, block, row)
+        row_ref[b : b + 1, :] = row[0:1, :]
+    homes = inverse_of(lambda b: row_ref[b : b + 1, :], dense_blocks, blocks, -1)
+    for b in range(blocks):
         home_ref[b : b + 1, :] = homes[b]
     for copy in copies[2:]:
         copy.wait()
@@ -195,20 +218,18 @@
                         eh * 3 + c, node : node + length, :
                     ]
             pool_ref[eh, f, 30:32, :] = jnp.zeros((2, own), jnp.float32)
-    blocks = own // LANES
     sublane = lax.broadcasted_iota(jnp.int32, (8, LANES), 0)
 
-    def slots(sb, carry):
-        row = rows8(jnp.minimum(send_ref[pl.ds(sb, 1), :], own - 1))
+    def pick(db, carry):
+        row = rows8(jnp.minimum(row_ref[pl.ds(db, 1), :], own - 1))
         lane, which = row & (LANES - 1), row >> 7
         hits = [which == b for b in range(blocks)]
         for group in range(18):
-            value = take(flat_ref[group * 8 : group * 8 + 8, 0:LANES], lane)
+            rows = slice(group * 8, group * 8 + 8)
+            value = take(flat_ref[rows, 0:LANES], lane)
             for b in range(1, blocks):
-                value = jnp.where(
-                    hits[b], take(flat_ref[group * 8 : group * 8 + 8, lanes_at(b)], lane), value
-                )
-            feature_ref[group * 8 : group * 8 + 8, lanes_at(sb)] = value
+                value = jnp.where(hits[b], take(flat_ref[rows, lanes_at(b)], lane), value)
+            dense_ref[rows, lanes_at(db)] = value
         nbr = take(nb_ref[:, 0:LANES], lane)
         for b in range(1, blocks):
             nbr = jnp.where(hits[b], take(nb_ref[:, lanes_at(b)], lane), nbr)
@@ -233,11 +254,25 @@
                 value = groups[group] * sign if group < 4 else groups[group]
                 length = 8 if group % 4 < 3 else 6
                 at = 144 + (group // 4 * 4 + f) * 30 + group % 4 * 8
-                feature_ref[at : at + length, lanes_at(sb)] = value[:length]
+                dense_ref[at : at + length, lanes_at(db)] = value[:length]
         return carry
 
-    lax.fori_loop(0, send_blocks, slots, 0)
-    out_ref[...] = jnp.transpose(feature_ref[...])
+    lax.fori_loop(0, dense_blocks, pick, 0)
+    before_ref[...] = dense_ref[0:64, :]
+    chunks = LANES * out_ref.shape[0] // (send_blocks * LANES)
+    for sb in range(send_blocks):
+        rank = rows8(rank_ref[sb : sb + 1, :])
+        lane = rank & (LANES - 1)
+        hits = [(rank >> 7) == b for b in range(dense_blocks)]
+        for group in range(dense_ref.shape[0] // 8):
+            rows = slice(group * 8, group * 8 + 8)
+            value = jnp.zeros((8, LANES), jnp.float32)
+            for b in range(dense_blocks):
+                value = jnp.where(hits[b], take(dense_ref[rows, lanes_at(b)], lane), value)
+            feature_ref[rows, :] = value
+        out_ref[sb * chunks : (sb + 1) * chunks] = jnp.transpose(feature_ref[...]).reshape(
+            chunks, LANES // chunks, feature_ref.shape[0]
+        )
 
 
 def fine_pool(state_ref, pool_ref):
@@ -411,31 +446,29 @@
 
 
 def coarse_flux(
-    blocks, mirror, nbr_ref, normals_ref, scale_ref, pool_ref, flux_ref, jump_ref, sorted_ref,
-    spread_ref,
+    sources, number_of, mirror, nbr_ref, normals_ref, scale_ref, own_ref, flux_ref, jump_ref,
+    sorted_ref, spread_ref, ends=None,
 ):
     own_blocks = flux_ref.shape[2] // LANES
-    sources = [
-        lambda g, n=n: pool_ref[n // blocks, g * 8 : g * 8 + 8, lanes_at(n % blocks)]
-        for n in range(4 * blocks)
-    ]
     lane_number = lax.broadcasted_iota(jnp.int32, (8, LANES), 1)
     zero = jnp.zeros((8, LANES), jnp.float32)
 
-    def one(eb, carry):
+    def one(eb, outer):
         at = lanes_at(eb)
         for f in range(4):
             code = rows8(nbr_ref[f : f + 1, at])
-            block = code >> 9
-            which = jnp.where(block < blocks, (code & 3) * blocks + block, 4 * blocks)
-            groups = gather32(sources, which, (code >> 2) & (LANES - 1), [zero] * 4)
+            which, lane = number_of(f, at, code)
+            groups = gather32(sources, which, lane, [zero] * 4)
             if mirror:
                 wall = code == 4 * (lane_number + eb * LANES) + f
                 sign = jnp.where(wall, -1.0, 1.0)
                 groups = [group * sign for group in groups]
+            if outer:
+                face = jnp.where(code >= 4 * own_blocks * LANES, code & 3, 4)
+                groups = gather32(ends, face, (code >> 2) & (LANES - 1), groups)
             for g in range(4):
                 jump_ref[f, g * 8 : g * 8 + 8, :] = (
-                    groups[g] - pool_ref[f, g * 8 : g * 8 + 8, at]
+                    groups[g] - own_ref[f, g * 8 : g * 8 + 8, at]
                 )
         regroup(jump_ref, sorted_ref)
         scale = scale_ref[:, at]
@@ -444,9 +477,32 @@
         flux = crossed([spread_ref[c] for c in range(3)], [sorted_ref[c] for c in range(3)])
         for c in range(3):
             flux_ref[c, :, at] = flux[c]
+
+    def inner(eb, carry):
+        one(eb, False)
         return carry
 
-    lax.fori_loop(0, own_blocks, one, 0)
+    if ends is None:
+        lax.fori_loop(0, own_blocks, inner, 0)
+    else:
+        one(0, True)
+        lax.fori_loop(1, own_blocks - 1, inner, 0)
+        one(own_blocks - 1, True)
+
+
+def own_faces(pool_ref, own):
+    blocks = own // LANES
+    sources = [
+        lambda g, n=n: pool_ref[n // blocks, g * 8 : g * 8 + 8, lanes_at(n % blocks)]
+        for n in range(4 * blocks)
+    ]
+
+    def number_of(f, at, code):
+        block = code >> 9
+        which = jnp.where(block < blocks, (code & 3) * blocks + block, 4 * blocks)
+        return which, (code >> 2) & (LANES - 1)
+
+    return sources, number_of
 
 
 def coarse_update(
@@ -476,16 +532,64 @@
     lax.fori_loop(0, own_blocks, one, 0)
 
 
-def coarse_magnetic_kernel(
-    returned_ref, home_ref, fields_ref, below_ref, above_ref, geometry_ref, normals_ref,
-    scale_ref, nbr_ref, derivatives_ref, lift_ref,
+def early_kernel(
+    fields_ref, home_ref, geometry_ref, normals_ref, scale_ref, nbr_ref, derivatives_ref, lift_ref,
+    magnetic_ref, code_ref,
+    pool_ref, flux_ref, jump_ref, sorted_ref, spread_ref, stack_ref, grad_ref, lifted_ref,
+):
+    own = fields_ref.shape[2]
+    blocks = own // LANES
+    coarse_pool(fields_ref, 0, pool_ref)
+    sources, number_of = own_faces(pool_ref, own)
+    coarse_flux(
+        sources, number_of, True, nbr_ref, normals_ref, scale_ref, pool_ref, flux_ref, jump_ref,
+        sorted_ref, spread_ref,
+    )
+
+    def out(c, at, value):
+        magnetic_ref[c, :, at] = value
+
+    coarse_update(
+        -COARSE_STEP, lambda c: fields_ref[c], lambda c, at: fields_ref[3 + c, :, at], out,
+        geometry_ref, derivatives_ref, lift_ref, stack_ref, flux_ref, grad_ref, lifted_ref,
+    )
+    width = jump_ref.shape[2] * 2
+
+    def locate(eb, carry):
+        at = lanes_at(eb)
+        for f in range(4):
+            code = rows8(nbr_ref[f : f + 1, at])
+            home = jnp.full((8, LANES), -1, jnp.int32)
+            for b in range(blocks):
+                block = take(rows8(home_ref[b : b + 1, :]), (code >> 2) & (LANES - 1))
+                home = jnp.where((code >> 9) == b, block, home)
+            code_ref[f : f + 1, at] = jnp.where(home < 0, -1, (code & 3) * width + home)[0:1, :]
+        return carry
+
+    lax.fori_loop(0, blocks, locate, 0)
+
+
+def merge_kernel(
+    returned_ref, home_ref, slot_ref, before_ref, code_ref, magnetic_ref, fields_ref, below_ref,
+    above_ref, geometry_ref, normals_ref, scale_ref, nbr_ref, derivatives_ref, lift_ref,
     merged_ref, ends_ref,
-    flat_ref, back_ref, pool_ref, flux_ref, jump_ref, sorted_ref, spread_ref, stack_ref,
-    grad_ref, lifted_ref,
+    flat_ref, back_ref, dense_ref, change_ref, fine_pool_ref, end_pool_ref,
+    pool_ref, flux_ref, jump_ref, sorted_ref, spread_ref, stack_ref, grad_ref, lifted_ref,
 ):
     own = fields_ref.shape[2]
     slot_blocks = returned_ref.shape[0] // LANES
+    dense_blocks = dense_ref.shape[1] // LANES
     back_ref[...] = jnp.transpose(returned_ref[...])
+    for db in range(dense_blocks):
+        slot = rows8(slot_ref[db : db + 1, :])
+        lane = slot & (LANES - 1)
+        hits = [(slot >> 7) == b for b in range(slot_blocks)]
+        for group in range(15):
+            rows = slice(group * 8, group * 8 + 8)
+            value = jnp.zeros((8, LANES), jnp.float32)
+            for b in range(slot_blocks):
+                value = jnp.where(hits[b], take(back_ref[rows, lanes_at(b)], lane), value)
+            dense_ref[rows, lanes_at(db)] = value
     for c in range(6):
         flat_ref[c * 20 : c * 20 + 20, :] = fields_ref[c]
 
@@ -493,35 +597,59 @@
         at = lanes_at(eb)
         home = rows8(home_ref[pl.ds(eb, 1), :])
         lane = home & (LANES - 1)
-        hits = [(home >> 7) == b for b in range(slot_blocks)]
+        hits = [(home >> 7) == b for b in range(dense_blocks)]
         for group in range(15):
             rows = slice(group * 8, group * 8 + 8)
             value = flat_ref[rows, at]
-            for b in range(slot_blocks):
-                value = jnp.where(hits[b], take(back_ref[rows, lanes_at(b)], lane), value)
+            for b in range(dense_blocks):
+                value = jnp.where(hits[b], take(dense_ref[rows, lanes_at(b)], lane), value)
             flat_ref[rows, at] = value
         return carry
 
     lax.fori_loop(0, own // LANES, merge, 0)
     for c in range(6):
         merged_ref[c] = flat_ref[c * 20 : c * 20 + 20, :]
-    coarse_pool(merged_ref, 0, pool_ref)
+    for c in range(3):
+        change_ref[c] = merged_ref[c] - fields_ref[c]
+    coarse_pool(change_ref, 0, pool_ref)
+    dense_ref[0:64, :] = dense_ref[0:64, :] - before_ref[...]
+    for f in range(4):
+        for c in range(3):
+            for place, node, length in RUNS[f]:
+                rows = slice(c * 10 + place, c * 10 + place + length)
+                first = c * 20 + node
+                fine_pool_ref[f, rows, :] = dense_ref[first : first + length, :]
     halo = halo_rows(below_ref[...], above_ref[...])
 
     def store(f, place, length, value):
-        pool_ref[f, place : place + length, own : own + LANES] = value
+        end_pool_ref[f, place : place + length, :] = value
 
     coarse_halo(halo, store)
+    sources = [
+        lambda g, n=n: fine_pool_ref[
+            n // dense_blocks, g * 8 : g * 8 + 8, lanes_at(n % dense_blocks)
+        ]
+        for n in range(4 * dense_blocks)
+    ]
+    ends = [lambda g, f=f: end_pool_ref[f, g * 8 : g * 8 + 8, :] for f in range(4)]
+
+    def number_of(f, at, code):
+        fine = rows8(code_ref[f : f + 1, at])
+        return fine >> 7, fine & (LANES - 1)
+
     coarse_flux(
-        own // LANES + 1, True, nbr_ref, normals_ref, scale_ref, pool_ref, flux_ref, jump_ref,
-        sorted_ref, spread_ref,
-    )
+        sources, number_of, True, nbr_ref, normals_ref, scale_ref, pool_ref, flux_ref, jump_ref,
+        sorted_ref, spread_ref, ends,
+    )
+
+    def target(c, at):
+        return magnetic_ref[c, :, at] + (merged_ref[3 + c, :, at] - fields_ref[3 + c, :, at])
 
     def out(c, at, value):
         merged_ref[3 + c, :, at] = value
 
     coarse_update(
-        -COARSE_STEP, lambda c: merged_ref[c], lambda c, at: merged_ref[3 + c, :, at], out,
+        -COARSE_STEP, lambda c: change_ref[c], target, out,
         geometry_ref, derivatives_ref, lift_ref, stack_ref, flux_ref, grad_ref, lifted_ref,
     )
     low_half = lax.broadcasted_iota(jnp.int32, (20, LANES), 1) < LANES // 2
@@ -539,8 +667,9 @@
 ):
     own = merged_ref.shape[2]
     coarse_pool(merged_ref, 3, pool_ref)
+    sources, number_of = own_faces(pool_ref, own)
     coarse_flux(
-        own // LANES, False, nbr_ref, normals_ref, scale_ref, pool_ref, flux_ref, jump_ref,
+        sources, number_of, False, nbr_ref, normals_ref, scale_ref, pool_ref, flux_ref, jump_ref,
         sorted_ref, spread_ref,
     )
 
@@ -625,12 +754,10 @@
     return shifted(block, 1, place), shifted(block, -1, place)
 
 
-def swap_slots(rows, width):
-    peers = lax.axis_size("dom")
-    chunks = rows.reshape(peers, rows.shape[0] // peers, width)
-    return lax.all_to_all(chunks, "dom", split_axis=0, concat_axis=0, tiled=True).reshape(
-        rows.shape[0], width
-    )
+def swap_slots(rows):
+    width = rows.shape[-1]
+    chunks = rows.reshape(lax.axis_size("dom"), -1, width)
+    return lax.all_to_all(chunks, "dom", split_axis=0, concat_axis=0, tiled=True).reshape(-1, width)
 
 
 def per_device(
@@ -654,21 +781,40 @@
     table = lax.ppermute(table, RING, [(i, device_of(i)) for i in range(count)])
     send = send_rows.reshape(slots // LANES, LANES)
     order = slot_order(lax.axis_size("dom"), slots // lax.axis_size("dom"))
-    packed, ends, home = call(
+    dense = 2 * fine
+    packed, ends, home, dense_slots, before = call(
         pack_kernel,
-        [((slots, 384), f32), ((64, LANES), f32), ((own // LANES, LANES), i32)],
+        [
+            ((lax.axis_size("dom"), slots // lax.axis_size("dom"), 384), f32), ((64, LANES), f32),
+            ((own // LANES, LANES), i32), ((dense // LANES, LANES), i32), ((64, dense), f32),
+        ],
         [
             (send.shape, i32), (send.shape, i32), (fields.shape, f32), (face_nbr.shape, i32),
             (geometry.shape, f32), (normals.shape, f32), (face_scale.shape, f32),
-            (send.shape, i32), ((144, own), f32), ((8, own), i32), ((2, 4, 32, own), f32),
-            ((384, slots), f32),
+            (send.shape, i32), (send.shape, i32), ((dense // LANES, LANES), i32),
+            ((144, own), f32), ((8, own), i32), ((2, 4, 32, own), f32), ((384, dense), f32),
+            ((384, LANES), f32),
         ],
         send, jnp.asarray(order.reshape(send.shape)), fields, face_nbr, geometry, normals,
         face_scale,
         hbm=range(7),
         vmem=PACK_VMEM_BYTES,
     )
-    received = swap_slots(packed, 384)
+    received = swap_slots(packed)
+    ends_below, ends_above = exchange(ends)
+    work = [
+        ((3, 40, own), f32), ((4, 32, LANES), f32), ((3, 40, LANES), f32), ((3, 40, LANES), f32),
+        ((72, 20), f32), ((3, 72, own), f32), ((3, 20, own), f32),
+    ]
+    early, fine_code = call(
+        early_kernel,
+        [((3, 20, own), f32), (face_nbr.shape, i32)],
+        [((4, 32, own), f32)] + work,
+        fields, home, geometry, normals, face_scale, face_nbr, derivatives, lift_matrix,
+    )
+    received, table, ends_below, ends_above, early, fine_code = lax.optimization_barrier(
+        (received, table, ends_below, ends_above, early, fine_code)
+    )
     state, traces = ((20, 3 * fine), f32), ((4, 32, fine), f32)
     efield, hfield, normal, factors, held, pool, halo, lane, back = call(
         functools.partial(unpack_kernel, width),
@@ -680,14 +826,8 @@
         received, table,
     )
     scratch = [((72, 20), f32), traces, ((3, 40, fine), f32), ((40, 3 * fine), f32)]
-    end_parts = []
     for half in range(2 * SUBSTEPS - 1):
         below, above = exchange(halo, device_of)
-        if half in (0, 1):
-            halo, ends = lax.optimization_barrier((halo, ends))
-            part = shifted(ends, 1 - 2 * half)
-            below, above, part = lax.optimization_barrier((below, above, part))
-            end_parts.append(part)
         magnetic = half % 2 == 0
         source, target = (efield, hfield) if magnetic else (hfield, efield)
         new, pool, halo = call(
@@ -706,17 +846,16 @@
         hfield, efield, pool, below, above, held, normal, factors, table, back, derivatives,
         lift_matrix,
     )
-    returned = swap_slots(outgoing, LANES)
-    work = [
-        ((3, 40, own), f32), ((4, 32, LANES), f32), ((3, 40, LANES), f32), ((3, 40, LANES), f32),
-        ((72, 20), f32), ((3, 72, own), f32), ((3, 20, own), f32),
-    ]
+    returned = swap_slots(outgoing)
     merged, ends = call(
-        coarse_magnetic_kernel,
+        merge_kernel,
         [((6, 20, own), f32), ((64, LANES), f32)],
-        [((120, own), f32), ((128, slots), f32), ((4, 32, own + LANES), f32)] + work,
-        returned, home, fields, end_parts[0], end_parts[1], geometry, normals, face_scale, face_nbr,
-        derivatives, lift_matrix,
+        [
+            ((120, own), f32), ((128, slots), f32), ((120, dense), f32), ((3, 20, own), f32),
+            ((4, 32, dense), f32), traces, ((4, 32, own), f32),
+        ] + work,
+        returned, home, dense_slots, before, fine_code, early, fields, ends_below, ends_above,
+        geometry, normals, face_scale, face_nbr, derivatives, lift_matrix,
     )
     below, above = exchange(ends)
     (electric,) = call(

time: 203 us -> 187 us (0.921)
  waiting for transfers between devices: 39.3 us -> 23.6 us
  local copies, waits for them, and re-layouts: 3.4 us -> 1.09 us
    all_to_all x1, waiting for transfers between devices: 23.6 us -> 9.31 us  [swap_slots(): lax.all_to_all(chunks, 'dom', split_axis=0, concat_axis=0, tiled=True)]
    reshape x1 -> x0, local copies, waits for them, and re-layouts: 2.25 us -> none  [swap_slots(): chunks = rows.reshape(peers, rows.shape[0] // peers, width)]
    pallas_call x13 -> x14, Pallas kernels: 30.2 us -> 32.1 us  [call(): pl.pallas_call(kernel, out_shape=[jax.ShapeDtypeStruct(shape, dtype) for...]
  transfers between devices with their start and end apart: 22 -> 22, of which waited for: 9 -> 9; matrix products, arithmetic and copies ran while one was open for 0% -> 0% of each run, Pallas kernels for 3% -> 8%
where the time goes in v3:
time: 187 us; the launch traced here: 186 us
  starting transfers between devices  91.8 us (49%)
  blocking collectives  36.6 us (20%)
  Pallas kernels  32.1 us (17%)
  waiting for transfers between devices  23.6 us (13%)
    ppermute x20, starting transfers between devices, shifted(): return lax.ppermute(block, RING, pairs)  72.6 us
    all_to_all x1, blocking collectives, swap_slots(): lax.all_to_all(chunks, 'dom', split_axis=0, concat_axis=0, tiled=True)  36.6 us
    pallas_call x14, Pallas kernels, call(): pl.pallas_call(kernel, out_shape=[jax.ShapeDtypeStruct(shape, dtype) for...  32.1 us
    all_to_all x1, starting transfers between devices, swap_slots(): lax.all_to_all(chunks, 'dom', split_axis=0, concat_axis=0, tiled=True)  18.6 us
    ppermute x20, waiting for transfers between devices, shifted(): return lax.ppermute(block, RING, pairs)  14.2 us
    all_to_all x1, waiting for transfers between devices, swap_slots(): lax.all_to_all(chunks, 'dom', split_axis=0, concat_axis=0, tiled=True)  9.31 us
  transfers between devices with their start and end apart: 22, of which 9 were waited for; matrix products, arithmetic and copies ran while one was open for 0% of the time, Pallas kernels for 8%

profile of v3, /device:TPU:1, one launch (start us, length us, event | category | flops | bytes accessed | tf_op | source)
XLA Modules:
  0.0 185.8 jit_solution(4140379202336730038)
XLA Ops:
  0.0 6.4 %shard_map.118 = (f32[128,4,384]{2,1,0:T(4,128)}, f32[64,128]{1,0:T(8,128)}, s32[8,128]{1,0:T(8,128)}, s32[2,128]{1,0:T(2,128)}, f32[64,256]{1,0:T(8,128)}) custom-call(s32[4,128]{1,0:T(4,128)} %bitcast.7, s32[4,128]{1,0:T(4,128)} %constant.1.clone.order_hbm, f32[6,20,1024]{2,1,0:T(8,128)} %fields_ref.3, s32[4,1024]{1,0:T(4,128)} %nbr_ref.7, ...), custom_call_target="tpu_custom_call" | custom-call | tf_op jit(solution)/shard_map/pallas_call | solution.py:731
  6.6 18.6 %all-to-all-start = ((f32[128,4,384]{2,1,0:T(4,128)}), f32[128,4,384]{2,1,0:T(4,128)S(1)}, u32[]{:S(2)}, u32[]{:S(2)}) async-start(f32[128,4,384]{2,1,0:T(4,128)} %get-tuple-element.50), calls=%async_computation | async-start | bytes 1572864 | tf_op jit(solution)/shard_map/all_to_all | solution.py:760
  25.2 3.1 %collective-permute-start.1 = (f32[64,128]{1,0:T(8,128)S(1)}, f32[64,128]{1,0:T(8,128)S(1)}, u32[]{:S(2)}, u32[]{:S(2)}) collective-permute-start(f32[64,128]{1,0:T(8,128)S(1)} %copy-done.13), channel_id=1, source_target_pairs={{0,1},{1,2},{2,3},{3,4},{4,5},{5,6},{6,7},{7,8},{8,9},{9,10},{10,1... | collective-permute-start | bytes 98312 | tf_op jit(solution)/shard_map/ppermute | solution.py:750
  28.3 4.0 %collective-permute-start.2 = (f32[64,128]{1,0:T(8,128)S(1)}, f32[64,128]{1,0:T(8,128)S(1)}, u32[]{:S(2)}, u32[]{:S(2)}) collective-permute-start(f32[64,128]{1,0:T(8,128)S(1)} %copy-done.13), channel_id=1, source_target_pairs={{0,511},{1,0},{2,1},{3,2},{4,3},{5,4},{6,5},{7,6},{8,7},{9,8},{10,... | collective-permute-start | bytes 98312 | tf_op jit(solution)/shard_map/ppermute | solution.py:750
  33.2 7.8 %shard_map.119 = (f32[3,20,1024]{2,1,0:T(8,128)S(1)}, s32[4,1024]{1,0:T(4,128)S(1)}) custom-call(f32[6,20,1024]{2,1,0:T(8,128)S(1)} %copy-done, s32[8,128]{1,0:T(8,128)S(1)} %copy-done.8, f32[9,1024]{1,0:T(8,128)S(1)} %copy-done.4, f32[3,4,1024]{2,1,0:T(4,128)S(1)} %copy-done.3, f32[4,1024]{1,0:T(4,128)S(1)} %copy-done.6, s32[4,1024]{1,0:T(4,128)S(1)} %copy-done.5, ...), custom_call_target="tpu_custom_call" | custom-call | tf_op jit(solution)/shard_map/pallas_call | solution.py:731
  41.0 9.3 %all-to-all-done = f32[128,4,384]{2,1,0:T(4,128)S(1)} async-done(((f32[128,4,384]{2,1,0:T(4,128)}), f32[128,4,384]{2,1,0:T(4,128)S(1)}, u32[]{:S(2)}, u32[]{:S(2)}) %all-to-all-start) | async-done | bytes 786464 | tf_op jit(solution)/shard_map/all_to_all | solution.py:760
  51.2 3.1 %collective-permute-start.3 = (f32[32,128]{1,0:T(8,128)S(1)}, f32[32,128]{1,0:T(8,128)S(1)}, u32[]{:S(2)}, u32[]{:S(2)}) collective-permute-start(f32[32,128]{1,0:T(8,128)S(1)} %get-tuple-element.60), channel_id=1, source_target_pairs={{0,1},{1,2},{2,3},{3,4},{4,5},{5,6},{6,7},{7,8},{8,9},{9,10},{10,1... | collective-permute-start | bytes 49160 | tf_op jit(solution)/shard_map/ppermute | solution.py:750
  54.4 4.7 %collective-permute-start.4 = (f32[32,128]{1,0:T(8,128)S(1)}, f32[32,128]{1,0:T(8,128)S(1)}, u32[]{:S(2)}, u32[]{:S(2)}) collective-permute-start(f32[32,128]{1,0:T(8,128)S(1)} %get-tuple-element.60), channel_id=1, source_target_pairs={{0,451},{1,0},{2,1},{3,2},{4,3},{5,4},{6,5},{7,6},{8,7},{9,8},{10,... | collective-permute-start | bytes 49160 | tf_op jit(solution)/shard_map/ppermute | solution.py:750
  60.5 2.0 %collective-permute-start.5 = (f32[32,128]{1,0:T(8,128)S(1)}, f32[32,128]{1,0:T(8,128)S(1)}, u32[]{:S(2)}, u32[]{:S(2)}) collective-permute-start(f32[32,128]{1,0:T(8,128)S(1)} %get-tuple-element.67), channel_id=1, source_target_pairs={{0,1},{1,2},{2,3},{3,4},{4,5},{5,6},{6,7},{7,8},{8,9},{9,10},{10,1... | collective-permute-start | bytes 49160 | tf_op jit(solution)/shard_map/ppermute | solution.py:750
  62.5 5.3 %collective-permute-start.6 = (f32[32,128]{1,0:T(8,128)S(1)}, f32[32,128]{1,0:T(8,128)S(1)}, u32[]{:S(2)}, u32[]{:S(2)}) collective-permute-start(f32[32,128]{1,0:T(8,128)S(1)} %get-tuple-element.67), channel_id=1, source_target_pairs={{0,451},{1,0},{2,1},{3,2},{4,3},{5,4},{6,5},{7,6},{8,7},{9,8},{10,... | collective-permute-start | bytes 49160 | tf_op jit(solution)/shard_map/ppermute | solution.py:750
  69.2 4.0 %collective-permute-start.7 = (f32[32,128]{1,0:T(8,128)S(1)}, f32[32,128]{1,0:T(8,128)S(1)}, u32[]{:S(2)}, u32[]{:S(2)}) collective-permute-start(f32[32,128]{1,0:T(8,128)S(1)} %get-tuple-element.70), channel_id=1, source_target_pairs={{0,1},{1,2},{2,3},{3,4},{4,5},{5,6},{6,7},{7,8},{8,9},{9,10},{10,1... | collective-permute-start | bytes 49160 | tf_op jit(solution)/shard_map/ppermute | solution.py:750
  73.2 3.3 %collective-permute-start.8 = (f32[32,128]{1,0:T(8,128)S(1)}, f32[32,128]{1,0:T(8,128)S(1)}, u32[]{:S(2)}, u32[]{:S(2)}) collective-permute-start(f32[32,128]{1,0:T(8,128)S(1)} %get-tuple-element.70), channel_id=1, source_target_pairs={{0,451},{1,0},{2,1},{3,2},{4,3},{5,4},{6,5},{7,6},{8,7},{9,8},{10,... | collective-permute-start | bytes 49160 | tf_op jit(solution)/shard_map/ppermute | solution.py:750
  78.5 4.7 %collective-permute-start.9 = (f32[32,128]{1,0:T(8,128)S(1)}, f32[32,128]{1,0:T(8,128)S(1)}, u32[]{:S(2)}, u32[]{:S(2)}) collective-permute-start(f32[32,128]{1,0:T(8,128)S(1)} %get-tuple-element.73), channel_id=1, source_target_pairs={{0,1},{1,2},{2,3},{3,4},{4,5},{5,6},{6,7},{7,8},{8,9},{9,10},{10,1... | collective-permute-start | bytes 49160 | tf_op jit(solution)/shard_map/ppermute | solution.py:750
  83.2 2.1 %collective-permute-start.10 = (f32[32,128]{1,0:T(8,128)S(1)}, f32[32,128]{1,0:T(8,128)S(1)}, u32[]{:S(2)}, u32[]{:S(2)}) collective-permute-start(f32[32,128]{1,0:T(8,128)S(1)} %get-tuple-element.73), channel_id=1, source_target_pairs={{0,451},{1,0},{2,1},{3,2},{4,3},{5,4},{6,5},{7,6},{8,7},{9,8},{10,... | collective-permute-start | bytes 49160 | tf_op jit(solution)/shard_map/ppermute | solution.py:750
  85.3 2.4 %collective-permute-done.10.high_ref = f32[32,128]{1,0:T(8,128)S(1)} collective-permute-done((f32[32,128]{1,0:T(8,128)S(1)}, f32[32,128]{1,0:T(8,128)S(1)}, u32[]{:S(2)}, u32[]{:S(2)}) %collective-permute-start.10) | collective-permute-done | bytes 16416 | tf_op jit(solution)/shard_map/ppermute | solution.py:750
  88.3 4.4 %collective-permute-start.11 = (f32[32,128]{1,0:T(8,128)S(1)}, f32[32,128]{1,0:T(8,128)S(1)}, u32[]{:S(2)}, u32[]{:S(2)}) collective-permute-start(f32[32,128]{1,0:T(8,128)S(1)} %get-tuple-element.76), channel_id=1, source_target_pairs={{0,1},{1,2},{2,3},{3,4},{4,5},{5,6},{6,7},{7,8},{8,9},{9,10},{10,1... | collective-permute-start | bytes 49160 | tf_op jit(solution)/shard_map/ppermute | solution.py:750
  92.6 2.4 %collective-permute-start.12 = (f32[32,128]{1,0:T(8,128)S(1)}, f32[32,128]{1,0:T(8,128)S(1)}, u32[]{:S(2)}, u32[]{:S(2)}) collective-permute-start(f32[32,128]{1,0:T(8,128)S(1)} %get-tuple-element.76), channel_id=1, source_target_pairs={{0,451},{1,0},{2,1},{3,2},{4,3},{5,4},{6,5},{7,6},{8,7},{9,8},{10,... | collective-permute-start | bytes 49160 | tf_op jit(solution)/shard_map/ppermute | solution.py:750
  95.1 2.1 %collective-permute-done.12.high_ref = f32[32,128]{1,0:T(8,128)S(1)} collective-permute-done((f32[32,128]{1,0:T(8,128)S(1)}, f32[32,128]{1,0:T(8,128)S(1)}, u32[]{:S(2)}, u32[]{:S(2)}) %collective-permute-start.12) | collective-permute-done | bytes 16416 | tf_op jit(solution)/shard_map/ppermute | solution.py:750
  97.7 4.5 %collective-permute-start.13 = (f32[32,128]{1,0:T(8,128)S(1)}, f32[32,128]{1,0:T(8,128)S(1)}, u32[]{:S(2)}, u32[]{:S(2)}) collective-permute-start(f32[32,128]{1,0:T(8,128)S(1)} %get-tuple-element.79), channel_id=1, source_target_pairs={{0,1},{1,2},{2,3},{3,4},{4,5},{5,6},{6,7},{7,8},{8,9},{9,10},{10,1... | collective-permute-start | bytes 49160 | tf_op jit(solution)/shard_map/ppermute | solution.py:750
  102.2 2.3 %collective-permute-start.14 = (f32[32,128]{1,0:T(8,128)S(1)}, f32[32,128]{1,0:T(8,128)S(1)}, u32[]{:S(2)}, u32[]{:S(2)}) collective-permute-start(f32[32,128]{1,0:T(8,128)S(1)} %get-tuple-element.79), channel_id=1, source_target_pairs={{0,451},{1,0},{2,1},{3,2},{4,3},{5,4},{6,5},{7,6},{8,7},{9,8},{10,... | collective-permute-start | bytes 49160 | tf_op jit(solution)/shard_map/ppermute | solution.py:750
  104.5 2.5 %collective-permute-done.14.high_ref = f32[32,128]{1,0:T(8,128)S(1)} collective-permute-done((f32[32,128]{1,0:T(8,128)S(1)}, f32[32,128]{1,0:T(8,128)S(1)}, u32[]{:S(2)}, u32[]{:S(2)}) %collective-permute-start.14) | collective-permute-done | bytes 16416 | tf_op jit(solution)/shard_map/ppermute | solution.py:750
  107.5 4.3 %collective-permute-start.15 = (f32[32,128]{1,0:T(8,128)S(1)}, f32[32,128]{1,0:T(8,128)S(1)}, u32[]{:S(2)}, u32[]{:S(2)}) collective-permute-start(f32[32,128]{1,0:T(8,128)S(1)} %get-tuple-element.82), channel_id=1, source_target_pairs={{0,1},{1,2},{2,3},{3,4},{4,5},{5,6},{6,7},{7,8},{8,9},{9,10},{10,1... | collective-permute-start | bytes 49160 | tf_op jit(solution)/shard_map/ppermute | solution.py:750
  111.8 2.5 %collective-permute-start.16 = (f32[32,128]{1,0:T(8,128)S(1)}, f32[32,128]{1,0:T(8,128)S(1)}, u32[]{:S(2)}, u32[]{:S(2)}) collective-permute-start(f32[32,128]{1,0:T(8,128)S(1)} %get-tuple-element.82), channel_id=1, source_target_pairs={{0,451},{1,0},{2,1},{3,2},{4,3},{5,4},{6,5},{7,6},{8,7},{9,8},{10,... | collective-permute-start | bytes 49160 | tf_op jit(solution)/shard_map/ppermute | solution.py:750
  114.3 2.0 %collective-permute-done.16.high_ref = f32[32,128]{1,0:T(8,128)S(1)} collective-permute-done((f32[32,128]{1,0:T(8,128)S(1)}, f32[32,128]{1,0:T(8,128)S(1)}, u32[]{:S(2)}, u32[]{:S(2)}) %collective-permute-start.16) | collective-permute-done | bytes 16416 | tf_op jit(solution)/shard_map/ppermute | solution.py:750
  116.9 4.6 %collective-permute-start.17 = (f32[32,128]{1,0:T(8,128)S(1)}, f32[32,128]{1,0:T(8,128)S(1)}, u32[]{:S(2)}, u32[]{:S(2)}) collective-permute-start(f32[32,128]{1,0:T(8,128)S(1)} %get-tuple-element.85), channel_id=1, source_target_pairs={{0,1},{1,2},{2,3},{3,4},{4,5},{5,6},{6,7},{7,8},{8,9},{9,10},{10,1... | collective-permute-start | bytes 49160 | tf_op jit(solution)/shard_map/ppermute | solution.py:750
  121.5 2.4 %collective-permute-start.18 = (f32[32,128]{1,0:T(8,128)S(1)}, f32[32,128]{1,0:T(8,128)S(1)}, u32[]{:S(2)}, u32[]{:S(2)}) collective-permute-start(f32[32,128]{1,0:T(8,128)S(1)} %get-tuple-element.85), channel_id=1, source_target_pairs={{0,451},{1,0},{2,1},{3,2},{4,3},{5,4},{6,5},{7,6},{8,7},{9,8},{10,... | collective-permute-start | bytes 49160 | tf_op jit(solution)/shard_map/ppermute | solution.py:750
  123.9 2.2 %collective-permute-done.18.high_ref = f32[32,128]{1,0:T(8,128)S(1)} collective-permute-done((f32[32,128]{1,0:T(8,128)S(1)}, f32[32,128]{1,0:T(8,128)S(1)}, u32[]{:S(2)}, u32[]{:S(2)}) %collective-permute-start.18) | collective-permute-done | bytes 16416 | tf_op jit(solution)/shard_map/ppermute | solution.py:750
  126.8 36.6 %all_to_all.10 = f32[128,4,128]{2,1,0:T(4,128)S(1)} all-to-all(f32[128,4,128]{2,1,0:T(4,128)S(1)} %bitcast.6), channel_id=1, replica_groups=mesh['dom'=128,'sub'=4] {'dom'}, dimensions={0} | all-to-all | bytes 524288 | tf_op jit(solution)/shard_map/all_to_all | solution.py:760
  164.1 4.6 %shard_map.129 = (f32[6,20,1024]{2,1,0:T(8,128)S(1)}, f32[64,128]{1,0:T(8,128)S(1)}) custom-call(f32[512,128]{1,0:T(8,128)S(1)} %bitcast.5, s32[8,128]{1,0:T(8,128)S(1)} %copy-done.8, s32[2,128]{1,0:T(2,128)S(1)} %copy-done.9, f32[64,256]{1,0:T(8,128)S(1)} %copy-done.7, s32[4,1024]{1,0:T(4,128)S(1)} %get-tuple-element.89.code_ref, ...), custom_call_target="tpu_custom_call" | custom-call | tf_op jit(solution)/shard_map/pallas_call | solution.py:731
  168.7 1.9 %collective-permute-start.19 = (f32[64,128]{1,0:T(8,128)S(1)}, f32[64,128]{1,0:T(8,128)S(1)}, u32[]{:S(2)}, u32[]{:S(2)}) collective-permute-start(f32[64,128]{1,0:T(8,128)S(1)} %get-tuple-element.94), channel_id=1, source_target_pairs={{0,1},{1,2},{2,3},{3,4},{4,5},{5,6},{6,7},{7,8},{8,9},{9,10},{10,1... | collective-permute-start | bytes 98312 | tf_op jit(solution)/shard_map/ppermute | solution.py:750
  170.6 7.0 %collective-permute-start.20 = (f32[64,128]{1,0:T(8,128)S(1)}, f32[64,128]{1,0:T(8,128)S(1)}, u32[]{:S(2)}, u32[]{:S(2)}) collective-permute-start(f32[64,128]{1,0:T(8,128)S(1)} %get-tuple-element.94), channel_id=1, source_target_pairs={{0,511},{1,0},{2,1},{3,2},{4,3},{5,4},{6,5},{7,6},{8,7},{9,8},{10,... | collective-permute-start | bytes 98312 | tf_op jit(solution)/shard_map/ppermute | solution.py:750
  177.6 6.7 %shard_map.130.electric_ref = f32[3,20,1024]{2,1,0:T(8,128)S(1)} custom-call(f32[6,20,1024]{2,1,0:T(8,128)S(1)} %get-tuple-element.93.merged_ref, f32[9,1024]{1,0:T(8,128)S(1)} %copy-done.4, f32[3,4,1024]{2,1,0:T(4,128)S(1)} %copy-done.3, f32[4,1024]{1,0:T(4,128)S(1)} %copy-done.6, s32[4,1024]{1,0:T(4,128)S(1)} %copy-done.5, f32[3,20,20]{2,1,0:T(8,128)S(1)} %copy-done.1, ...), custom_call_target="tpu_custom_call" | custom-call | tf_op jit(solution)/shard_map/pallas_call | solution.py:731
  (58 shorter events, 11.4 us)
Async XLA Ops:
  6.5 25.9 %copy-start.10 = (s32[4,128]{1,0:T(4,128)S(1)}, s32[4,128]{1,0:T(4,128)}, u32[]{:S(2)}) copy-start(s32[4,128]{1,0:T(4,128)} %param.22) | copy-start | bytes 6148
  6.5 25.9 %copy-start.11 = (s32[2,16]{1,0:T(2,128)S(1)}, s32[2,16]{1,0:T(2,128)}, u32[]{:S(2)}) copy-start(s32[2,16]{1,0:T(2,128)} %param.21) | copy-start | bytes 388
  6.5 25.9 %copy-start.12 = (s32[128]{0:T(128)S(1)}, s32[128]{0:T(128)}, u32[]{:S(2)}) copy-start(s32[128]{0:T(128)} %param.20) | copy-start | bytes 1540
  6.5 26.6 %copy-start = (f32[6,20,1024]{2,1,0:T(8,128)S(1)}, f32[6,20,1024]{2,1,0:T(8,128)}, u32[]{:S(2)}) copy-start(f32[6,20,1024]{2,1,0:T(8,128)} %fields_ref.3) | copy-start | bytes 1474564
  6.5 26.6 %copy-start.1 = (f32[3,20,20]{2,1,0:T(8,128)S(1)}, f32[3,20,20]{2,1,0:T(8,128)}, u32[]{:S(2)}) copy-start(f32[3,20,20]{2,1,0:T(8,128)} %derivatives_ref.21) | copy-start | bytes 14404
  6.5 26.6 %copy-start.3 = (f32[3,4,1024]{2,1,0:T(4,128)S(1)}, f32[3,4,1024]{2,1,0:T(4,128)}, u32[]{:S(2)}) copy-start(f32[3,4,1024]{2,1,0:T(4,128)} %normals_ref.7) | copy-start | bytes 147460
  6.5 26.6 %copy-start.4 = (f32[9,1024]{1,0:T(8,128)S(1)}, f32[9,1024]{1,0:T(8,128)}, u32[]{:S(2)}) copy-start(f32[9,1024]{1,0:T(8,128)} %geometry_ref.5) | copy-start | bytes 110596
  6.5 26.6 %copy-start.5 = (s32[4,1024]{1,0:T(4,128)S(1)}, s32[4,1024]{1,0:T(4,128)}, u32[]{:S(2)}) copy-start(s32[4,1024]{1,0:T(4,128)} %nbr_ref.7) | copy-start | bytes 49156
  6.6 26.6 %copy-start.6 = (f32[4,1024]{1,0:T(4,128)S(1)}, f32[4,1024]{1,0:T(4,128)}, u32[]{:S(2)}) copy-start(f32[4,1024]{1,0:T(4,128)} %scale_ref.7) | copy-start | bytes 49156
  6.6 43.7 %all-to-all-start = ((f32[128,4,384]{2,1,0:T(4,128)}), f32[128,4,384]{2,1,0:T(4,128)S(1)}, u32[]{:S(2)}, u32[]{:S(2)}) async-start(f32[128,4,384]{2,1,0:T(4,128)} %get-tuple-element.50), calls=%async_computation | async-start | bytes 1572864 | tf_op jit(solution)/shard_map/all_to_all | solution.py:760
  25.2 25.4 %collective-permute-start.1 = (f32[64,128]{1,0:T(8,128)S(1)}, f32[64,128]{1,0:T(8,128)S(1)}, u32[]{:S(2)}, u32[]{:S(2)}) collective-permute-start(f32[64,128]{1,0:T(8,128)S(1)} %copy-done.13), channel_id=1, source_target_pairs={{0,1},{1,2},{2,3},{3,4},{4,5},{5,6},{6,7},{7,8},{8,9},{9,10},{10,1... | collective-permute-start | bytes 98312 | tf_op jit(solution)/shard_map/ppermute | solution.py:750
  28.3 22.3 %collective-permute-start.2 = (f32[64,128]{1,0:T(8,128)S(1)}, f32[64,128]{1,0:T(8,128)S(1)}, u32[]{:S(2)}, u32[]{:S(2)}) collective-permute-start(f32[64,128]{1,0:T(8,128)S(1)} %copy-done.13), channel_id=1, source_target_pairs={{0,511},{1,0},{2,1},{3,2},{4,3},{5,4},{6,5},{7,6},{8,7},{9,8},{10,... | collective-permute-start | bytes 98312 | tf_op jit(solution)/shard_map/ppermute | solution.py:750
  32.4 18.1 %collective-permute-start = (s32[8,128]{1,0:T(8,128)S(1)}, s32[8,128]{1,0:T(8,128)S(1)}, u32[]{:S(2)}, u32[]{:S(2)}) collective-permute-start(s32[8,128]{1,0:T(8,128)S(1)} %fusion), channel_id=1, source_target_pairs={{0,0},{1,1},{2,2},{3,3},{4,4},{5,5},{6,6},{7,7},{8,8},{9,9},{10,10... | collective-permute-start | bytes 12296 | tf_op jit(solution)/shard_map/ppermute | solution.py:781
  51.2 7.9 %collective-permute-start.3 = (f32[32,128]{1,0:T(8,128)S(1)}, f32[32,128]{1,0:T(8,128)S(1)}, u32[]{:S(2)}, u32[]{:S(2)}) collective-permute-start(f32[32,128]{1,0:T(8,128)S(1)} %get-tuple-element.60), channel_id=1, source_target_pairs={{0,1},{1,2},{2,3},{3,4},{4,5},{5,6},{6,7},{7,8},{8,9},{9,10},{10,1... | collective-permute-start | bytes 49160 | tf_op jit(solution)/shard_map/ppermute | solution.py:750
  54.4 5.6 %collective-permute-start.4 = (f32[32,128]{1,0:T(8,128)S(1)}, f32[32,128]{1,0:T(8,128)S(1)}, u32[]{:S(2)}, u32[]{:S(2)}) collective-permute-start(f32[32,128]{1,0:T(8,128)S(1)} %get-tuple-element.60), channel_id=1, source_target_pairs={{0,451},{1,0},{2,1},{3,2},{4,3},{5,4},{6,5},{7,6},{8,7},{9,8},{10,... | collective-permute-start | bytes 49160 | tf_op jit(solution)/shard_map/ppermute | solution.py:750
  60.5 7.3 %collective-permute-start.5 = (f32[32,128]{1,0:T(8,128)S(1)}, f32[32,128]{1,0:T(8,128)S(1)}, u32[]{:S(2)}, u32[]{:S(2)}) collective-permute-start(f32[32,128]{1,0:T(8,128)S(1)} %get-tuple-element.67), channel_id=1, source_target_pairs={{0,1},{1,2},{2,3},{3,4},{4,5},{5,6},{6,7},{7,8},{8,9},{9,10},{10,1... | collective-permute-start | bytes 49160 | tf_op jit(solution)/shard_map/ppermute | solution.py:750
  62.5 6.2 %collective-permute-start.6 = (f32[32,128]{1,0:T(8,128)S(1)}, f32[32,128]{1,0:T(8,128)S(1)}, u32[]{:S(2)}, u32[]{:S(2)}) collective-permute-start(f32[32,128]{1,0:T(8,128)S(1)} %get-tuple-element.67), channel_id=1, source_target_pairs={{0,451},{1,0},{2,1},{3,2},{4,3},{5,4},{6,5},{7,6},{8,7},{9,8},{10,... | collective-permute-start | bytes 49160 | tf_op jit(solution)/shard_map/ppermute | solution.py:750
  69.2 7.4 %collective-permute-start.7 = (f32[32,128]{1,0:T(8,128)S(1)}, f32[32,128]{1,0:T(8,128)S(1)}, u32[]{:S(2)}, u32[]{:S(2)}) collective-permute-start(f32[32,128]{1,0:T(8,128)S(1)} %get-tuple-element.70), channel_id=1, source_target_pairs={{0,1},{1,2},{2,3},{3,4},{4,5},{5,6},{6,7},{7,8},{8,9},{9,10},{10,1... | collective-permute-start | bytes 49160 | tf_op jit(solution)/shard_map/ppermute | solution.py:750
  73.2 4.7 %collective-permute-start.8 = (f32[32,128]{1,0:T(8,128)S(1)}, f32[32,128]{1,0:T(8,128)S(1)}, u32[]{:S(2)}, u32[]{:S(2)}) collective-permute-start(f32[32,128]{1,0:T(8,128)S(1)} %get-tuple-element.70), channel_id=1, source_target_pairs={{0,451},{1,0},{2,1},{3,2},{4,3},{5,4},{6,5},{7,6},{8,7},{9,8},{10,... | collective-permute-start | bytes 49160 | tf_op jit(solution)/shard_map/ppermute | solution.py:750
  78.5 6.8 %collective-permute-start.9 = (f32[32,128]{1,0:T(8,128)S(1)}, f32[32,128]{1,0:T(8,128)S(1)}, u32[]{:S(2)}, u32[]{:S(2)}) collective-permute-start(f32[32,128]{1,0:T(8,128)S(1)} %get-tuple-element.73), channel_id=1, source_target_pairs={{0,1},{1,2},{2,3},{3,4},{4,5},{5,6},{6,7},{7,8},{8,9},{9,10},{10,1... | collective-permute-start | bytes 49160 | tf_op jit(solution)/shard_map/ppermute | solution.py:750
  83.2 4.5 %collective-permute-start.10 = (f32[32,128]{1,0:T(8,128)S(1)}, f32[32,128]{1,0:T(8,128)S(1)}, u32[]{:S(2)}, u32[]{:S(2)}) collective-permute-start(f32[32,128]{1,0:T(8,128)S(1)} %get-tuple-element.73), channel_id=1, source_target_pairs={{0,451},{1,0},{2,1},{3,2},{4,3},{5,4},{6,5},{7,6},{8,7},{9,8},{10,... | collective-permute-start | bytes 49160 | tf_op jit(solution)/shard_map/ppermute | solution.py:750
  88.3 6.8 %collective-permute-start.11 = (f32[32,128]{1,0:T(8,128)S(1)}, f32[32,128]{1,0:T(8,128)S(1)}, u32[]{:S(2)}, u32[]{:S(2)}) collective-permute-start(f32[32,128]{1,0:T(8,128)S(1)} %get-tuple-element.76), channel_id=1, source_target_pairs={{0,1},{1,2},{2,3},{3,4},{4,5},{5,6},{6,7},{7,8},{8,9},{9,10},{10,1... | collective-permute-start | bytes 49160 | tf_op jit(solution)/shard_map/ppermute | solution.py:750
  92.6 4.5 %collective-permute-start.12 = (f32[32,128]{1,0:T(8,128)S(1)}, f32[32,128]{1,0:T(8,128)S(1)}, u32[]{:S(2)}, u32[]{:S(2)}) collective-permute-start(f32[32,128]{1,0:T(8,128)S(1)} %get-tuple-element.76), channel_id=1, source_target_pairs={{0,451},{1,0},{2,1},{3,2},{4,3},{5,4},{6,5},{7,6},{8,7},{9,8},{10,... | collective-permute-start | bytes 49160 | tf_op jit(solution)/shard_map/ppermute | solution.py:750
  97.7 6.8 %collective-permute-start.13 = (f32[32,128]{1,0:T(8,128)S(1)}, f32[32,128]{1,0:T(8,128)S(1)}, u32[]{:S(2)}, u32[]{:S(2)}) collective-permute-start(f32[32,128]{1,0:T(8,128)S(1)} %get-tuple-element.79), channel_id=1, source_target_pairs={{0,1},{1,2},{2,3},{3,4},{4,5},{5,6},{6,7},{7,8},{8,9},{9,10},{10,1... | collective-permute-start | bytes 49160 | tf_op jit(solution)/shard_map/ppermute | solution.py:750
  102.2 4.8 %collective-permute-start.14 = (f32[32,128]{1,0:T(8,128)S(1)}, f32[32,128]{1,0:T(8,128)S(1)}, u32[]{:S(2)}, u32[]{:S(2)}) collective-permute-start(f32[32,128]{1,0:T(8,128)S(1)} %get-tuple-element.79), channel_id=1, source_target_pairs={{0,451},{1,0},{2,1},{3,2},{4,3},{5,4},{6,5},{7,6},{8,7},{9,8},{10,... | collective-permute-start | bytes 49160 | tf_op jit(solution)/shard_map/ppermute | solution.py:750
  107.5 6.8 %collective-permute-start.15 = (f32[32,128]{1,0:T(8,128)S(1)}, f32[32,128]{1,0:T(8,128)S(1)}, u32[]{:S(2)}, u32[]{:S(2)}) collective-permute-start(f32[32,128]{1,0:T(8,128)S(1)} %get-tuple-element.82), channel_id=1, source_target_pairs={{0,1},{1,2},{2,3},{3,4},{4,5},{5,6},{6,7},{7,8},{8,9},{9,10},{10,1... | collective-permute-start | bytes 49160 | tf_op jit(solution)/shard_map/ppermute | solution.py:750
  111.8 4.5 %collective-permute-start.16 = (f32[32,128]{1,0:T(8,128)S(1)}, f32[32,128]{1,0:T(8,128)S(1)}, u32[]{:S(2)}, u32[]{:S(2)}) collective-permute-start(f32[32,128]{1,0:T(8,128)S(1)} %get-tuple-element.82), channel_id=1, source_target_pairs={{0,451},{1,0},{2,1},{3,2},{4,3},{5,4},{6,5},{7,6},{8,7},{9,8},{10,... | collective-permute-start | bytes 49160 | tf_op jit(solution)/shard_map/ppermute | solution.py:750
  116.9 7.0 %collective-permute-start.17 = (f32[32,128]{1,0:T(8,128)S(1)}, f32[32,128]{1,0:T(8,128)S(1)}, u32[]{:S(2)}, u32[]{:S(2)}) collective-permute-start(f32[32,128]{1,0:T(8,128)S(1)} %get-tuple-element.85), channel_id=1, source_target_pairs={{0,1},{1,2},{2,3},{3,4},{4,5},{5,6},{6,7},{7,8},{8,9},{9,10},{10,1... | collective-permute-start | bytes 49160 | tf_op jit(solution)/shard_map/ppermute | solution.py:750
  121.5 4.6 %collective-permute-start.18 = (f32[32,128]{1,0:T(8,128)S(1)}, f32[32,128]{1,0:T(8,128)S(1)}, u32[]{:S(2)}, u32[]{:S(2)}) collective-permute-start(f32[32,128]{1,0:T(8,128)S(1)} %get-tuple-element.85), channel_id=1, source_target_pairs={{0,451},{1,0},{2,1},{3,2},{4,3},{5,4},{6,5},{7,6},{8,7},{9,8},{10,... | collective-permute-start | bytes 49160 | tf_op jit(solution)/shard_map/ppermute | solution.py:750
  126.8 36.6 %copy-start.7 = (f32[64,256]{1,0:T(8,128)S(1)}, f32[64,256]{1,0:T(8,128)}, u32[]{:S(2)}) copy-start(f32[64,256]{1,0:T(8,128)} %get-tuple-element.88.before_ref) | copy-start | bytes 196612
  168.7 15.7 %collective-permute-start.19 = (f32[64,128]{1,0:T(8,128)S(1)}, f32[64,128]{1,0:T(8,128)S(1)}, u32[]{:S(2)}, u32[]{:S(2)}) collective-permute-start(f32[64,128]{1,0:T(8,128)S(1)} %get-tuple-element.94), channel_id=1, source_target_pairs={{0,1},{1,2},{2,3},{3,4},{4,5},{5,6},{6,7},{7,8},{8,9},{9,10},{10,1... | collective-permute-start | bytes 98312 | tf_op jit(solution)/shard_map/ppermute | solution.py:750
  170.6 13.8 %collective-permute-start.20 = (f32[64,128]{1,0:T(8,128)S(1)}, f32[64,128]{1,0:T(8,128)S(1)}, u32[]{:S(2)}, u32[]{:S(2)}) collective-permute-start(f32[64,128]{1,0:T(8,128)S(1)} %get-tuple-element.94), channel_id=1, source_target_pairs={{0,511},{1,0},{2,1},{3,2},{4,3},{5,4},{6,5},{7,6},{8,7},{9,8},{10,... | collective-permute-start | bytes 98312 | tf_op jit(solution)/shard_map/ppermute | solution.py:750
  (4 other events, 28.2 us)

commit v4 on v3

--- a/solution.py
+++ b/solution.py
@@ -15,6 +15,7 @@
 VMEM_BYTES = 40 * 2**20
 PACK_VMEM_BYTES = 60 * 2**20
 RING = ("dom", "sub")
+REACH = 4
 highest = lax.Precision.HIGHEST
 
 
@@ -275,29 +276,10 @@
         )
 
 
-def fine_pool(state_ref, pool_ref):
-    for f in range(4):
-        for c in range(3):
-            for place, node, length in RUNS[f]:
-                pool_ref[f, c * 10 + place : c * 10 + place + length, :] = state_ref[
-                    node : node + length, lanes_at(c)
-                ]
-        pool_ref[f, 30:32, :] = jnp.zeros((2, LANES), jnp.float32)
-
-
-def exported(pool_ref, lane):
-    face = lax.broadcasted_iota(jnp.int32, (8, LANES), 1) & 3
-    zero = jnp.zeros((8, LANES), jnp.float32)
-    return gather32(
-        [lambda g, f=f: pool_ref[f, g * 8 : g * 8 + 8, :] for f in range(4)], face, lane, [zero] * 4
-    )
-
-
 def unpack_kernel(
-    width, received_ref, table_ref,
-    efield_ref, hfield_ref, normal_ref, geometry_ref, held_ref, pool_ref, halo_ref, lane_ref,
-    back_ref,
-    feature_ref, picked_ref,
+    width, received_ref, table_ref, lift_ref,
+    out_ref, back_ref,
+    feature_ref, picked_ref, held_ref, sorted_ref, normal_ref, flux_ref,
 ):
     nbr_ref, slots_ref = table_ref.at[0:4], table_ref.at[4:5]
     slot_blocks = received_ref.shape[0] // LANES
@@ -311,108 +293,179 @@
         for b in range(1, slot_blocks):
             value = jnp.where(hits[b], take(feature_ref[at, lanes_at(b)], lane), value)
         picked_ref[at, :] = value
-    for c in range(3):
-        efield_ref[:, lanes_at(c)] = picked_ref[c * 20 : c * 20 + 20, :]
-        hfield_ref[:, lanes_at(c)] = picked_ref[60 + c * 20 : 80 + c * 20, :]
-    geometry_ref[...] = picked_ref[120:136, :]
-    spread_normals(
-        lambda c, f: picked_ref[129 + 4 * c + f : 130 + 4 * c + f, :], normal_ref
-    )
+    spread_normals(lambda c, f: picked_ref[129 + 4 * c + f : 130 + 4 * c + f, :], normal_ref)
     frozen_code = 4 * LANES + 4 * 2 * width
-    for f in range(4):
-        frozen = jnp.broadcast_to(nbr_ref[f : f + 1, :] == frozen_code, (30, LANES))
-        for eh in range(2):
+    for eh in range(2):
+        for f in range(4):
+            frozen = jnp.broadcast_to(nbr_ref[f : f + 1, :] == frozen_code, (30, LANES))
             at = 144 + (eh * 4 + f) * 30
-            held_ref[eh, f, 0:30, :] = jnp.where(frozen, picked_ref[at : at + 30, :], 0.0)
-            held_ref[eh, f, 30:32, :] = jnp.zeros((2, LANES), jnp.float32)
+            held_ref[f, 0:30, :] = jnp.where(frozen, picked_ref[at : at + 30, :], 0.0)
+        regroup(held_ref, sorted_ref)
+        flux = crossed([normal_ref[c] for c in range(3)], [sorted_ref[c] for c in range(3)])
+        for c in range(3):
+            flux_ref[:, lanes_at(eh * 3 + c)] = flux[c]
+    lifted = dot(0.5 * lift_ref[...], flux_ref[...])
     place = lax.broadcasted_iota(jnp.int32, (8, LANES), 1)
     both = take(table_ref[...], (place >> 2) & (width - 1))
-    lane_ref[...] = jnp.where(place < LANES // 2, rows8(both[6:7, :]), rows8(both[5:6, :]))
-    fine_pool(efield_ref, pool_ref)
-    groups = exported(pool_ref, lane_ref[...])
-    for g in range(4):
-        halo_ref[g * 8 : g * 8 + 8, :] = groups[g]
+    lane = jnp.where(place < LANES // 2, rows8(both[6:7, :]), rows8(both[5:6, :]))
+    picked_ref[144:264, :] = jnp.concatenate(
+        [lifted[:, k * LANES : (k + 1) * LANES] for k in range(6)]
+    )
+    picked_ref[264:268, :] = nbr_ref[...].astype(jnp.float32)
+    picked_ref[268:272, :] = lane[0:4, :].astype(jnp.float32)
+    for k in range(out_ref.shape[0]):
+        out_ref[k] = picked_ref[0:272, :]
     backs = inverse_of(lambda b: slots_ref[...], 1, slot_blocks, 0)
     for b in range(slot_blocks):
         back_ref[b : b + 1, :] = backs[b]
 
 
-def fine_rate(
-    source_ref, pool_ref, low_ref, high_ref, held_ref, normal_ref, geometry_ref, nbr_ref,
+def window_state(spot_ref, aligned, shifted, rows, block_ref):
+    half = 2 * REACH
+
+    def fetch(w, carry):
+        spot = spot_ref[w]
+
+        @pl.when(spot < half)
+        def _():
+            block_ref[w, 0:rows, :] = aligned[spot, 0:rows, :]
+
+        @pl.when(spot >= half)
+        def _():
+            block_ref[w, 0:rows, :] = shifted[spot - half, 0:rows, :]
+
+        return carry
+
+    lax.fori_loop(0, 2 * REACH + 1, fetch, 0)
+
+
+def window_steps(
+    derivatives_ref, lift_ref, block_ref, efield_ref, hfield_ref, pool_ref, export_ref, jump_ref,
+    sorted_ref, spread_ref, flux_ref, grad_ref, lifted_ref, stack_ref,
+):
+    blocks = 2 * REACH + 1
+    stack_derivatives(derivatives_ref, stack_ref)
+    lift = 0.5 * lift_ref[...]
+    half_lanes = lax.broadcasted_iota(jnp.int32, (8, LANES), 1) < LANES // 2
+    face = lax.broadcasted_iota(jnp.int32, (8, LANES), 1) & 3
+    zero = jnp.zeros((8, LANES), jnp.float32)
+
+    def prepare(w, carry):
+        for c in range(3):
+            efield_ref[:, lanes_at(w * 3 + c)] = block_ref[w, c * 20 : c * 20 + 20, :]
+            hfield_ref[:, lanes_at(w * 3 + c)] = block_ref[w, 60 + c * 20 : 80 + c * 20, :]
+        spread_normals(
+            lambda c, f: block_ref[w, 129 + 4 * c + f : 130 + 4 * c + f, :], spread_ref.at[w]
+        )
+        return carry
+
+    lax.fori_loop(0, blocks, prepare, 0)
+    for level in range(1, REACH + 1):
+        magnetic = level % 2 == 1
+        source_ref, target_ref = (efield_ref, hfield_ref) if magnetic else (hfield_ref, efield_ref)
+        step = -FINE_STEP if magnetic else FINE_STEP
+        held = 144 if magnetic else 204
+        first, last = level, blocks - level
+
+        def expose(w, carry, source_ref=source_ref):
+            for f in range(4):
+                for c in range(3):
+                    for place, node, length in RUNS[f]:
+                        pool_ref[w, f, c * 10 + place : c * 10 + place + length, :] = source_ref[
+                            node : node + length, lanes_at(w * 3 + c)
+                        ]
+            lane = rows8(block_ref[w, 268:269, :]).astype(jnp.int32)
+            groups = gather32(
+                [lambda g, f=f: pool_ref[w, f, g * 8 : g * 8 + 8, :] for f in range(4)],
+                face, lane, [zero] * 4,
+            )
+            for g in range(4):
+                export_ref[w, g * 8 : g * 8 + 8, :] = groups[g]
+            return carry
+
+        lax.fori_loop(first - 1, last + 1, expose, 0)
+
+        def gather(w, carry):
+            sources = [
+                lambda g, f=f: pool_ref[w, f, g * 8 : g * 8 + 8, :] for f in range(4)
+            ]
+            halo = [
+                jnp.where(
+                    half_lanes,
+                    export_ref[w - 1, g * 8 : g * 8 + 8, :],
+                    export_ref[w + 1, g * 8 : g * 8 + 8, :],
+                )
+                for g in range(4)
+            ]
+            sources.append(lambda g: halo[g])
+            for f in range(4):
+                code = rows8(block_ref[w, 264 + f : 265 + f, :]).astype(jnp.int32)
+                local = code < 4 * LANES
+                which = jnp.where(local, code & 3, code >> 7)
+                lane = jnp.where(local, code >> 2, code) & (LANES - 1)
+                groups = gather32(sources, which, lane, [zero] * 4)
+                for g in range(4):
+                    jump_ref[f, g * 8 : g * 8 + 8, :] = (
+                        groups[g] - pool_ref[w, f, g * 8 : g * 8 + 8, :]
+                    )
+            regroup(jump_ref, sorted_ref)
+            flux = crossed([spread_ref[w, c] for c in range(3)], [sorted_ref[c] for c in range(3)])
+            for c in range(3):
+                flux_ref[:, lanes_at(w * 3 + c)] = flux[c]
+            return carry
+
+        lax.fori_loop(first, last, gather, 0)
+        span = slice(first * 3 * LANES, last * 3 * LANES)
+        grad_ref[:, span] = dot(stack_ref[...], source_ref[:, span])
+        lifted_ref[:, span] = dot(lift, flux_ref[:, span])
+
+        def update(w, carry, target_ref=target_ref, step=step, held=held):
+            def factor(m, a):
+                return block_ref[w, 120 + 3 * m + a : 121 + 3 * m + a, :]
+
+            def grad(a, c):
+                return grad_ref[a * 24 : a * 24 + 20, lanes_at(w * 3 + c)]
+
+            for c in range(3):
+                at = lanes_at(w * 3 + c)
+                rate = (
+                    curl_part(c, factor, grad)
+                    + lifted_ref[:, at]
+                    + block_ref[w, held + c * 20 : held + c * 20 + 20, :]
+                )
+                target_ref[:, at] = target_ref[:, at] + step * rate
+            return carry
+
+        lax.fori_loop(first, last, update, 0)
+
+
+def first_window_kernel(
+    spot_ref, aligned_ref, shifted_ref, derivatives_ref, lift_ref,
+    out_ref,
+    block_ref, efield_ref, hfield_ref, *scratch,
+):
+    window_state(spot_ref, aligned_ref, shifted_ref, 272, block_ref)
+    window_steps(derivatives_ref, lift_ref, block_ref, efield_ref, hfield_ref, *scratch)
+    for c in range(3):
+        electric = efield_ref[:, lanes_at(REACH * 3 + c)]
+        magnetic = hfield_ref[:, lanes_at(REACH * 3 + c)]
+        for k in range(out_ref.shape[0]):
+            out_ref[k, c * 20 : c * 20 + 20, :] = electric
+            out_ref[k, 60 + c * 20 : 80 + c * 20, :] = magnetic
+
+
+def last_window_kernel(
+    spot_ref, aligned_ref, shifted_ref, aligned_state_ref, shifted_state_ref, back_ref,
     derivatives_ref, lift_ref,
-    stack_ref, jump_ref, sorted_ref, flux_ref,
-):
-    stack_derivatives(derivatives_ref, stack_ref)
-    grads = dot(stack_ref[...], source_ref[...])
-    half = lax.broadcasted_iota(jnp.int32, (8, LANES), 1) < LANES // 2
-    halo = [
-        jnp.where(half, low_ref[g * 8 : g * 8 + 8, :], high_ref[g * 8 : g * 8 + 8, :])
-        for g in range(4)
-    ]
-    sources = [lambda g, f=f: pool_ref[f, g * 8 : g * 8 + 8, :] for f in range(4)]
-    sources.append(lambda g: halo[g])
-    for f in range(4):
-        code = rows8(nbr_ref[f : f + 1, :])
-        local = code < 4 * LANES
-        which = jnp.where(local, code & 3, code >> 7)
-        lane = jnp.where(local, code >> 2, code) & (LANES - 1)
-        groups = gather32(
-            sources, which, lane, [held_ref[f, g * 8 : g * 8 + 8, :] for g in range(4)]
-        )
-        for g in range(4):
-            jump_ref[f, g * 8 : g * 8 + 8, :] = groups[g] - pool_ref[f, g * 8 : g * 8 + 8, :]
-    regroup(jump_ref, sorted_ref)
-    flux = crossed([normal_ref[c] for c in range(3)], [sorted_ref[c] for c in range(3)])
+    out_ref,
+    result_ref, feature_ref, block_ref, efield_ref, hfield_ref, *scratch,
+):
+    window_state(spot_ref, aligned_ref, shifted_ref, 272, block_ref)
+    window_state(spot_ref, aligned_state_ref, shifted_state_ref, 120, block_ref)
+    window_steps(derivatives_ref, lift_ref, block_ref, efield_ref, hfield_ref, *scratch)
     for c in range(3):
-        flux_ref[:, lanes_at(c)] = flux[c]
-    lifted = dot(0.5 * lift_ref[...], flux_ref[...])
-
-    def factor(m, a):
-        return geometry_ref[3 * m + a : 3 * m + a + 1, :]
-
-    def grad(a, c):
-        return grads[a * 24 : a * 24 + 20, c * LANES : (c + 1) * LANES]
-
-    return [
-        curl_part(c, factor, grad) + lifted[:, c * LANES : (c + 1) * LANES] for c in range(3)
-    ]
-
-
-def fine_kernel(
-    magnetic,
-    source_ref, target_ref, pool_ref, low_ref, high_ref, held_ref, normal_ref, geometry_ref,
-    nbr_ref, lane_ref, derivatives_ref, lift_ref,
-    out_ref, new_pool_ref, halo_ref,
-    *scratch,
-):
-    field = 0 if magnetic else 1
-    step = -FINE_STEP if magnetic else FINE_STEP
-    rate = fine_rate(
-        source_ref, pool_ref, low_ref, high_ref, held_ref.at[field], normal_ref, geometry_ref,
-        nbr_ref, derivatives_ref, lift_ref, *scratch,
-    )
-    for c in range(3):
-        out_ref[:, lanes_at(c)] = target_ref[:, lanes_at(c)] + step * rate[c]
-    fine_pool(out_ref, new_pool_ref)
-    groups = exported(new_pool_ref, lane_ref[...])
-    for g in range(4):
-        halo_ref[g * 8 : g * 8 + 8, :] = groups[g]
-
-
-def last_fine_kernel(
-    source_ref, target_ref, pool_ref, low_ref, high_ref, held_ref, normal_ref, geometry_ref,
-    nbr_ref, back_ref, derivatives_ref, lift_ref,
-    out_ref,
-    result_ref, feature_ref,
-    *scratch,
-):
-    rate = fine_rate(
-        source_ref, pool_ref, low_ref, high_ref, held_ref.at[1], normal_ref, geometry_ref,
-        nbr_ref, derivatives_ref, lift_ref, *scratch,
-    )
-    for c in range(3):
-        result_ref[c * 20 : c * 20 + 20, :] = target_ref[:, lanes_at(c)] + FINE_STEP * rate[c]
-        result_ref[60 + c * 20 : 80 + c * 20, :] = source_ref[:, lanes_at(c)]
+        result_ref[c * 20 : c * 20 + 20, :] = efield_ref[:, lanes_at(REACH * 3 + c)]
+        result_ref[60 + c * 20 : 80 + c * 20, :] = hfield_ref[:, lanes_at(REACH * 3 + c)]
     result_ref[120:128, :] = jnp.zeros((8, LANES), jnp.float32)
     for b in range(back_ref.shape[0]):
         lane = rows8(back_ref[b : b + 1, :])
@@ -723,10 +776,12 @@
         out_ref[3 + c] = merged_ref[3 + c]
 
 
-def call(kernel, outs, scratch, *args, hbm=(), vmem=VMEM_BYTES):
+def call(kernel, outs, scratch, *args, hbm=(), smem=(), vmem=VMEM_BYTES):
     whole = pl.BlockSpec(memory_space=pltpu.VMEM)
     specs = [
-        pl.BlockSpec(memory_space=pltpu.HBM) if number in hbm else whole for number in range(len(args))
+        pl.BlockSpec(memory_space=pltpu.HBM if number in hbm else pltpu.SMEM if number in smem
+                     else pltpu.VMEM)
+        for number in range(len(args))
     ]
     return pl.pallas_call(
         kernel,
@@ -744,14 +799,35 @@
     return int(seats(lax.axis_size("dom"))[block // sub]) * sub + block % sub
 
 
-def shifted(block, by, place=int):
+def exchange(block):
     count = lax.axis_size(RING)
-    pairs = [(place(i), place((i + by) % count)) for i in range(count)]
-    return lax.ppermute(block, RING, pairs)
-
-
-def exchange(block, place=int):
-    return shifted(block, 1, place), shifted(block, -1, place)
+    up = [(i, (i + 1) % count) for i in range(count)]
+    down = [(target, source) for source, target in up]
+    return lax.ppermute(block, RING, up), lax.ppermute(block, RING, down)
+
+
+def share(copies):
+    count, size = lax.axis_size(RING), copies.shape[0]
+
+    def within(start):
+        groups = [
+            [device_of((first + i + start) % count) for i in range(size)]
+            for first in range(0, count, size)
+        ]
+        return lax.all_to_all(copies, RING, 0, 0, axis_index_groups=groups, tiled=True)
+
+    return within(0), within(size // 2)
+
+
+def spots(count, size):
+    table = np.zeros((count, 16), np.int32)
+    for block in range(count):
+        for w in range(2 * REACH + 1):
+            at = block % size + w - REACH
+            if not 0 <= at < size:
+                at = (block + size // 2) % size + w - REACH + size
+            table[device_of(block), w] = at
+    return table
 
 
 def swap_slots(rows):
@@ -779,6 +855,11 @@
     )
     count = lax.axis_size(RING)
     table = lax.ppermute(table, RING, [(i, device_of(i)) for i in range(count)])
+    me = lax.axis_index(RING)
+    spot = lax.dynamic_index_in_dim(
+        jnp.asarray(spots(count, 2 * REACH)), me, keepdims=False
+    )
+    traces = ((4, 32, fine), f32)
     send = send_rows.reshape(slots // LANES, LANES)
     order = slot_order(lax.axis_size("dom"), slots // lax.axis_size("dom"))
     dense = 2 * fine
@@ -812,39 +893,41 @@
         [((4, 32, own), f32)] + work,
         fields, home, geometry, normals, face_scale, face_nbr, derivatives, lift_matrix,
     )
-    received, table, ends_below, ends_above, early, fine_code = lax.optimization_barrier(
-        (received, table, ends_below, ends_above, early, fine_code)
-    )
-    state, traces = ((20, 3 * fine), f32), ((4, 32, fine), f32)
-    efield, hfield, normal, factors, held, pool, halo, lane, back = call(
+    received, table, ends_below, ends_above, early, fine_code, spot = lax.optimization_barrier(
+        (received, table, ends_below, ends_above, early, fine_code, spot)
+    )
+    group = 2 * REACH
+    blocks = group + 1
+    copies, back = call(
         functools.partial(unpack_kernel, width),
+        [((group, 272, fine), f32), ((slots // LANES, LANES), i32)],
         [
-            state, state, ((3, 40, fine), f32), ((16, fine), f32), ((2, 4, 32, fine), f32),
-            traces, ((32, fine), f32), ((8, fine), i32), ((slots // LANES, LANES), i32),
+            ((384, slots), f32), ((384, fine), f32), traces, ((3, 40, fine), f32),
+            ((3, 40, fine), f32), ((40, 6 * fine), f32),
         ],
-        [((384, slots), f32), ((384, fine), f32)],
-        received, table,
-    )
-    scratch = [((72, 20), f32), traces, ((3, 40, fine), f32), ((40, 3 * fine), f32)]
-    for half in range(2 * SUBSTEPS - 1):
-        below, above = exchange(halo, device_of)
-        magnetic = half % 2 == 0
-        source, target = (efield, hfield) if magnetic else (hfield, efield)
-        new, pool, halo = call(
-            functools.partial(fine_kernel, magnetic),
-            [state, traces, ((32, fine), f32)],
-            scratch,
-            source, target, pool, below, above, held, normal, factors, table, lane,
-            derivatives, lift_matrix,
-        )
-        efield, hfield = (efield, new) if magnetic else (new, hfield)
-    below, above = exchange(halo, device_of)
+        received, table, lift_matrix,
+    )
+    window = [
+        ((blocks, 272, fine), f32), ((20, blocks * 3 * fine), f32), ((20, blocks * 3 * fine), f32),
+        ((blocks, 4, 32, fine), f32), ((blocks, 32, fine), f32), traces, ((3, 40, fine), f32),
+        ((blocks, 3, 40, fine), f32), ((40, blocks * 3 * fine), f32),
+        ((72, blocks * 3 * fine), f32), ((20, blocks * 3 * fine), f32), ((72, 20), f32),
+    ]
+    aligned, offset = share(copies)
+    (copies,) = call(
+        first_window_kernel,
+        [((group, 120, fine), f32)],
+        window,
+        spot, aligned, offset, derivatives, lift_matrix,
+        smem=(0,),
+    )
+    aligned_state, offset_state = share(copies)
     (outgoing,) = call(
-        last_fine_kernel,
+        last_window_kernel,
         [((slots, LANES), f32)],
-        [((128, fine), f32), ((128, slots), f32)] + scratch,
-        hfield, efield, pool, below, above, held, normal, factors, table, back, derivatives,
-        lift_matrix,
+        [((128, fine), f32), ((128, slots), f32)] + window,
+        spot, aligned, offset, aligned_state, offset_state, back, derivatives, lift_matrix,
+        smem=(0,),
     )
     returned = swap_slots(outgoing)
     merged, ends = call(

time: 187 us -> 177 us (0.947)
  starting transfers between devices: 91.8 us -> 32.4 us
  blocking collectives: 36.6 us -> 86.1 us
  Pallas kernels: 32.1 us -> 47.5 us
  waiting for transfers between devices: 23.6 us -> 8.66 us
    all_to_all x0 -> x4, blocking collectives: none -> 63.6 us  [within(): lax.all_to_all(copies, RING, 0, 0, axis_index_groups=groups, tiled=True)]
    ppermute x20 -> x4, starting transfers between devices: 72.6 us -> 13.2 us  [exchange(): return (lax.ppermute(block, RING, up), lax.ppermute(block, RING, down))]
    pallas_call x14 -> x8, Pallas kernels: 32.1 us -> 47.5 us  [call(): pl.pallas_call(kernel, out_shape=[jax.ShapeDtypeStruct(shape, dtype) for...]
    ppermute x20 -> x4, waiting for transfers between devices: 14.2 us -> 0.01 us  [exchange(): return (lax.ppermute(block, RING, up), lax.ppermute(block, RING, down))]
    all_to_all x1, blocking collectives: 36.6 us -> 22.5 us  [swap_slots(): lax.all_to_all(chunks, 'dom', split_axis=0, concat_axis=0, tiled=True)]
  transfers between devices with their start and end apart: 22 -> 6, of which waited for: 9 -> 1; matrix products, arithmetic and copies ran while one was open for 0% -> 1% of each run, Pallas kernels for 8% -> 8%
where the time goes in v4:
time: 177 us; the launch traced here: 176 us
  blocking collectives  86.1 us (49%)
  Pallas kernels  47.5 us (27%)
  starting transfers between devices  32.4 us (18%)
  waiting for transfers between devices  8.66 us (5%)
    all_to_all x4, blocking collectives, within(): lax.all_to_all(copies, RING, 0, 0, axis_index_groups=groups, tiled=True)  63.6 us
    pallas_call x8, Pallas kernels, call(): pl.pallas_call(kernel, out_shape=[jax.ShapeDtypeStruct(shape, dtype) for...  47.5 us
    all_to_all x1, blocking collectives, swap_slots(): lax.all_to_all(chunks, 'dom', split_axis=0, concat_axis=0, tiled=True)  22.5 us
    all_to_all x1, starting transfers between devices, swap_slots(): lax.all_to_all(chunks, 'dom', split_axis=0, concat_axis=0, tiled=True)  18.6 us
    ppermute x4, starting transfers between devices, exchange(): return (lax.ppermute(block, RING, up), lax.ppermute(block, RING, down))  13.2 us
    all_to_all x1, waiting for transfers between devices, swap_slots(): lax.all_to_all(chunks, 'dom', split_axis=0, concat_axis=0, tiled=True)  8.65 us
  transfers between devices with their start and end apart: 6, of which 1 were waited for; matrix products, arithmetic and copies ran while one was open for 1% of the time, Pallas kernels for 8%

profile of v4, /device:TPU:1, one launch (start us, length us, event | category | flops | bytes accessed | tf_op | source)
XLA Modules:
  0.0 176.1 jit_solution(3432815388620425044)
XLA Ops:
  0.1 6.5 %shard_map.127 = (f32[128,4,384]{2,1,0:T(4,128)}, f32[64,128]{1,0:T(8,128)}, s32[8,128]{1,0:T(8,128)}, s32[2,128]{1,0:T(2,128)}, f32[64,256]{1,0:T(8,128)}) custom-call(s32[4,128]{1,0:T(4,128)} %bitcast.9, s32[4,128]{1,0:T(4,128)} %constant.24.clone.order_hbm, f32[6,20,1024]{2,1,0:T(8,128)} %fields_ref.3, s32[4,1024]{1,0:T(4,128)} %nbr_ref.7, ...), custom_call_target="tpu_custom_call" | custom-call | tf_op jit(solution)/shard_map/pallas_call | solution.py:786
  6.6 18.6 %all-to-all-start = ((f32[128,4,384]{2,1,0:T(4,128)}), f32[128,4,384]{2,1,0:T(4,128)S(1)}, u32[]{:S(2)}, u32[]{:S(2)}) async-start(f32[128,4,384]{2,1,0:T(4,128)} %get-tuple-element.23), calls=%async_computation | async-start | bytes 1572864 | tf_op jit(solution)/shard_map/all_to_all | solution.py:836
  25.2 5.2 %collective-permute-start.2 = (f32[64,128]{1,0:T(8,128)S(1)}, f32[64,128]{1,0:T(8,128)S(1)}, u32[]{:S(2)}, u32[]{:S(2)}) collective-permute-start(f32[64,128]{1,0:T(8,128)S(1)} %copy-done.13), channel_id=1, source_target_pairs={{1,0},{2,1},{3,2},{4,3},{5,4},{6,5},{7,6},{8,7},{9,8},{10,9},{11,1... | collective-permute-start | bytes 98312 | tf_op jit(solution)/shard_map/ppermute | solution.py:806
  30.4 1.9 %collective-permute-start.1 = (f32[64,128]{1,0:T(8,128)S(1)}, f32[64,128]{1,0:T(8,128)S(1)}, u32[]{:S(2)}, u32[]{:S(2)}) collective-permute-start(f32[64,128]{1,0:T(8,128)S(1)} %copy-done.13), channel_id=1, source_target_pairs={{0,1},{1,2},{2,3},{3,4},{4,5},{5,6},{6,7},{7,8},{8,9},{9,10},{10,1... | collective-permute-start | bytes 98312 | tf_op jit(solution)/shard_map/ppermute | solution.py:806
  32.3 0.1 pad.8.clone
  32.4 0.0 copy-done.12
  32.4 0.1 fusion
  32.4 0.7 collective-permute-start
  33.1 0.7 dynamic-slice_bitcast_fusion.spot_ref
  33.8 0.0 copy-done
  33.8 0.0 copy-done.3
  33.9 7.8 %shard_map.128 = (f32[3,20,1024]{2,1,0:T(8,128)S(1)}, s32[4,1024]{1,0:T(4,128)S(1)}) custom-call(f32[6,20,1024]{2,1,0:T(8,128)S(1)} %copy-done, s32[8,128]{1,0:T(8,128)S(1)} %copy-done.8, f32[9,1024]{1,0:T(8,128)S(1)} %copy-done.2, f32[3,4,1024]{2,1,0:T(4,128)S(1)} %copy-done.1, f32[4,1024]{1,0:T(4,128)S(1)} %copy-done.6, s32[4,1024]{1,0:T(4,128)S(1)} %copy-done.5, ...), custom_call_target="tpu_custom_call" | custom-call | tf_op jit(solution)/shard_map/pallas_call | solution.py:786
  41.7 8.6 %all-to-all-done = f32[128,4,384]{2,1,0:T(4,128)S(1)} async-done(((f32[128,4,384]{2,1,0:T(4,128)}), f32[128,4,384]{2,1,0:T(4,128)S(1)}, u32[]{:S(2)}, u32[]{:S(2)}) %all-to-all-start) | async-done | bytes 786464 | tf_op jit(solution)/shard_map/all_to_all | solution.py:836
  50.3 0.3 reshape.16.received_ref
  50.6 0.0 collective-permute-done.table_ref
  50.6 0.0 collective-permute-done.2.above_ref
  50.6 0.0 collective-permute-done.1.below_ref
  50.6 0.7 shard_map.129
  51.4 21.8 %all_to_all.30.aligned_ref = f32[8,272,128]{2,1,0:T(8,128)S(1)} all-to-all(f32[8,272,128]{2,1,0:T(8,128)S(1)} %get-tuple-element.31), channel_id=1, replica_groups={{0,1,2,3,4,5,6,7},{8,9,10,11,12,13,14,15},{16,17,18,19,20,21,22,23},{24..., dimensions={0} | all-to-all | bytes 2228224 | tf_op jit(solution)/shard_map/all_to_all | solution.py:817
  73.1 15.9 %all_to_all.31.shifted_ref = f32[8,272,128]{2,1,0:T(8,128)S(1)} all-to-all(f32[8,272,128]{2,1,0:T(8,128)S(1)} %get-tuple-element.31), channel_id=1, replica_groups={{4,5,6,7,8,9,10,11},{12,13,14,15,16,17,18,19},{20,21,22,23,24,25,26,27}..., dimensions={0} | all-to-all | bytes 2228224 | tf_op jit(solution)/shard_map/all_to_all | solution.py:817
  89.0 9.6 %shard_map.130 = f32[8,120,128]{2,1,0:T(8,128)S(1)} custom-call(s32[16]{0:T(128)S(1)} %dynamic-slice_bitcast_fusion.spot_ref, f32[8,272,128]{2,1,0:T(8,128)S(1)} %all_to_all.30.aligned_ref, f32[8,272,128]{2,1,0:T(8,128)S(1)} %all_to_all.31.shifted_ref, f32[3,20,20]{2,1,0:T(8,128)S(1)} %copy-done.3, f32[20,40]{1,0:T(8,128)S(1)} %copy-done.4), custom_call_target="tpu_custom_call" | custom-call | tf_op jit(solution)/shard_map/pallas_call | solution.py:786
  98.7 14.6 %all_to_all.32.aligned_state_ref = f32[8,120,128]{2,1,0:T(8,128)S(1)} all-to-all(f32[8,120,128]{2,1,0:T(8,128)S(1)} %shard_map.130), channel_id=1, replica_groups={{0,1,2,3,4,5,6,7},{8,9,10,11,12,13,14,15},{16,17,18,19,20,21,22,23},{24..., dimensions={0} | all-to-all | bytes 983040 | tf_op jit(solution)/shard_map/all_to_all | solution.py:817
  113.2 11.4 %all_to_all.33.shifted_state_ref = f32[8,120,128]{2,1,0:T(8,128)S(1)} all-to-all(f32[8,120,128]{2,1,0:T(8,128)S(1)} %shard_map.130), channel_id=1, replica_groups={{4,5,6,7,8,9,10,11},{12,13,14,15,16,17,18,19},{20,21,22,23,24,25,26,27}..., dimensions={0} | all-to-all | bytes 983040 | tf_op jit(solution)/shard_map/all_to_all | solution.py:817
  124.7 10.1 %shard_map.131 = f32[512,128]{1,0:T(8,128)S(1)} custom-call(s32[16]{0:T(128)S(1)} %dynamic-slice_bitcast_fusion.spot_ref, f32[8,272,128]{2,1,0:T(8,128)S(1)} %all_to_all.30.aligned_ref, f32[8,272,128]{2,1,0:T(8,128)S(1)} %all_to_all.31.shifted_ref, f32[8,120,128]{2,1,0:T(8,128)S(1)} %all_to_all.32.aligned_state_ref, ...), custom_call_target="tpu_custom_call" | custom-call | tf_op jit(solution)/shard_map/pallas_call | solution.py:786
  134.7 22.5 %all_to_all.34 = f32[128,4,128]{2,1,0:T(4,128)S(1)} all-to-all(f32[128,4,128]{2,1,0:T(4,128)S(1)} %bitcast.8), channel_id=1, replica_groups=mesh['dom'=128,'sub'=4] {'dom'}, dimensions={0} | all-to-all | bytes 524288 | tf_op jit(solution)/shard_map/all_to_all | solution.py:836
  157.2 4.6 %shard_map.132 = (f32[6,20,1024]{2,1,0:T(8,128)S(1)}, f32[64,128]{1,0:T(8,128)S(1)}) custom-call(f32[512,128]{1,0:T(8,128)S(1)} %bitcast.7, s32[8,128]{1,0:T(8,128)S(1)} %copy-done.8, s32[2,128]{1,0:T(2,128)S(1)} %copy-done.9, f32[64,256]{1,0:T(8,128)S(1)} %copy-done.7, s32[4,1024]{1,0:T(4,128)S(1)} %get-tuple-element.35.code_ref, ...), custom_call_target="tpu_custom_call" | custom-call | tf_op jit(solution)/shard_map/pallas_call | solution.py:786
  161.8 4.2 %collective-permute-start.4 = (f32[64,128]{1,0:T(8,128)S(1)}, f32[64,128]{1,0:T(8,128)S(1)}, u32[]{:S(2)}, u32[]{:S(2)}) collective-permute-start(f32[64,128]{1,0:T(8,128)S(1)} %get-tuple-element.40), channel_id=1, source_target_pairs={{1,0},{2,1},{3,2},{4,3},{5,4},{6,5},{7,6},{8,7},{9,8},{10,9},{11,1... | collective-permute-start | bytes 98312 | tf_op jit(solution)/shard_map/ppermute | solution.py:806
  166.0 1.9 %collective-permute-start.3 = (f32[64,128]{1,0:T(8,128)S(1)}, f32[64,128]{1,0:T(8,128)S(1)}, u32[]{:S(2)}, u32[]{:S(2)}) collective-permute-start(f32[64,128]{1,0:T(8,128)S(1)} %get-tuple-element.40), channel_id=1, source_target_pairs={{0,1},{1,2},{2,3},{3,4},{4,5},{5,6},{6,7},{7,8},{8,9},{9,10},{10,1... | collective-permute-start | bytes 98312 | tf_op jit(solution)/shard_map/ppermute | solution.py:806
  168.0 6.7 %shard_map.133.electric_ref = f32[3,20,1024]{2,1,0:T(8,128)S(1)} custom-call(f32[6,20,1024]{2,1,0:T(8,128)S(1)} %get-tuple-element.39.merged_ref, f32[9,1024]{1,0:T(8,128)S(1)} %copy-done.2, f32[3,4,1024]{2,1,0:T(4,128)S(1)} %copy-done.1, f32[4,1024]{1,0:T(4,128)S(1)} %copy-done.6, s32[4,1024]{1,0:T(4,128)S(1)} %copy-done.5, f32[3,20,20]{2,1,0:T(8,128)S(1)} %copy-done.3, ...), custom_call_target="tpu_custom_call" | custom-call | tf_op jit(solution)/shard_map/pallas_call | solution.py:786
  174.7 0.0 collective-permute-done.4.above_ref
  174.7 0.0 collective-permute-done.3.below_ref
  174.7 1.4 shard_map.134
  (25 shorter events, 0.1 us)
Async XLA Ops:
  0.0 32.4 %copy-start.10 = (s32[4,128]{1,0:T(4,128)S(1)}, s32[4,128]{1,0:T(4,128)}, u32[]{:S(2)}) copy-start(s32[4,128]{1,0:T(4,128)} %param.23) | copy-start | bytes 6148
  0.0 32.4 %copy-start.11 = (s32[2,16]{1,0:T(2,128)S(1)}, s32[2,16]{1,0:T(2,128)}, u32[]{:S(2)}) copy-start(s32[2,16]{1,0:T(2,128)} %param.22) | copy-start | bytes 388
  0.0 32.4 %copy-start.12 = (s32[128]{0:T(128)S(1)}, s32[128]{0:T(128)}, u32[]{:S(2)}) copy-start(s32[128]{0:T(128)} %param.21) | copy-start | bytes 1540
  0.0 33.8 %copy-start = (f32[6,20,1024]{2,1,0:T(8,128)S(1)}, f32[6,20,1024]{2,1,0:T(8,128)}, u32[]{:S(2)}) copy-start(f32[6,20,1024]{2,1,0:T(8,128)} %fields_ref.3) | copy-start | bytes 1474564
  0.0 33.8 %copy-start.1 = (f32[3,4,1024]{2,1,0:T(4,128)S(1)}, f32[3,4,1024]{2,1,0:T(4,128)}, u32[]{:S(2)}) copy-start(f32[3,4,1024]{2,1,0:T(4,128)} %normals_ref.7) | copy-start | bytes 147460
  0.0 33.8 %copy-start.2 = (f32[9,1024]{1,0:T(8,128)S(1)}, f32[9,1024]{1,0:T(8,128)}, u32[]{:S(2)}) copy-start(f32[9,1024]{1,0:T(8,128)} %geometry_ref.5) | copy-start | bytes 110596
  0.0 33.8 %copy-start.3 = (f32[3,20,20]{2,1,0:T(8,128)S(1)}, f32[3,20,20]{2,1,0:T(8,128)}, u32[]{:S(2)}) copy-start(f32[3,20,20]{2,1,0:T(8,128)} %derivatives_ref.9) | copy-start | bytes 14404
  0.0 33.8 %copy-start.4 = (f32[20,40]{1,0:T(8,128)S(1)}, f32[20,40]{1,0:T(8,128)}, u32[]{:S(2)}) copy-start(f32[20,40]{1,0:T(8,128)} %lift_ref.13) | copy-start | bytes 9604
  0.1 33.8 %copy-start.5 = (s32[4,1024]{1,0:T(4,128)S(1)}, s32[4,1024]{1,0:T(4,128)}, u32[]{:S(2)}) copy-start(s32[4,1024]{1,0:T(4,128)} %nbr_ref.7) | copy-start | bytes 49156
  0.1 33.8 %copy-start.6 = (f32[4,1024]{1,0:T(4,128)S(1)}, f32[4,1024]{1,0:T(4,128)}, u32[]{:S(2)}) copy-start(f32[4,1024]{1,0:T(4,128)} %scale_ref.7) | copy-start | bytes 49156
  6.6 18.6 %copy-start.13 = (f32[64,128]{1,0:T(8,128)S(1)}, f32[64,128]{1,0:T(8,128)}, u32[]{:S(2)}) copy-start(f32[64,128]{1,0:T(8,128)} %get-tuple-element.24) | copy-start | bytes 98308
  6.6 27.3 %copy-start.8 = (s32[8,128]{1,0:T(8,128)S(1)}, s32[8,128]{1,0:T(8,128)}, u32[]{:S(2)}) copy-start(s32[8,128]{1,0:T(8,128)} %get-tuple-element.25.home_ref) | copy-start | bytes 12292
  6.6 43.7 %all-to-all-start = ((f32[128,4,384]{2,1,0:T(4,128)}), f32[128,4,384]{2,1,0:T(4,128)S(1)}, u32[]{:S(2)}, u32[]{:S(2)}) async-start(f32[128,4,384]{2,1,0:T(4,128)} %get-tuple-element.23), calls=%async_computation | async-start | bytes 1572864 | tf_op jit(solution)/shard_map/all_to_all | solution.py:836
  25.2 25.4 %collective-permute-start.2 = (f32[64,128]{1,0:T(8,128)S(1)}, f32[64,128]{1,0:T(8,128)S(1)}, u32[]{:S(2)}, u32[]{:S(2)}) collective-permute-start(f32[64,128]{1,0:T(8,128)S(1)} %copy-done.13), channel_id=1, source_target_pairs={{1,0},{2,1},{3,2},{4,3},{5,4},{6,5},{7,6},{8,7},{9,8},{10,9},{11,1... | collective-permute-start | bytes 98312 | tf_op jit(solution)/shard_map/ppermute | solution.py:806
  30.4 20.3 %collective-permute-start.1 = (f32[64,128]{1,0:T(8,128)S(1)}, f32[64,128]{1,0:T(8,128)S(1)}, u32[]{:S(2)}, u32[]{:S(2)}) collective-permute-start(f32[64,128]{1,0:T(8,128)S(1)} %copy-done.13), channel_id=1, source_target_pairs={{0,1},{1,2},{2,3},{3,4},{4,5},{5,6},{6,7},{7,8},{8,9},{9,10},{10,1... | collective-permute-start | bytes 98312 | tf_op jit(solution)/shard_map/ppermute | solution.py:806
  32.4 18.1 %collective-permute-start = (s32[8,128]{1,0:T(8,128)S(1)}, s32[8,128]{1,0:T(8,128)S(1)}, u32[]{:S(2)}, u32[]{:S(2)}) collective-permute-start(s32[8,128]{1,0:T(8,128)S(1)} %fusion), channel_id=1, source_target_pairs={{0,0},{1,1},{2,2},{3,3},{4,4},{5,5},{6,6},{7,7},{8,8},{9,9},{10,10... | collective-permute-start | bytes 12296 | tf_op jit(solution)/shard_map/ppermute | solution.py:857
  124.7 32.6 %copy-start.7 = (f32[64,256]{1,0:T(8,128)S(1)}, f32[64,256]{1,0:T(8,128)}, u32[]{:S(2)}) copy-start(f32[64,256]{1,0:T(8,128)} %get-tuple-element.34.before_ref) | copy-start | bytes 196612
  124.7 32.6 %copy-start.9 = (s32[2,128]{1,0:T(2,128)S(1)}, s32[2,128]{1,0:T(2,128)}, u32[]{:S(2)}) copy-start(s32[2,128]{1,0:T(2,128)} %get-tuple-element.33.slot_ref) | copy-start | bytes 3076
  161.8 12.8 %collective-permute-start.4 = (f32[64,128]{1,0:T(8,128)S(1)}, f32[64,128]{1,0:T(8,128)S(1)}, u32[]{:S(2)}, u32[]{:S(2)}) collective-permute-start(f32[64,128]{1,0:T(8,128)S(1)} %get-tuple-element.40), channel_id=1, source_target_pairs={{1,0},{2,1},{3,2},{4,3},{5,4},{6,5},{7,6},{8,7},{9,8},{10,9},{11,1... | collective-permute-start | bytes 98312 | tf_op jit(solution)/shard_map/ppermute | solution.py:806
  166.0 8.7 %collective-permute-start.3 = (f32[64,128]{1,0:T(8,128)S(1)}, f32[64,128]{1,0:T(8,128)S(1)}, u32[]{:S(2)}, u32[]{:S(2)}) collective-permute-start(f32[64,128]{1,0:T(8,128)S(1)} %get-tuple-element.40), channel_id=1, source_target_pairs={{0,1},{1,2},{2,3},{3,4},{4,5},{5,6},{6,7},{7,8},{8,9},{9,10},{10,1... | collective-permute-start | bytes 98312 | tf_op jit(solution)/shard_map/ppermute | solution.py:806

commit v5 on v4

--- a/solution.py
+++ b/solution.py
@@ -320,19 +320,16 @@
         back_ref[b : b + 1, :] = backs[b]
 
 
-def window_state(spot_ref, aligned, shifted, rows, block_ref):
-    half = 2 * REACH
+def window_state(spot_ref, parts, rows, block_ref):
+    size = parts[0].shape[0]
 
     def fetch(w, carry):
         spot = spot_ref[w]
-
-        @pl.when(spot < half)
-        def _():
-            block_ref[w, 0:rows, :] = aligned[spot, 0:rows, :]
-
-        @pl.when(spot >= half)
-        def _():
-            block_ref[w, 0:rows, :] = shifted[spot - half, 0:rows, :]
+        for number, part in enumerate(parts):
+
+            @pl.when((spot >= number * size) & (spot < number * size + size))
+            def _(number=number, part=part):
+                block_ref[w, 0:rows, :] = part[spot - number * size, 0:rows, :]
 
         return carry
 
@@ -440,11 +437,11 @@
 
 
 def first_window_kernel(
-    spot_ref, aligned_ref, shifted_ref, derivatives_ref, lift_ref,
+    spot_ref, row_ref, next_ref, twin_ref, derivatives_ref, lift_ref,
     out_ref,
     block_ref, efield_ref, hfield_ref, *scratch,
 ):
-    window_state(spot_ref, aligned_ref, shifted_ref, 272, block_ref)
+    window_state(spot_ref, (row_ref, next_ref, twin_ref), 272, block_ref)
     window_steps(derivatives_ref, lift_ref, block_ref, efield_ref, hfield_ref, *scratch)
     for c in range(3):
         electric = efield_ref[:, lanes_at(REACH * 3 + c)]
@@ -455,13 +452,13 @@
 
 
 def last_window_kernel(
-    spot_ref, aligned_ref, shifted_ref, aligned_state_ref, shifted_state_ref, back_ref,
-    derivatives_ref, lift_ref,
+    spot_ref, row_ref, next_ref, twin_ref, row_state_ref, next_state_ref, twin_state_ref,
+    back_ref, derivatives_ref, lift_ref,
     out_ref,
     result_ref, feature_ref, block_ref, efield_ref, hfield_ref, *scratch,
 ):
-    window_state(spot_ref, aligned_ref, shifted_ref, 272, block_ref)
-    window_state(spot_ref, aligned_state_ref, shifted_state_ref, 120, block_ref)
+    window_state(spot_ref, (row_ref, next_ref, twin_ref), 272, block_ref)
+    window_state(spot_ref, (row_state_ref, next_state_ref, twin_state_ref), 120, block_ref)
     window_steps(derivatives_ref, lift_ref, block_ref, efield_ref, hfield_ref, *scratch)
     for c in range(3):
         result_ref[c * 20 : c * 20 + 20, :] = efield_ref[:, lanes_at(REACH * 3 + c)]
@@ -807,26 +804,25 @@
 
 
 def share(copies):
-    count, size = lax.axis_size(RING), copies.shape[0]
-
-    def within(start):
-        groups = [
-            [device_of((first + i + start) % count) for i in range(size)]
-            for first in range(0, count, size)
-        ]
-        return lax.all_to_all(copies, RING, 0, 0, axis_index_groups=groups, tiled=True)
-
-    return within(0), within(size // 2)
+    row = lax.all_to_all(copies, "sub", 0, 0, tiled=True)
+    count = lax.axis_size("dom")
+    seat_of = seats(count)
+
+    def swap(partner):
+        pairs = [(int(seat_of[d]), int(seat_of[partner(d) % count])) for d in range(count)]
+        return lax.ppermute(row, "dom", pairs)
+
+    return row, swap(lambda d: d - 1 if d % 2 == 0 else d + 1), swap(lambda d: d ^ 1)
 
 
 def spots(count, size):
     table = np.zeros((count, 16), np.int32)
     for block in range(count):
+        d, s = divmod(block, size)
         for w in range(2 * REACH + 1):
-            at = block % size + w - REACH
-            if not 0 <= at < size:
-                at = (block + size // 2) % size + w - REACH + size
-            table[device_of(block), w] = at
+            step, at = divmod(s + w - REACH, size)
+            part = 0 if step == 0 else 2 if (d + step) % count == d ^ 1 else 1
+            table[device_of(block), w] = part * size + at
     return table
 
 
@@ -857,7 +853,7 @@
     table = lax.ppermute(table, RING, [(i, device_of(i)) for i in range(count)])
     me = lax.axis_index(RING)
     spot = lax.dynamic_index_in_dim(
-        jnp.asarray(spots(count, 2 * REACH)), me, keepdims=False
+        jnp.asarray(spots(count, lax.axis_size("sub"))), me, keepdims=False
     )
     traces = ((4, 32, fine), f32)
     send = send_rows.reshape(slots // LANES, LANES)
@@ -896,8 +892,8 @@
     received, table, ends_below, ends_above, early, fine_code, spot = lax.optimization_barrier(
         (received, table, ends_below, ends_above, early, fine_code, spot)
     )
-    group = 2 * REACH
-    blocks = group + 1
+    group = lax.axis_size("sub")
+    blocks = 2 * REACH + 1
     copies, back = call(
         functools.partial(unpack_kernel, width),
         [((group, 272, fine), f32), ((slots // LANES, LANES), i32)],
@@ -913,20 +909,20 @@
         ((blocks, 3, 40, fine), f32), ((40, blocks * 3 * fine), f32),
         ((72, blocks * 3 * fine), f32), ((20, blocks * 3 * fine), f32), ((72, 20), f32),
     ]
-    aligned, offset = share(copies)
+    rows = share(copies)
     (copies,) = call(
         first_window_kernel,
         [((group, 120, fine), f32)],
         window,
-        spot, aligned, offset, derivatives, lift_matrix,
+        spot, *rows, derivatives, lift_matrix,
         smem=(0,),
     )
-    aligned_state, offset_state = share(copies)
+    states = share(copies)
     (outgoing,) = call(
         last_window_kernel,
         [((slots, LANES), f32)],
         [((128, fine), f32), ((128, slots), f32)] + window,
-        spot, aligned, offset, aligned_state, offset_state, back, derivatives, lift_matrix,
+        spot, *rows, *states, back, derivatives, lift_matrix,
         smem=(0,),
     )
     returned = swap_slots(outgoing)

time: 177 us -> 161 us (0.910)
  blocking collectives: 86.1 us -> 40.9 us
  waiting for transfers between devices: 8.66 us -> 23.5 us
  starting transfers between devices: 32.4 us -> 45.9 us
    all_to_all x4 -> x2, blocking collectives: 63.6 us -> 19.6 us  [share(): row = lax.all_to_all(copies, 'sub', 0, 0, tiled=True)]
    ppermute x0 -> x4, waiting for transfers between devices: none -> 14.9 us  [swap(): return lax.ppermute(row, 'dom', pairs)]
    ppermute x0 -> x4, starting transfers between devices: none -> 13.3 us  [swap(): return lax.ppermute(row, 'dom', pairs)]
  transfers between devices with their start and end apart: 6 -> 10, of which waited for: 1 -> 3; matrix products, arithmetic and copies ran while one was open for 1% -> 1% of each run, Pallas kernels for 8% -> 9%
where the time goes in v5:
time: 161 us; the launch traced here: 160 us
  Pallas kernels  47.6 us (30%)
  starting transfers between devices  45.9 us (29%)
  blocking collectives  40.9 us (25%)
  waiting for transfers between devices  23.5 us (15%)
  local copies, waits for them, and re-layouts  1.76 us (1%)
    pallas_call x8, Pallas kernels, call(): pl.pallas_call(kernel, out_shape=[jax.ShapeDtypeStruct(shape, dtype) for...  47.6 us
    all_to_all x1, blocking collectives, swap_slots(): lax.all_to_all(chunks, 'dom', split_axis=0, concat_axis=0, tiled=True)  21.3 us
    all_to_all x2, blocking collectives, share(): row = lax.all_to_all(copies, 'sub', 0, 0, tiled=True)  19.6 us
    all_to_all x1, starting transfers between devices, swap_slots(): lax.all_to_all(chunks, 'dom', split_axis=0, concat_axis=0, tiled=True)  18.6 us
    ppermute x4, waiting for transfers between devices, swap(): return lax.ppermute(row, 'dom', pairs)  14.9 us
    ppermute x4, starting transfers between devices, exchange(): return (lax.ppermute(block, RING, up), lax.ppermute(block, RING, down))  13.4 us
    ppermute x4, starting transfers between devices, swap(): return lax.ppermute(row, 'dom', pairs)  13.3 us
    all_to_all x1, waiting for transfers between devices, swap_slots(): lax.all_to_all(chunks, 'dom', split_axis=0, concat_axis=0, tiled=True)  8.56 us
  transfers between devices with their start and end apart: 10, of which 3 were waited for; matrix products, arithmetic and copies ran while one was open for 1% of the time, Pallas kernels for 9%

profile of v5, /device:TPU:1, one launch (start us, length us, event | category | flops | bytes accessed | tf_op | source)
XLA Modules:
  0.0 160.1 jit_solution(18366528904040860578)
XLA Ops:
  0.0 6.4 %shard_map.127 = (f32[128,4,384]{2,1,0:T(4,128)}, f32[64,128]{1,0:T(8,128)}, s32[8,128]{1,0:T(8,128)}, s32[2,128]{1,0:T(2,128)}, f32[64,256]{1,0:T(8,128)}) custom-call(s32[4,128]{1,0:T(4,128)} %bitcast.9, s32[4,128]{1,0:T(4,128)} %constant.24.clone.order_hbm, f32[6,20,1024]{2,1,0:T(8,128)} %fields_ref.3, s32[4,1024]{1,0:T(4,128)} %nbr_ref.7, ...), custom_call_target="tpu_custom_call" | custom-call | tf_op jit(solution)/shard_map/pallas_call | solution.py:783
  6.5 0.0 copy-start.10
  6.5 0.0 copy-start.11
  6.5 0.0 copy-start
  6.6 18.6 %all-to-all-start = ((f32[128,4,384]{2,1,0:T(4,128)}), f32[128,4,384]{2,1,0:T(4,128)S(1)}, u32[]{:S(2)}, u32[]{:S(2)}) async-start(f32[128,4,384]{2,1,0:T(4,128)} %get-tuple-element.23), calls=%async_computation | async-start | bytes 1572864 | tf_op jit(solution)/shard_map/all_to_all | solution.py:832
  25.2 5.2 %collective-permute-start.2 = (f32[64,128]{1,0:T(8,128)S(1)}, f32[64,128]{1,0:T(8,128)S(1)}, u32[]{:S(2)}, u32[]{:S(2)}) collective-permute-start(f32[64,128]{1,0:T(8,128)S(1)} %copy-done.13), channel_id=1, source_target_pairs={{1,0},{2,1},{3,2},{4,3},{5,4},{6,5},{7,6},{8,7},{9,8},{10,9},{11,1... | collective-permute-start | bytes 98312 | tf_op jit(solution)/shard_map/ppermute | solution.py:803
  30.3 1.9 %collective-permute-start.1 = (f32[64,128]{1,0:T(8,128)S(1)}, f32[64,128]{1,0:T(8,128)S(1)}, u32[]{:S(2)}, u32[]{:S(2)}) collective-permute-start(f32[64,128]{1,0:T(8,128)S(1)} %copy-done.13), channel_id=1, source_target_pairs={{0,1},{1,2},{2,3},{3,4},{4,5},{5,6},{6,7},{7,8},{8,9},{9,10},{10,1... | collective-permute-start | bytes 98312 | tf_op jit(solution)/shard_map/ppermute | solution.py:803
  32.3 0.1 pad.8.clone
  32.3 0.1 fusion
  32.4 0.7 collective-permute-start
  33.1 0.7 dynamic-slice_bitcast_fusion.spot_ref
  33.8 7.9 %shard_map.128 = (f32[3,20,1024]{2,1,0:T(8,128)S(1)}, s32[4,1024]{1,0:T(4,128)S(1)}) custom-call(f32[6,20,1024]{2,1,0:T(8,128)S(1)} %copy-done, s32[8,128]{1,0:T(8,128)S(1)} %copy-done.8, f32[9,1024]{1,0:T(8,128)S(1)} %copy-done.2, f32[3,4,1024]{2,1,0:T(4,128)S(1)} %copy-done.1, f32[4,1024]{1,0:T(4,128)S(1)} %copy-done.6, s32[4,1024]{1,0:T(4,128)S(1)} %copy-done.5, ...), custom_call_target="tpu_custom_call" | custom-call | tf_op jit(solution)/shard_map/pallas_call | solution.py:783
  41.7 8.6 %all-to-all-done = f32[128,4,384]{2,1,0:T(4,128)S(1)} async-done(((f32[128,4,384]{2,1,0:T(4,128)}), f32[128,4,384]{2,1,0:T(4,128)S(1)}, u32[]{:S(2)}, u32[]{:S(2)}) %all-to-all-start) | async-done | bytes 786464 | tf_op jit(solution)/shard_map/all_to_all | solution.py:832
  50.3 0.3 reshape.16.received_ref
  50.6 0.7 shard_map.129
  51.3 11.7 %all_to_all.20.row_ref = f32[4,272,128]{2,1,0:T(8,128)S(1)} all-to-all(f32[4,272,128]{2,1,0:T(8,128)S(1)} %get-tuple-element.31), channel_id=1, replica_groups=mesh['dom'=128,'sub'=4] {'sub'}, dimensions={0} | all-to-all | bytes 1114112 | tf_op jit(solution)/shard_map/all_to_all | solution.py:807
  63.1 4.7 %collective-permute-start.4 = (f32[4,272,128]{2,1,0:T(8,128)S(1)}, f32[4,272,128]{2,1,0:T(8,128)S(1)}, u32[]{:S(2)}, u32[]{:S(2)}) collective-permute-start(f32[4,272,128]{2,1,0:T(8,128)S(1)} %all_to_all.20.row_ref), channel_id=1, source_target_pairs={{0,4},{4,0},{8,12},{12,8},{16,20},{20,16},{24,28},{28,24},{32,36},... | collective-permute-start | bytes 1671176 | tf_op jit(solution)/shard_map/ppermute | solution.py:813
  67.8 1.9 %collective-permute-start.3 = (f32[4,272,128]{2,1,0:T(8,128)S(1)}, f32[4,272,128]{2,1,0:T(8,128)S(1)}, u32[]{:S(2)}, u32[]{:S(2)}) collective-permute-start(f32[4,272,128]{2,1,0:T(8,128)S(1)} %all_to_all.20.row_ref), channel_id=1, source_target_pairs={{0,448},{4,8},{8,4},{12,16},{16,12},{20,24},{24,20},{28,32},{32,28... | collective-permute-start | bytes 1671176 | tf_op jit(solution)/shard_map/ppermute | solution.py:813
  69.8 9.2 %collective-permute-done.3.next_ref = f32[4,272,128]{2,1,0:T(8,128)S(1)} collective-permute-done((f32[4,272,128]{2,1,0:T(8,128)S(1)}, f32[4,272,128]{2,1,0:T(8,128)S(1)}, u32[]{:S(2)}, u32[]{:S(2)}) %collective-permute-start.3) | collective-permute-done | bytes 557088 | tf_op jit(solution)/shard_map/ppermute | solution.py:813
  79.0 9.7 %shard_map.130 = f32[4,120,128]{2,1,0:T(8,128)S(1)} custom-call(s32[16]{0:T(128)S(1)} %dynamic-slice_bitcast_fusion.spot_ref, f32[4,272,128]{2,1,0:T(8,128)S(1)} %all_to_all.20.row_ref, f32[4,272,128]{2,1,0:T(8,128)S(1)} %collective-permute-done.3.next_ref, f32[4,272,128]{2,1,0:T(8,128)S(1)} %collective-permute-done.4.twin_ref, f32[3,20,20]{2,1,0:T(8,128)S(1)} %copy-done.3, ...), custom_call_target="tpu_custom_call" | custom-call | tf_op jit(solution)/shard_map/pallas_call | solution.py:783
  88.7 7.8 %all_to_all.21.row_state_ref = f32[4,120,128]{2,1,0:T(8,128)S(1)} all-to-all(f32[4,120,128]{2,1,0:T(8,128)S(1)} %shard_map.130), channel_id=1, replica_groups=mesh['dom'=128,'sub'=4] {'sub'}, dimensions={0} | all-to-all | bytes 491520 | tf_op jit(solution)/shard_map/all_to_all | solution.py:807
  96.5 4.5 %collective-permute-start.6 = (f32[4,120,128]{2,1,0:T(8,128)S(1)}, f32[4,120,128]{2,1,0:T(8,128)S(1)}, u32[]{:S(2)}, u32[]{:S(2)}) collective-permute-start(f32[4,120,128]{2,1,0:T(8,128)S(1)} %all_to_all.21.row_state_ref), channel_id=1, source_target_pairs={{0,4},{4,0},{8,12},{12,8},{16,20},{20,16},{24,28},{28,24},{32,36},... | collective-permute-start | bytes 737288 | tf_op jit(solution)/shard_map/ppermute | solution.py:813
  101.0 2.1 %collective-permute-start.5 = (f32[4,120,128]{2,1,0:T(8,128)S(1)}, f32[4,120,128]{2,1,0:T(8,128)S(1)}, u32[]{:S(2)}, u32[]{:S(2)}) collective-permute-start(f32[4,120,128]{2,1,0:T(8,128)S(1)} %all_to_all.21.row_state_ref), channel_id=1, source_target_pairs={{0,448},{4,8},{8,4},{12,16},{16,12},{20,24},{24,20},{28,32},{32,28... | collective-permute-start | bytes 737288 | tf_op jit(solution)/shard_map/ppermute | solution.py:813
  103.2 5.7 %collective-permute-done.5.next_state_ref = f32[4,120,128]{2,1,0:T(8,128)S(1)} collective-permute-done((f32[4,120,128]{2,1,0:T(8,128)S(1)}, f32[4,120,128]{2,1,0:T(8,128)S(1)}, u32[]{:S(2)}, u32[]{:S(2)}) %collective-permute-start.5) | collective-permute-done | bytes 245792 | tf_op jit(solution)/shard_map/ppermute | solution.py:813
  108.9 10.1 %shard_map.131 = f32[512,128]{1,0:T(8,128)S(1)} custom-call(s32[16]{0:T(128)S(1)} %dynamic-slice_bitcast_fusion.spot_ref, f32[4,272,128]{2,1,0:T(8,128)S(1)} %all_to_all.20.row_ref, f32[4,272,128]{2,1,0:T(8,128)S(1)} %collective-permute-done.3.next_ref, f32[4,272,128]{2,1,0:T(8,128)S(1)} %collective-permute-done.4.twin_ref, ...), custom_call_target="tpu_custom_call" | custom-call | tf_op jit(solution)/shard_map/pallas_call | solution.py:783
  119.0 21.3 %all_to_all.22 = f32[128,4,128]{2,1,0:T(4,128)S(1)} all-to-all(f32[128,4,128]{2,1,0:T(4,128)S(1)} %bitcast.8), channel_id=1, replica_groups=mesh['dom'=128,'sub'=4] {'dom'}, dimensions={0} | all-to-all | bytes 524288 | tf_op jit(solution)/shard_map/all_to_all | solution.py:832
  140.4 0.6 copy-done.9
  141.0 4.6 %shard_map.132 = (f32[6,20,1024]{2,1,0:T(8,128)S(1)}, f32[64,128]{1,0:T(8,128)S(1)}) custom-call(f32[512,128]{1,0:T(8,128)S(1)} %bitcast.7, s32[8,128]{1,0:T(8,128)S(1)} %copy-done.8, s32[2,128]{1,0:T(2,128)S(1)} %copy-done.9, f32[64,256]{1,0:T(8,128)S(1)} %copy-done.7, s32[4,1024]{1,0:T(4,128)S(1)} %get-tuple-element.35.code_ref, ...), custom_call_target="tpu_custom_call" | custom-call | tf_op jit(solution)/shard_map/pallas_call | solution.py:783
  145.6 4.4 %collective-permute-start.8 = (f32[64,128]{1,0:T(8,128)S(1)}, f32[64,128]{1,0:T(8,128)S(1)}, u32[]{:S(2)}, u32[]{:S(2)}) collective-permute-start(f32[64,128]{1,0:T(8,128)S(1)} %get-tuple-element.40), channel_id=1, source_target_pairs={{1,0},{2,1},{3,2},{4,3},{5,4},{6,5},{7,6},{8,7},{9,8},{10,9},{11,1... | collective-permute-start | bytes 98312 | tf_op jit(solution)/shard_map/ppermute | solution.py:803
  150.0 1.9 %collective-permute-start.7 = (f32[64,128]{1,0:T(8,128)S(1)}, f32[64,128]{1,0:T(8,128)S(1)}, u32[]{:S(2)}, u32[]{:S(2)}) collective-permute-start(f32[64,128]{1,0:T(8,128)S(1)} %get-tuple-element.40), channel_id=1, source_target_pairs={{0,1},{1,2},{2,3},{3,4},{4,5},{5,6},{6,7},{7,8},{8,9},{9,10},{10,1... | collective-permute-start | bytes 98312 | tf_op jit(solution)/shard_map/ppermute | solution.py:803
  151.9 6.7 %shard_map.133.electric_ref = f32[3,20,1024]{2,1,0:T(8,128)S(1)} custom-call(f32[6,20,1024]{2,1,0:T(8,128)S(1)} %get-tuple-element.39.merged_ref, f32[9,1024]{1,0:T(8,128)S(1)} %copy-done.2, f32[3,4,1024]{2,1,0:T(4,128)S(1)} %copy-done.1, f32[4,1024]{1,0:T(4,128)S(1)} %copy-done.6, s32[4,1024]{1,0:T(4,128)S(1)} %copy-done.5, f32[3,20,20]{2,1,0:T(8,128)S(1)} %copy-done.3, ...), custom_call_target="tpu_custom_call" | custom-call | tf_op jit(solution)/shard_map/pallas_call | solution.py:783
  158.7 1.4 shard_map.134
  (31 shorter events, 0.1 us)
Async XLA Ops:
  6.4 18.7 %copy-start.13 = (f32[64,128]{1,0:T(8,128)S(1)}, f32[64,128]{1,0:T(8,128)}, u32[]{:S(2)}) copy-start(f32[64,128]{1,0:T(8,128)} %get-tuple-element.24) | copy-start | bytes 98308
  6.5 25.9 %copy-start.10 = (s32[4,128]{1,0:T(4,128)S(1)}, s32[4,128]{1,0:T(4,128)}, u32[]{:S(2)}) copy-start(s32[4,128]{1,0:T(4,128)} %param.23) | copy-start | bytes 6148
  6.5 25.9 %copy-start.11 = (s32[2,16]{1,0:T(2,128)S(1)}, s32[2,16]{1,0:T(2,128)}, u32[]{:S(2)}) copy-start(s32[2,16]{1,0:T(2,128)} %param.22) | copy-start | bytes 388
  6.5 25.9 %copy-start.12 = (s32[128]{0:T(128)S(1)}, s32[128]{0:T(128)}, u32[]{:S(2)}) copy-start(s32[128]{0:T(128)} %param.21) | copy-start | bytes 1540
  6.5 27.3 %copy-start = (f32[6,20,1024]{2,1,0:T(8,128)S(1)}, f32[6,20,1024]{2,1,0:T(8,128)}, u32[]{:S(2)}) copy-start(f32[6,20,1024]{2,1,0:T(8,128)} %fields_ref.3) | copy-start | bytes 1474564
  6.5 27.3 %copy-start.1 = (f32[3,4,1024]{2,1,0:T(4,128)S(1)}, f32[3,4,1024]{2,1,0:T(4,128)}, u32[]{:S(2)}) copy-start(f32[3,4,1024]{2,1,0:T(4,128)} %normals_ref.7) | copy-start | bytes 147460
  6.5 27.3 %copy-start.2 = (f32[9,1024]{1,0:T(8,128)S(1)}, f32[9,1024]{1,0:T(8,128)}, u32[]{:S(2)}) copy-start(f32[9,1024]{1,0:T(8,128)} %geometry_ref.5) | copy-start | bytes 110596
  6.5 27.3 %copy-start.4 = (f32[20,40]{1,0:T(8,128)S(1)}, f32[20,40]{1,0:T(8,128)}, u32[]{:S(2)}) copy-start(f32[20,40]{1,0:T(8,128)} %lift_ref.13) | copy-start | bytes 9604
  6.5 27.3 %copy-start.5 = (s32[4,1024]{1,0:T(4,128)S(1)}, s32[4,1024]{1,0:T(4,128)}, u32[]{:S(2)}) copy-start(s32[4,1024]{1,0:T(4,128)} %nbr_ref.7) | copy-start | bytes 49156
  6.6 27.3 %copy-start.6 = (f32[4,1024]{1,0:T(4,128)S(1)}, f32[4,1024]{1,0:T(4,128)}, u32[]{:S(2)}) copy-start(f32[4,1024]{1,0:T(4,128)} %scale_ref.7) | copy-start | bytes 49156
  6.6 43.7 %all-to-all-start = ((f32[128,4,384]{2,1,0:T(4,128)}), f32[128,4,384]{2,1,0:T(4,128)S(1)}, u32[]{:S(2)}, u32[]{:S(2)}) async-start(f32[128,4,384]{2,1,0:T(4,128)} %get-tuple-element.23), calls=%async_computation | async-start | bytes 1572864 | tf_op jit(solution)/shard_map/all_to_all | solution.py:832
  25.1 8.7 %copy-start.3 = (f32[3,20,20]{2,1,0:T(8,128)S(1)}, f32[3,20,20]{2,1,0:T(8,128)}, u32[]{:S(2)}) copy-start(f32[3,20,20]{2,1,0:T(8,128)} %derivatives_ref.9) | copy-start | bytes 14404
  25.2 25.4 %collective-permute-start.2 = (f32[64,128]{1,0:T(8,128)S(1)}, f32[64,128]{1,0:T(8,128)S(1)}, u32[]{:S(2)}, u32[]{:S(2)}) collective-permute-start(f32[64,128]{1,0:T(8,128)S(1)} %copy-done.13), channel_id=1, source_target_pairs={{1,0},{2,1},{3,2},{4,3},{5,4},{6,5},{7,6},{8,7},{9,8},{10,9},{11,1... | collective-permute-start | bytes 98312 | tf_op jit(solution)/shard_map/ppermute | solution.py:803
  30.3 20.2 %collective-permute-start.1 = (f32[64,128]{1,0:T(8,128)S(1)}, f32[64,128]{1,0:T(8,128)S(1)}, u32[]{:S(2)}, u32[]{:S(2)}) collective-permute-start(f32[64,128]{1,0:T(8,128)S(1)} %copy-done.13), channel_id=1, source_target_pairs={{0,1},{1,2},{2,3},{3,4},{4,5},{5,6},{6,7},{7,8},{8,9},{9,10},{10,1... | collective-permute-start | bytes 98312 | tf_op jit(solution)/shard_map/ppermute | solution.py:803
  32.4 18.1 %collective-permute-start = (s32[8,128]{1,0:T(8,128)S(1)}, s32[8,128]{1,0:T(8,128)S(1)}, u32[]{:S(2)}, u32[]{:S(2)}) collective-permute-start(s32[8,128]{1,0:T(8,128)S(1)} %fusion), channel_id=1, source_target_pairs={{0,0},{1,1},{2,2},{3,3},{4,4},{5,5},{6,6},{7,7},{8,8},{9,9},{10,10... | collective-permute-start | bytes 12296 | tf_op jit(solution)/shard_map/ppermute | solution.py:853
  33.1 0.8 copy-start.8
  63.1 6.7 %collective-permute-start.4 = (f32[4,272,128]{2,1,0:T(8,128)S(1)}, f32[4,272,128]{2,1,0:T(8,128)S(1)}, u32[]{:S(2)}, u32[]{:S(2)}) collective-permute-start(f32[4,272,128]{2,1,0:T(8,128)S(1)} %all_to_all.20.row_ref), channel_id=1, source_target_pairs={{0,4},{4,0},{8,12},{12,8},{16,20},{20,16},{24,28},{28,24},{32,36},... | collective-permute-start | bytes 1671176 | tf_op jit(solution)/shard_map/ppermute | solution.py:813
  67.8 11.1 %collective-permute-start.3 = (f32[4,272,128]{2,1,0:T(8,128)S(1)}, f32[4,272,128]{2,1,0:T(8,128)S(1)}, u32[]{:S(2)}, u32[]{:S(2)}) collective-permute-start(f32[4,272,128]{2,1,0:T(8,128)S(1)} %all_to_all.20.row_ref), channel_id=1, source_target_pairs={{0,448},{4,8},{8,4},{12,16},{16,12},{20,24},{24,20},{28,32},{32,28... | collective-permute-start | bytes 1671176 | tf_op jit(solution)/shard_map/ppermute | solution.py:813
  96.5 6.7 %collective-permute-start.6 = (f32[4,120,128]{2,1,0:T(8,128)S(1)}, f32[4,120,128]{2,1,0:T(8,128)S(1)}, u32[]{:S(2)}, u32[]{:S(2)}) collective-permute-start(f32[4,120,128]{2,1,0:T(8,128)S(1)} %all_to_all.21.row_state_ref), channel_id=1, source_target_pairs={{0,4},{4,0},{8,12},{12,8},{16,20},{20,16},{24,28},{28,24},{32,36},... | collective-permute-start | bytes 737288 | tf_op jit(solution)/shard_map/ppermute | solution.py:813
  101.0 7.8 %collective-permute-start.5 = (f32[4,120,128]{2,1,0:T(8,128)S(1)}, f32[4,120,128]{2,1,0:T(8,128)S(1)}, u32[]{:S(2)}, u32[]{:S(2)}) collective-permute-start(f32[4,120,128]{2,1,0:T(8,128)S(1)} %all_to_all.21.row_state_ref), channel_id=1, source_target_pairs={{0,448},{4,8},{8,4},{12,16},{16,12},{20,24},{24,20},{28,32},{32,28... | collective-permute-start | bytes 737288 | tf_op jit(solution)/shard_map/ppermute | solution.py:813
  119.0 21.4 %copy-start.7 = (f32[64,256]{1,0:T(8,128)S(1)}, f32[64,256]{1,0:T(8,128)}, u32[]{:S(2)}) copy-start(f32[64,256]{1,0:T(8,128)} %get-tuple-element.34.before_ref) | copy-start | bytes 196612
  140.4 0.6 copy-start.9
  145.6 13.1 %collective-permute-start.8 = (f32[64,128]{1,0:T(8,128)S(1)}, f32[64,128]{1,0:T(8,128)S(1)}, u32[]{:S(2)}, u32[]{:S(2)}) collective-permute-start(f32[64,128]{1,0:T(8,128)S(1)} %get-tuple-element.40), channel_id=1, source_target_pairs={{1,0},{2,1},{3,2},{4,3},{5,4},{6,5},{7,6},{8,7},{9,8},{10,9},{11,1... | collective-permute-start | bytes 98312 | tf_op jit(solution)/shard_map/ppermute | solution.py:803
  150.0 8.7 %collective-permute-start.7 = (f32[64,128]{1,0:T(8,128)S(1)}, f32[64,128]{1,0:T(8,128)S(1)}, u32[]{:S(2)}, u32[]{:S(2)}) collective-permute-start(f32[64,128]{1,0:T(8,128)S(1)} %get-tuple-element.40), channel_id=1, source_target_pairs={{0,1},{1,2},{2,3},{3,4},{4,5},{5,6},{6,7},{7,8},{8,9},{9,10},{10,1... | collective-permute-start | bytes 98312 | tf_op jit(solution)/shard_map/ppermute | solution.py:803

commit v6 on v5

--- a/solution.py
+++ b/solution.py
@@ -222,7 +222,7 @@
     sublane = lax.broadcasted_iota(jnp.int32, (8, LANES), 0)
 
     def pick(db, carry):
-        row = rows8(jnp.minimum(row_ref[pl.ds(db, 1), :], own - 1))
+        row = rows8(jnp.minimum(row_ref[db : db + 1, :], own - 1))
         lane, which = row & (LANES - 1), row >> 7
         hits = [which == b for b in range(blocks)]
         for group in range(18):
@@ -258,7 +258,8 @@
                 dense_ref[at : at + length, lanes_at(db)] = value[:length]
         return carry
 
-    lax.fori_loop(0, dense_blocks, pick, 0)
+    for db in range(dense_blocks):
+        pick(db, 0)
     before_ref[...] = dense_ref[0:64, :]
     chunks = LANES * out_ref.shape[0] // (send_blocks * LANES)
     for sb in range(send_blocks):
@@ -356,7 +357,8 @@
         )
         return carry
 
-    lax.fori_loop(0, blocks, prepare, 0)
+    for w in range(blocks):
+        prepare(w, 0)
     for level in range(1, REACH + 1):
         magnetic = level % 2 == 1
         source_ref, target_ref = (efield_ref, hfield_ref) if magnetic else (hfield_ref, efield_ref)
@@ -380,7 +382,8 @@
                 export_ref[w, g * 8 : g * 8 + 8, :] = groups[g]
             return carry
 
-        lax.fori_loop(first - 1, last + 1, expose, 0)
+        for w in range(first - 1, last + 1):
+            expose(w, 0)
 
         def gather(w, carry):
             sources = [
@@ -402,16 +405,17 @@
                 lane = jnp.where(local, code >> 2, code) & (LANES - 1)
                 groups = gather32(sources, which, lane, [zero] * 4)
                 for g in range(4):
-                    jump_ref[f, g * 8 : g * 8 + 8, :] = (
+                    jump_ref[w, f, g * 8 : g * 8 + 8, :] = (
                         groups[g] - pool_ref[w, f, g * 8 : g * 8 + 8, :]
                     )
-            regroup(jump_ref, sorted_ref)
-            flux = crossed([spread_ref[w, c] for c in range(3)], [sorted_ref[c] for c in range(3)])
+            regroup(jump_ref.at[w], sorted_ref.at[w])
+            flux = crossed([spread_ref[w, c] for c in range(3)], [sorted_ref[w, c] for c in range(3)])
             for c in range(3):
                 flux_ref[:, lanes_at(w * 3 + c)] = flux[c]
             return carry
 
-        lax.fori_loop(first, last, gather, 0)
+        for w in range(first, last):
+            gather(w, 0)
         span = slice(first * 3 * LANES, last * 3 * LANES)
         grad_ref[:, span] = dot(stack_ref[...], source_ref[:, span])
         lifted_ref[:, span] = dot(lift, flux_ref[:, span])
@@ -433,7 +437,8 @@
                 target_ref[:, at] = target_ref[:, at] + step * rate
             return carry
 
-        lax.fori_loop(first, last, update, 0)
+        for w in range(first, last):
+            update(w, 0)
 
 
 def first_window_kernel(
@@ -517,27 +522,19 @@
                 face = jnp.where(code >= 4 * own_blocks * LANES, code & 3, 4)
                 groups = gather32(ends, face, (code >> 2) & (LANES - 1), groups)
             for g in range(4):
-                jump_ref[f, g * 8 : g * 8 + 8, :] = (
+                jump_ref[eb, f, g * 8 : g * 8 + 8, :] = (
                     groups[g] - own_ref[f, g * 8 : g * 8 + 8, at]
                 )
-        regroup(jump_ref, sorted_ref)
+        regroup(jump_ref.at[eb], sorted_ref.at[eb])
         scale = scale_ref[:, at]
         scaled = [normals_ref[c, :, at] * scale for c in range(3)]
-        spread_normals(lambda c, f: scaled[c][f : f + 1, :], spread_ref)
-        flux = crossed([spread_ref[c] for c in range(3)], [sorted_ref[c] for c in range(3)])
+        spread_normals(lambda c, f: scaled[c][f : f + 1, :], spread_ref.at[eb])
+        flux = crossed([spread_ref[eb, c] for c in range(3)], [sorted_ref[eb, c] for c in range(3)])
         for c in range(3):
             flux_ref[c, :, at] = flux[c]
 
-    def inner(eb, carry):
-        one(eb, False)
-        return carry
-
-    if ends is None:
-        lax.fori_loop(0, own_blocks, inner, 0)
-    else:
-        one(0, True)
-        lax.fori_loop(1, own_blocks - 1, inner, 0)
-        one(own_blocks - 1, True)
+    for eb in range(own_blocks):
+        one(eb, ends is not None and eb in (0, own_blocks - 1))
 
 
 def own_faces(pool_ref, own):
@@ -566,7 +563,7 @@
         grad_ref[c] = dot(stack_ref[...], source(c))
         lifted_ref[c] = dot(lift, flux_ref[c])
 
-    def one(eb, carry):
+    def one(eb):
         at = lanes_at(eb)
 
         def factor(m, a):
@@ -577,9 +574,9 @@
 
         for c in range(3):
             out(c, at, target(c, at) + step * (curl_part(c, factor, grad) + lifted_ref[c, :, at]))
-        return carry
-
-    lax.fori_loop(0, own_blocks, one, 0)
+
+    for eb in range(own_blocks):
+        one(eb)
 
 
 def early_kernel(
@@ -603,7 +600,7 @@
         -COARSE_STEP, lambda c: fields_ref[c], lambda c, at: fields_ref[3 + c, :, at], out,
         geometry_ref, derivatives_ref, lift_ref, stack_ref, flux_ref, grad_ref, lifted_ref,
     )
-    width = jump_ref.shape[2] * 2
+    width = LANES * 2
 
     def locate(eb, carry):
         at = lanes_at(eb)
@@ -643,9 +640,9 @@
     for c in range(6):
         flat_ref[c * 20 : c * 20 + 20, :] = fields_ref[c]
 
-    def merge(eb, carry):
+    def merge(eb):
         at = lanes_at(eb)
-        home = rows8(home_ref[pl.ds(eb, 1), :])
+        home = rows8(home_ref[eb : eb + 1, :])
         lane = home & (LANES - 1)
         hits = [(home >> 7) == b for b in range(dense_blocks)]
         for group in range(15):
@@ -654,9 +651,9 @@
             for b in range(dense_blocks):
                 value = jnp.where(hits[b], take(dense_ref[rows, lanes_at(b)], lane), value)
             flat_ref[rows, at] = value
-        return carry
-
-    lax.fori_loop(0, own // LANES, merge, 0)
+
+    for eb in range(own // LANES):
+        merge(eb)
     for c in range(6):
         merged_ref[c] = flat_ref[c * 20 : c * 20 + 20, :]
     for c in range(3):
@@ -880,7 +877,8 @@
     received = swap_slots(packed)
     ends_below, ends_above = exchange(ends)
     work = [
-        ((3, 40, own), f32), ((4, 32, LANES), f32), ((3, 40, LANES), f32), ((3, 40, LANES), f32),
+        ((3, 40, own), f32), ((own // LANES, 4, 32, LANES), f32),
+        ((own // LANES, 3, 40, LANES), f32), ((own // LANES, 3, 40, LANES), f32),
         ((72, 20), f32), ((3, 72, own), f32), ((3, 20, own), f32),
     ]
     early, fine_code = call(
@@ -905,7 +903,8 @@
     )
     window = [
         ((blocks, 272, fine), f32), ((20, blocks * 3 * fine), f32), ((20, blocks * 3 * fine), f32),
-        ((blocks, 4, 32, fine), f32), ((blocks, 32, fine), f32), traces, ((3, 40, fine), f32),
+        ((blocks, 4, 32, fine), f32), ((blocks, 32, fine), f32), ((blocks, 4, 32, fine), f32),
+        ((blocks, 3, 40, fine), f32),
         ((blocks, 3, 40, fine), f32), ((40, blocks * 3 * fine), f32),
         ((72, blocks * 3 * fine), f32), ((20, blocks * 3 * fine), f32), ((72, 20), f32),
     ]

time: 161 us -> 148 us (0.919)
  Pallas kernels: 47.6 us -> 33.7 us
    pallas_call x8, Pallas kernels: 47.6 us -> 33.7 us  [call(): pl.pallas_call(kernel, out_shape=[jax.ShapeDtypeStruct(shape, dtype) for...]
where the time goes in v6:
time: 148 us; the launch traced here: 147 us
  starting transfers between devices  46 us (31%)
  blocking collectives  40.8 us (28%)
  Pallas kernels  33.7 us (23%)
  waiting for transfers between devices  24.5 us (17%)
  local copies, waits for them, and re-layouts  1.76 us (1%)
    pallas_call x8, Pallas kernels, call(): pl.pallas_call(kernel, out_shape=[jax.ShapeDtypeStruct(shape, dtype) for...  33.7 us
    all_to_all x1, blocking collectives, swap_slots(): lax.all_to_all(chunks, 'dom', split_axis=0, concat_axis=0, tiled=True)  21.3 us
    all_to_all x2, blocking collectives, share(): row = lax.all_to_all(copies, 'sub', 0, 0, tiled=True)  19.6 us
    all_to_all x1, starting transfers between devices, swap_slots(): lax.all_to_all(chunks, 'dom', split_axis=0, concat_axis=0, tiled=True)  18.6 us
    ppermute x4, waiting for transfers between devices, swap(): return lax.ppermute(row, 'dom', pairs)  15.1 us
    ppermute x4, starting transfers between devices, exchange(): return (lax.ppermute(block, RING, up), lax.ppermute(block, RING, down))  13.6 us
    ppermute x4, starting transfers between devices, swap(): return lax.ppermute(row, 'dom', pairs)  13.1 us
    all_to_all x1, waiting for transfers between devices, swap_slots(): lax.all_to_all(chunks, 'dom', split_axis=0, concat_axis=0, tiled=True)  9.45 us
  transfers between devices with their start and end apart: 10, of which 3 were waited for; matrix products, arithmetic and copies ran while one was open for 1% of the time, Pallas kernels for 9%

profile of v6, /device:TPU:1, one launch (start us, length us, event | category | flops | bytes accessed | tf_op | source)
XLA Modules:
  0.0 147.3 jit_solution(13713033317732421699)
XLA Ops:
  0.0 6.0 %shard_map.127 = (f32[128,4,384]{2,1,0:T(4,128)}, f32[64,128]{1,0:T(8,128)}, s32[8,128]{1,0:T(8,128)}, s32[2,128]{1,0:T(2,128)}, f32[64,256]{1,0:T(8,128)}) custom-call(s32[4,128]{1,0:T(4,128)} %bitcast.9, s32[4,128]{1,0:T(4,128)} %constant.24.clone.order_hbm, f32[6,20,1024]{2,1,0:T(8,128)} %fields_ref.3, s32[4,1024]{1,0:T(4,128)} %nbr_ref.7, ...), custom_call_target="tpu_custom_call" | custom-call | tf_op jit(solution)/shard_map/pallas_call | solution.py:780
  6.0 0.0 copy-start.11
  6.0 0.0 copy-start.12
  6.1 0.0 copy-start.2
  6.1 18.6 %all-to-all-start = ((f32[128,4,384]{2,1,0:T(4,128)}), f32[128,4,384]{2,1,0:T(4,128)S(1)}, u32[]{:S(2)}, u32[]{:S(2)}) async-start(f32[128,4,384]{2,1,0:T(4,128)} %get-tuple-element.23), calls=%async_computation | async-start | bytes 1572864 | tf_op jit(solution)/shard_map/all_to_all | solution.py:829
  24.7 5.2 %collective-permute-start.2 = (f32[64,128]{1,0:T(8,128)S(1)}, f32[64,128]{1,0:T(8,128)S(1)}, u32[]{:S(2)}, u32[]{:S(2)}) collective-permute-start(f32[64,128]{1,0:T(8,128)S(1)} %copy-done.13), channel_id=1, source_target_pairs={{1,0},{2,1},{3,2},{4,3},{5,4},{6,5},{7,6},{8,7},{9,8},{10,9},{11,1... | collective-permute-start | bytes 98312 | tf_op jit(solution)/shard_map/ppermute | solution.py:800
  29.9 1.9 %collective-permute-start.1 = (f32[64,128]{1,0:T(8,128)S(1)}, f32[64,128]{1,0:T(8,128)S(1)}, u32[]{:S(2)}, u32[]{:S(2)}) collective-permute-start(f32[64,128]{1,0:T(8,128)S(1)} %copy-done.13), channel_id=1, source_target_pairs={{0,1},{1,2},{2,3},{3,4},{4,5},{5,6},{6,7},{7,8},{8,9},{9,10},{10,1... | collective-permute-start | bytes 98312 | tf_op jit(solution)/shard_map/ppermute | solution.py:800
  31.8 0.1 pad.8.clone
  31.9 0.1 fusion
  32.0 0.7 collective-permute-start
  32.7 0.7 dynamic-slice_bitcast_fusion.spot_ref
  33.4 7.0 %shard_map.128 = (f32[3,20,1024]{2,1,0:T(8,128)S(1)}, s32[4,1024]{1,0:T(4,128)S(1)}) custom-call(f32[6,20,1024]{2,1,0:T(8,128)S(1)} %copy-done, s32[8,128]{1,0:T(8,128)S(1)} %copy-done.8, f32[9,1024]{1,0:T(8,128)S(1)} %copy-done.2, f32[3,4,1024]{2,1,0:T(4,128)S(1)} %copy-done.1, f32[4,1024]{1,0:T(4,128)S(1)} %copy-done.6, s32[4,1024]{1,0:T(4,128)S(1)} %copy-done.5, ...), custom_call_target="tpu_custom_call" | custom-call | tf_op jit(solution)/shard_map/pallas_call | solution.py:780
  40.4 9.5 %all-to-all-done = f32[128,4,384]{2,1,0:T(4,128)S(1)} async-done(((f32[128,4,384]{2,1,0:T(4,128)}), f32[128,4,384]{2,1,0:T(4,128)S(1)}, u32[]{:S(2)}, u32[]{:S(2)}) %all-to-all-start) | async-done | bytes 786464 | tf_op jit(solution)/shard_map/all_to_all | solution.py:829
  49.8 0.3 reshape.16.received_ref
  50.1 0.7 shard_map.129
  50.9 11.7 %all_to_all.20.row_ref = f32[4,272,128]{2,1,0:T(8,128)S(1)} all-to-all(f32[4,272,128]{2,1,0:T(8,128)S(1)} %get-tuple-element.31), channel_id=1, replica_groups=mesh['dom'=128,'sub'=4] {'sub'}, dimensions={0} | all-to-all | bytes 1114112 | tf_op jit(solution)/shard_map/all_to_all | solution.py:804
  62.6 4.7 %collective-permute-start.4 = (f32[4,272,128]{2,1,0:T(8,128)S(1)}, f32[4,272,128]{2,1,0:T(8,128)S(1)}, u32[]{:S(2)}, u32[]{:S(2)}) collective-permute-start(f32[4,272,128]{2,1,0:T(8,128)S(1)} %all_to_all.20.row_ref), channel_id=1, source_target_pairs={{0,4},{4,0},{8,12},{12,8},{16,20},{20,16},{24,28},{28,24},{32,36},... | collective-permute-start | bytes 1671176 | tf_op jit(solution)/shard_map/ppermute | solution.py:810
  67.4 1.9 %collective-permute-start.3 = (f32[4,272,128]{2,1,0:T(8,128)S(1)}, f32[4,272,128]{2,1,0:T(8,128)S(1)}, u32[]{:S(2)}, u32[]{:S(2)}) collective-permute-start(f32[4,272,128]{2,1,0:T(8,128)S(1)} %all_to_all.20.row_ref), channel_id=1, source_target_pairs={{0,448},{4,8},{8,4},{12,16},{16,12},{20,24},{24,20},{28,32},{32,28... | collective-permute-start | bytes 1671176 | tf_op jit(solution)/shard_map/ppermute | solution.py:810
  69.3 9.2 %collective-permute-done.3.next_ref = f32[4,272,128]{2,1,0:T(8,128)S(1)} collective-permute-done((f32[4,272,128]{2,1,0:T(8,128)S(1)}, f32[4,272,128]{2,1,0:T(8,128)S(1)}, u32[]{:S(2)}, u32[]{:S(2)}) %collective-permute-start.3) | collective-permute-done | bytes 557088 | tf_op jit(solution)/shard_map/ppermute | solution.py:810
  78.5 4.5 %shard_map.130 = f32[4,120,128]{2,1,0:T(8,128)S(1)} custom-call(s32[16]{0:T(128)S(1)} %dynamic-slice_bitcast_fusion.spot_ref, f32[4,272,128]{2,1,0:T(8,128)S(1)} %all_to_all.20.row_ref, f32[4,272,128]{2,1,0:T(8,128)S(1)} %collective-permute-done.3.next_ref, f32[4,272,128]{2,1,0:T(8,128)S(1)} %collective-permute-done.4.twin_ref, f32[3,20,20]{2,1,0:T(8,128)S(1)} %copy-done.3, ...), custom_call_target="tpu_custom_call" | custom-call | tf_op jit(solution)/shard_map/pallas_call | solution.py:780
  83.1 7.8 %all_to_all.21.row_state_ref = f32[4,120,128]{2,1,0:T(8,128)S(1)} all-to-all(f32[4,120,128]{2,1,0:T(8,128)S(1)} %shard_map.130), channel_id=1, replica_groups=mesh['dom'=128,'sub'=4] {'sub'}, dimensions={0} | all-to-all | bytes 491520 | tf_op jit(solution)/shard_map/all_to_all | solution.py:804
  90.9 4.5 %collective-permute-start.6 = (f32[4,120,128]{2,1,0:T(8,128)S(1)}, f32[4,120,128]{2,1,0:T(8,128)S(1)}, u32[]{:S(2)}, u32[]{:S(2)}) collective-permute-start(f32[4,120,128]{2,1,0:T(8,128)S(1)} %all_to_all.21.row_state_ref), channel_id=1, source_target_pairs={{0,4},{4,0},{8,12},{12,8},{16,20},{20,16},{24,28},{28,24},{32,36},... | collective-permute-start | bytes 737288 | tf_op jit(solution)/shard_map/ppermute | solution.py:810
  95.4 1.9 %collective-permute-start.5 = (f32[4,120,128]{2,1,0:T(8,128)S(1)}, f32[4,120,128]{2,1,0:T(8,128)S(1)}, u32[]{:S(2)}, u32[]{:S(2)}) collective-permute-start(f32[4,120,128]{2,1,0:T(8,128)S(1)} %all_to_all.21.row_state_ref), channel_id=1, source_target_pairs={{0,448},{4,8},{8,4},{12,16},{16,12},{20,24},{24,20},{28,32},{32,28... | collective-permute-start | bytes 737288 | tf_op jit(solution)/shard_map/ppermute | solution.py:810
  97.4 5.9 %collective-permute-done.5.next_state_ref = f32[4,120,128]{2,1,0:T(8,128)S(1)} collective-permute-done((f32[4,120,128]{2,1,0:T(8,128)S(1)}, f32[4,120,128]{2,1,0:T(8,128)S(1)}, u32[]{:S(2)}, u32[]{:S(2)}) %collective-permute-start.5) | collective-permute-done | bytes 245792 | tf_op jit(solution)/shard_map/ppermute | solution.py:810
  103.2 4.9 %shard_map.131 = f32[512,128]{1,0:T(8,128)S(1)} custom-call(s32[16]{0:T(128)S(1)} %dynamic-slice_bitcast_fusion.spot_ref, f32[4,272,128]{2,1,0:T(8,128)S(1)} %all_to_all.20.row_ref, f32[4,272,128]{2,1,0:T(8,128)S(1)} %collective-permute-done.3.next_ref, f32[4,272,128]{2,1,0:T(8,128)S(1)} %collective-permute-done.4.twin_ref, ...), custom_call_target="tpu_custom_call" | custom-call | tf_op jit(solution)/shard_map/pallas_call | solution.py:780
  108.2 21.3 %all_to_all.22 = f32[128,4,128]{2,1,0:T(4,128)S(1)} all-to-all(f32[128,4,128]{2,1,0:T(4,128)S(1)} %bitcast.8), channel_id=1, replica_groups=mesh['dom'=128,'sub'=4] {'dom'}, dimensions={0} | all-to-all | bytes 524288 | tf_op jit(solution)/shard_map/all_to_all | solution.py:829
  129.5 0.6 copy-done.9
  130.1 3.4 %shard_map.132 = (f32[6,20,1024]{2,1,0:T(8,128)S(1)}, f32[64,128]{1,0:T(8,128)S(1)}) custom-call(f32[512,128]{1,0:T(8,128)S(1)} %bitcast.7, s32[8,128]{1,0:T(8,128)S(1)} %copy-done.8, s32[2,128]{1,0:T(2,128)S(1)} %copy-done.9, f32[64,256]{1,0:T(8,128)S(1)} %copy-done.7, s32[4,1024]{1,0:T(4,128)S(1)} %get-tuple-element.35.code_ref, ...), custom_call_target="tpu_custom_call" | custom-call | tf_op jit(solution)/shard_map/pallas_call | solution.py:780
  133.5 4.4 %collective-permute-start.8 = (f32[64,128]{1,0:T(8,128)S(1)}, f32[64,128]{1,0:T(8,128)S(1)}, u32[]{:S(2)}, u32[]{:S(2)}) collective-permute-start(f32[64,128]{1,0:T(8,128)S(1)} %get-tuple-element.40), channel_id=1, source_target_pairs={{1,0},{2,1},{3,2},{4,3},{5,4},{6,5},{7,6},{8,7},{9,8},{10,9},{11,1... | collective-permute-start | bytes 98312 | tf_op jit(solution)/shard_map/ppermute | solution.py:800
  137.9 2.1 %collective-permute-start.7 = (f32[64,128]{1,0:T(8,128)S(1)}, f32[64,128]{1,0:T(8,128)S(1)}, u32[]{:S(2)}, u32[]{:S(2)}) collective-permute-start(f32[64,128]{1,0:T(8,128)S(1)} %get-tuple-element.40), channel_id=1, source_target_pairs={{0,1},{1,2},{2,3},{3,4},{4,5},{5,6},{6,7},{7,8},{8,9},{9,10},{10,1... | collective-permute-start | bytes 98312 | tf_op jit(solution)/shard_map/ppermute | solution.py:800
  140.0 5.8 %shard_map.133.electric_ref = f32[3,20,1024]{2,1,0:T(8,128)S(1)} custom-call(f32[6,20,1024]{2,1,0:T(8,128)S(1)} %get-tuple-element.39.merged_ref, f32[9,1024]{1,0:T(8,128)S(1)} %copy-done.2, f32[3,4,1024]{2,1,0:T(4,128)S(1)} %copy-done.1, f32[4,1024]{1,0:T(4,128)S(1)} %copy-done.6, s32[4,1024]{1,0:T(4,128)S(1)} %copy-done.5, f32[3,20,20]{2,1,0:T(8,128)S(1)} %copy-done.3, ...), custom_call_target="tpu_custom_call" | custom-call | tf_op jit(solution)/shard_map/pallas_call | solution.py:780
  145.9 1.4 shard_map.134
  (31 shorter events, 0.1 us)
Async XLA Ops:
  6.0 18.7 %copy-start.13 = (f32[64,128]{1,0:T(8,128)S(1)}, f32[64,128]{1,0:T(8,128)}, u32[]{:S(2)}) copy-start(f32[64,128]{1,0:T(8,128)} %get-tuple-element.24) | copy-start | bytes 98308
  6.0 25.9 %copy-start.10 = (s32[4,128]{1,0:T(4,128)S(1)}, s32[4,128]{1,0:T(4,128)}, u32[]{:S(2)}) copy-start(s32[4,128]{1,0:T(4,128)} %param.23) | copy-start | bytes 6148
  6.0 25.9 %copy-start.11 = (s32[2,16]{1,0:T(2,128)S(1)}, s32[2,16]{1,0:T(2,128)}, u32[]{:S(2)}) copy-start(s32[2,16]{1,0:T(2,128)} %param.22) | copy-start | bytes 388
  6.0 25.9 %copy-start.12 = (s32[128]{0:T(128)S(1)}, s32[128]{0:T(128)}, u32[]{:S(2)}) copy-start(s32[128]{0:T(128)} %param.21) | copy-start | bytes 1540
  6.1 27.3 %copy-start = (f32[6,20,1024]{2,1,0:T(8,128)S(1)}, f32[6,20,1024]{2,1,0:T(8,128)}, u32[]{:S(2)}) copy-start(f32[6,20,1024]{2,1,0:T(8,128)} %fields_ref.3) | copy-start | bytes 1474564
  6.1 27.3 %copy-start.1 = (f32[3,4,1024]{2,1,0:T(4,128)S(1)}, f32[3,4,1024]{2,1,0:T(4,128)}, u32[]{:S(2)}) copy-start(f32[3,4,1024]{2,1,0:T(4,128)} %normals_ref.7) | copy-start | bytes 147460
  6.1 27.3 %copy-start.2 = (f32[9,1024]{1,0:T(8,128)S(1)}, f32[9,1024]{1,0:T(8,128)}, u32[]{:S(2)}) copy-start(f32[9,1024]{1,0:T(8,128)} %geometry_ref.5) | copy-start | bytes 110596
  6.1 27.3 %copy-start.4 = (f32[20,40]{1,0:T(8,128)S(1)}, f32[20,40]{1,0:T(8,128)}, u32[]{:S(2)}) copy-start(f32[20,40]{1,0:T(8,128)} %lift_ref.13) | copy-start | bytes 9604
  6.1 27.3 %copy-start.5 = (s32[4,1024]{1,0:T(4,128)S(1)}, s32[4,1024]{1,0:T(4,128)}, u32[]{:S(2)}) copy-start(s32[4,1024]{1,0:T(4,128)} %nbr_ref.7) | copy-start | bytes 49156
  6.1 27.3 %copy-start.6 = (f32[4,1024]{1,0:T(4,128)S(1)}, f32[4,1024]{1,0:T(4,128)}, u32[]{:S(2)}) copy-start(f32[4,1024]{1,0:T(4,128)} %scale_ref.7) | copy-start | bytes 49156
  6.1 43.7 %all-to-all-start = ((f32[128,4,384]{2,1,0:T(4,128)}), f32[128,4,384]{2,1,0:T(4,128)S(1)}, u32[]{:S(2)}, u32[]{:S(2)}) async-start(f32[128,4,384]{2,1,0:T(4,128)} %get-tuple-element.23), calls=%async_computation | async-start | bytes 1572864 | tf_op jit(solution)/shard_map/all_to_all | solution.py:829
  24.7 8.7 %copy-start.3 = (f32[3,20,20]{2,1,0:T(8,128)S(1)}, f32[3,20,20]{2,1,0:T(8,128)}, u32[]{:S(2)}) copy-start(f32[3,20,20]{2,1,0:T(8,128)} %derivatives_ref.9) | copy-start | bytes 14404
  24.7 25.4 %collective-permute-start.2 = (f32[64,128]{1,0:T(8,128)S(1)}, f32[64,128]{1,0:T(8,128)S(1)}, u32[]{:S(2)}, u32[]{:S(2)}) collective-permute-start(f32[64,128]{1,0:T(8,128)S(1)} %copy-done.13), channel_id=1, source_target_pairs={{1,0},{2,1},{3,2},{4,3},{5,4},{6,5},{7,6},{8,7},{9,8},{10,9},{11,1... | collective-permute-start | bytes 98312 | tf_op jit(solution)/shard_map/ppermute | solution.py:800
  29.9 20.2 %collective-permute-start.1 = (f32[64,128]{1,0:T(8,128)S(1)}, f32[64,128]{1,0:T(8,128)S(1)}, u32[]{:S(2)}, u32[]{:S(2)}) collective-permute-start(f32[64,128]{1,0:T(8,128)S(1)} %copy-done.13), channel_id=1, source_target_pairs={{0,1},{1,2},{2,3},{3,4},{4,5},{5,6},{6,7},{7,8},{8,9},{9,10},{10,1... | collective-permute-start | bytes 98312 | tf_op jit(solution)/shard_map/ppermute | solution.py:800
  32.0 18.1 %collective-permute-start = (s32[8,128]{1,0:T(8,128)S(1)}, s32[8,128]{1,0:T(8,128)S(1)}, u32[]{:S(2)}, u32[]{:S(2)}) collective-permute-start(s32[8,128]{1,0:T(8,128)S(1)} %fusion), channel_id=1, source_target_pairs={{0,0},{1,1},{2,2},{3,3},{4,4},{5,5},{6,6},{7,7},{8,8},{9,9},{10,10... | collective-permute-start | bytes 12296 | tf_op jit(solution)/shard_map/ppermute | solution.py:850
  32.6 0.8 copy-start.8
  62.6 6.7 %collective-permute-start.4 = (f32[4,272,128]{2,1,0:T(8,128)S(1)}, f32[4,272,128]{2,1,0:T(8,128)S(1)}, u32[]{:S(2)}, u32[]{:S(2)}) collective-permute-start(f32[4,272,128]{2,1,0:T(8,128)S(1)} %all_to_all.20.row_ref), channel_id=1, source_target_pairs={{0,4},{4,0},{8,12},{12,8},{16,20},{20,16},{24,28},{28,24},{32,36},... | collective-permute-start | bytes 1671176 | tf_op jit(solution)/shard_map/ppermute | solution.py:810
  67.4 11.1 %collective-permute-start.3 = (f32[4,272,128]{2,1,0:T(8,128)S(1)}, f32[4,272,128]{2,1,0:T(8,128)S(1)}, u32[]{:S(2)}, u32[]{:S(2)}) collective-permute-start(f32[4,272,128]{2,1,0:T(8,128)S(1)} %all_to_all.20.row_ref), channel_id=1, source_target_pairs={{0,448},{4,8},{8,4},{12,16},{16,12},{20,24},{24,20},{28,32},{32,28... | collective-permute-start | bytes 1671176 | tf_op jit(solution)/shard_map/ppermute | solution.py:810
  90.9 6.5 %collective-permute-start.6 = (f32[4,120,128]{2,1,0:T(8,128)S(1)}, f32[4,120,128]{2,1,0:T(8,128)S(1)}, u32[]{:S(2)}, u32[]{:S(2)}) collective-permute-start(f32[4,120,128]{2,1,0:T(8,128)S(1)} %all_to_all.21.row_state_ref), channel_id=1, source_target_pairs={{0,4},{4,0},{8,12},{12,8},{16,20},{20,16},{24,28},{28,24},{32,36},... | collective-permute-start | bytes 737288 | tf_op jit(solution)/shard_map/ppermute | solution.py:810
  95.4 7.8 %collective-permute-start.5 = (f32[4,120,128]{2,1,0:T(8,128)S(1)}, f32[4,120,128]{2,1,0:T(8,128)S(1)}, u32[]{:S(2)}, u32[]{:S(2)}) collective-permute-start(f32[4,120,128]{2,1,0:T(8,128)S(1)} %all_to_all.21.row_state_ref), channel_id=1, source_target_pairs={{0,448},{4,8},{8,4},{12,16},{16,12},{20,24},{24,20},{28,32},{32,28... | collective-permute-start | bytes 737288 | tf_op jit(solution)/shard_map/ppermute | solution.py:810
  108.2 21.3 %copy-start.7 = (f32[64,256]{1,0:T(8,128)S(1)}, f32[64,256]{1,0:T(8,128)}, u32[]{:S(2)}) copy-start(f32[64,256]{1,0:T(8,128)} %get-tuple-element.34.before_ref) | copy-start | bytes 196612
  129.4 0.6 copy-start.9
  133.5 12.4 %collective-permute-start.8 = (f32[64,128]{1,0:T(8,128)S(1)}, f32[64,128]{1,0:T(8,128)S(1)}, u32[]{:S(2)}, u32[]{:S(2)}) collective-permute-start(f32[64,128]{1,0:T(8,128)S(1)} %get-tuple-element.40), channel_id=1, source_target_pairs={{1,0},{2,1},{3,2},{4,3},{5,4},{6,5},{7,6},{8,7},{9,8},{10,9},{11,1... | collective-permute-start | bytes 98312 | tf_op jit(solution)/shard_map/ppermute | solution.py:800
  137.9 8.0 %collective-permute-start.7 = (f32[64,128]{1,0:T(8,128)S(1)}, f32[64,128]{1,0:T(8,128)S(1)}, u32[]{:S(2)}, u32[]{:S(2)}) collective-permute-start(f32[64,128]{1,0:T(8,128)S(1)} %get-tuple-element.40), channel_id=1, source_target_pairs={{0,1},{1,2},{2,3},{3,4},{4,5},{5,6},{6,7},{7,8},{8,9},{9,10},{10,1... | collective-permute-start | bytes 98312 | tf_op jit(solution)/shard_map/ppermute | solution.py:800
